TPU v7x, 128 devices: a whole 4x4x4 slice. The times are simulated.
128 devices in a mesh: ctx: 16 (over x, y), exp: 8 (over z, core).
Axes of the slice: x: 4, y: 4, z: 4, core: 2. Of those that a mesh axis runs over, the one named last changes fastest.
Arguments:
- queries: bfloat16 [8, 2048, 2304], P('exp', 'ctx'), may hold values from -6 to 6
- key_vectors: bfloat16 [8, 2048, 2304], P('exp', 'ctx'), may hold values from -0.3125 to 0.3125
- values: bfloat16 [8, 2048, 2304], P('exp', 'ctx'), may hold values from -6 to 6
- log_decay: bfloat16 [8, 2048, 2304], P('exp', 'ctx')
- starts: int32 [8, 2048], P('exp', 'ctx'), may hold values 0 or 1
- residual_in: bfloat16 [8, 2048, 2304], P('exp', 'ctx'), may hold values from -6 to 6
- out_grad: bfloat16 [8, 2048, 2304], P('exp', 'ctx'), may hold values from -6 to 6
- expert_ids: int32 [8, 2048, 8], P('exp', 'ctx'), may hold values from 0 to 127, as said below
- slot_index: int32 [8, 2048, 8], P('exp', 'ctx'), may hold values from 0 to 127, as said below
- router: bfloat16 [2304, 128], replicated, may hold values from -0.125 to 0.125
- hidden_saved: bfloat16 [128, 1536, 512], P(('ctx', 'exp')), may hold values from -16 to 16
- w_down: bfloat16 [128, 512, 2304], P(('ctx', 'exp')), may hold values from -0.09375 to 0.09375
- momentum: bfloat16 [128, 512, 2304], P(('ctx', 'exp')), may hold values from -1.75 to 1.75
Outputs:
- grad_queries: bfloat16 [8, 2048, 2304], P('exp', 'ctx')
- grad_keys: bfloat16 [8, 2048, 2304], P('exp', 'ctx')
- grad_values: bfloat16 [8, 2048, 2304], P('exp', 'ctx')
- grad_decay: bfloat16 [8, 2048, 2304], P('exp', 'ctx')
- grad_residual: bfloat16 [8, 2048, 2304], P('exp', 'ctx')
- new_weights: bfloat16 [128, 512, 2304], P(('ctx', 'exp'))
- new_momentum: bfloat16 [128, 512, 2304], P(('ctx', 'exp'))
Inputs may be any that keep to these rules, and one draw needn't show every extreme that they name: `expert_ids`: each token's 8 experts are distinct; loads differ strongly between experts. slot_index[s, t, j] counts the routes to the same expert that come earlier, in order of token and then of j, among the tokens of the same device (the 128 tokens of one block of one sequence); routes with a slot of 12 or more are dropped, and some are in every draw.
All inputs are finite; a program needn't handle non-finite values. No bound on the sum of `starts` on one device may be relied on, other than what follows from the above.
Results may differ from a plain program's by a relative error of at most 0.019.
Values may be sent and summed in bfloat16 or wider, within the bound.
A program may use at most 192 MiB of HBM per device.

v0:
```python
import jax
import jax.numpy as jnp
from jax import lax
from jax.sharding import PartitionSpec as P

HEADS = 18
HD = 128
TOP = 8


NORM_EPS = 1e-06
LION_RATE = 0.001
BETA_ONE = 0.9
BETA_TWO = 0.99
WEIGHT_DECAY = 0.1
HIGHEST_PRECISION = lax.Precision.HIGHEST


def carried_in(value, axis, join, neutral):
    place = lax.axis_index(axis)
    gathered = jax.tree.map(
        lambda a, kind: lax.all_gather(a.astype(kind), axis), value, (jnp.bfloat16, jnp.bfloat16)
    )
    state = jax.tree.map(lambda a, e: jnp.zeros_like(a) + jnp.asarray(e, a.dtype), value, neutral)

    def one(step, state):
        return join(
            state,
            jax.tree.map(
                lambda a, own: lax.dynamic_index_in_dim(a, step, 0, False).astype(own.dtype),
                gathered,
                value,
            ),
        )

    return lax.fori_loop(0, place, one, state)


def carried_in_2(value, axis, join, neutral):
    count = lax.axis_size(axis)
    place = lax.axis_index(axis)
    ahead = count - 1 - place
    gathered = jax.tree.map(
        lambda a, kind: lax.all_gather(a.astype(kind), axis),
        value,
        jax.tree.map(lambda a: jnp.bfloat16 if a.dtype == jnp.float32 else a.dtype, value),
    )
    state = jax.tree.map(lambda a, e: jnp.zeros_like(a) + jnp.asarray(e, a.dtype), value, neutral)

    def one(step, state):
        source = count - 1 - step
        return join(
            state,
            jax.tree.map(
                lambda a, own: lax.dynamic_index_in_dim(a, source, 0, False).astype(own.dtype),
                gathered,
                value,
            ),
        )

    return lax.fori_loop(0, ahead, one, state)


def summary(key_block, value_block, decay_block, start_block):
    cumul = jnp.cumsum(decay_block, axis=0)
    segment = jnp.cumsum(start_block, dtype=jnp.int32)
    last_cum = cumul[-1]
    tail_mask = (segment == segment[-1]).astype(jnp.float32)
    key_end = key_block * jnp.exp(last_cum[None] - cumul) * tail_mask[:, None, None]
    fresh = jnp.einsum("shd,she->hde", key_end, value_block, precision=HIGHEST_PRECISION)
    passing = jnp.exp(last_cum) * (segment[-1] == 0).astype(jnp.float32)
    return (passing, fresh)


def block_forward(query_block, key_block, value_block, decay_block, start_block, in_state):
    length = query_block.shape[0]
    scaling = query_block.shape[2] ** (-0.5)
    cumul = jnp.cumsum(decay_block, axis=0)
    segment = jnp.cumsum(start_block, dtype=jnp.int32)
    position = jnp.arange(length, dtype=jnp.int32)
    allowed = (segment[:, None] == segment[None, :]) & (position[:, None] >= position[None, :])
    carried = (segment == 0).astype(jnp.float32)
    q_dec = query_block * jnp.exp(cumul)
    k_dec = key_block * jnp.exp(-cumul)
    scores = jnp.einsum("thd,shd->hts", q_dec, k_dec, precision=HIGHEST_PRECISION)
    scores = jnp.where(allowed[None], scores, 0.0)
    within = jnp.einsum("hts,she->the", scores, value_block, precision=HIGHEST_PRECISION)
    q_carried = q_dec * carried[:, None, None]
    inbound = jnp.einsum("thd,hde->the", q_carried, in_state, precision=HIGHEST_PRECISION)
    passing, fresh = summary(key_block, value_block, decay_block, start_block)
    return (scaling * (within + inbound), passing, fresh, q_carried)


def compose(earlier, later_pair):
    return (later_pair[0] * earlier[0], later_pair[0][..., None] * earlier[1] + later_pair[1])


def expert_step(saved, weight, moment, gathered, route_weight):
    produced = jnp.dot(saved, weight, preferred_element_type=jnp.float32).astype(jnp.bfloat16)
    scaled = (route_weight.astype(jnp.float32)[:, None] * gathered.astype(jnp.float32)).astype(
        jnp.bfloat16
    )
    gradient = lax.dot_general(
        saved, scaled, (((0,), (0,)), ((), ())), preferred_element_type=jnp.float32
    )
    weight_float = weight.astype(jnp.float32)
    moment_float = moment.astype(jnp.float32)
    direction = jnp.sign(BETA_ONE * moment_float + (1.0 - BETA_ONE) * gradient)
    new_weight = (weight_float - LION_RATE * (direction + WEIGHT_DECAY * weight_float)).astype(
        jnp.bfloat16
    )
    new_moment = (BETA_TWO * moment_float + (1.0 - BETA_TWO) * gradient).astype(jnp.bfloat16)
    return (produced, new_weight, new_moment)


def split_heads(array):
    return array[0].astype(jnp.float32).reshape(array.shape[1], HEADS, HD)


def local(
    queries,
    key_vectors,
    values,
    log_decay,
    starts,
    residual_in,
    out_grad,
    expert_ids,
    slot_index,
    router,
    hidden_saved,
    w_down,
    momentum,
):
    tok_rows = queries.shape[1]
    width = queries.shape[2]
    scaling = HD ** (-0.5)
    query_float = split_heads(queries)
    key_float = split_heads(key_vectors)
    value_float = split_heads(values)
    decay_float = split_heads(log_decay)
    start_row = starts[0]
    passing, fresh = summary(key_float, value_float, decay_float, start_row)
    identity_pair = (jnp.ones_like(passing), jnp.zeros_like(fresh))
    in_state = carried_in((passing, fresh), "ctx", compose, identity_pair)[1]

    def local_block(query_part, key_part, value_part, decay_part):
        attended, pass_part, fresh_part, q_part = block_forward(
            query_part, key_part, value_part, decay_part, start_row, in_state
        )
        return ((attended, pass_part[:, :, None] * in_state + fresh_part), q_part)

    block_out, pullback, q_carried = jax.vjp(
        local_block, query_float, key_float, value_float, decay_float, has_aux=True
    )
    attn_round = block_out[0].reshape(tok_rows, width).astype(jnp.bfloat16)
    mixed = residual_in[0].astype(jnp.float32) + attn_round.astype(jnp.float32)
    inverse = lax.rsqrt(jnp.mean(mixed * mixed, axis=-1, keepdims=True) + NORM_EPS)
    normed = (mixed * inverse).astype(jnp.bfloat16)
    logits = jnp.dot(normed, router, preferred_element_type=jnp.float32)
    expert_count = router.shape[1]
    chosen_ids = expert_ids[0]
    slot_rank = slot_index[0]
    onehot = (chosen_ids[:, :, None] == jnp.arange(expert_count, dtype=jnp.int32)).astype(
        jnp.float32
    )
    chosen = jnp.sum(onehot * logits[:, None, :], axis=-1)
    gate_values = jax.nn.sigmoid(chosen)
    gate_total = jnp.sum(gate_values, axis=1, keepdims=True)
    weights = gate_values / gate_total
    device_count = lax.axis_size(("ctx", "exp"))
    slot_count = hidden_saved.shape[1] // device_count
    keep_flat = (slot_rank < slot_count).reshape(-1)
    route_place = jnp.where(
        keep_flat, (chosen_ids * slot_count + slot_rank).reshape(-1), expert_count * slot_count
    )
    safe_place = jnp.minimum(route_place, expert_count * slot_count - 1)
    grad_rows = out_grad[0]
    repeated = jnp.broadcast_to(grad_rows[:, None, :], (tok_rows, TOP, width)).reshape(
        tok_rows * TOP, width
    )
    outgoing = (
        jnp.zeros((expert_count * slot_count, width), jnp.bfloat16)
        .at[route_place]
        .set(repeated, mode="drop")
    )
    outgoing_weight = (
        jnp.zeros((expert_count * slot_count,), jnp.bfloat16)
        .at[route_place]
        .set(weights.astype(jnp.bfloat16).reshape(-1), mode="drop")
    )
    incoming, incoming_weight = (
        lax.all_to_all(
            outgoing.reshape(expert_count, slot_count, width),
            ("ctx", "exp"),
            split_axis=0,
            concat_axis=0,
            tiled=True,
        ),
        lax.all_to_all(
            outgoing_weight.reshape(expert_count, slot_count),
            ("ctx", "exp"),
            split_axis=0,
            concat_axis=0,
            tiled=True,
        ),
    )
    gathered = incoming.reshape(device_count * slot_count, width)
    route_weight = incoming_weight.reshape(device_count * slot_count)
    produced, new_weight, new_moment = expert_step(
        hidden_saved[0], w_down[0], momentum[0], gathered, route_weight
    )
    returned = lax.all_to_all(
        produced.reshape(device_count, slot_count, width),
        ("ctx", "exp"),
        split_axis=0,
        concat_axis=0,
        tiled=True,
    )
    fetched = returned.reshape(expert_count * slot_count, width)[safe_place]
    picked = jnp.sum(repeated.astype(jnp.float32) * fetched.astype(jnp.float32), axis=-1)
    prob_grad = jnp.where(keep_flat, picked, 0.0).reshape(tok_rows, TOP)
    mix_sum = jnp.sum(weights * prob_grad, axis=1, keepdims=True)
    chosen_grad = (prob_grad - mix_sum) / gate_total * gate_values * (1.0 - gate_values)
    logit_grad = jnp.sum(onehot * chosen_grad[:, :, None], axis=1).astype(jnp.bfloat16)
    normed_grad = lax.dot_general(
        logit_grad, router, (((1,), (1,)), ((), ())), preferred_element_type=jnp.float32
    )
    mixed_grad = (
        grad_rows.astype(jnp.float32)
        + inverse * normed_grad
        - mixed
        * inverse
        * inverse
        * inverse
        * jnp.mean(normed_grad * mixed, axis=-1, keepdims=True)
    )
    grad_residual = mixed_grad.astype(jnp.bfloat16)
    cotangent = grad_residual.astype(jnp.float32).reshape(tok_rows, HEADS, HD)
    adjoint_term = scaling * jnp.einsum(
        "thd,the->hde", q_carried, cotangent, precision=HIGHEST_PRECISION
    )
    state_grad = carried_in_2((passing, adjoint_term), "ctx", compose, identity_pair)[1]
    grad_q, grad_k, grad_v, grad_g = pullback((cotangent, state_grad))
    return (
        grad_q.reshape(1, tok_rows, width).astype(jnp.bfloat16),
        grad_k.reshape(1, tok_rows, width).astype(jnp.bfloat16),
        grad_v.reshape(1, tok_rows, width).astype(jnp.bfloat16),
        grad_g.reshape(1, tok_rows, width).astype(jnp.bfloat16),
        grad_residual[None],
        new_weight[None],
        new_moment[None],
    )


def solution(mesh):
    in_specs = (
        P("exp", "ctx", None),
        P("exp", "ctx", None),
        P("exp", "ctx", None),
        P("exp", "ctx", None),
        P("exp", "ctx"),
        P("exp", "ctx", None),
        P("exp", "ctx", None),
        P("exp", "ctx", None),
        P("exp", "ctx", None),
        P(),
        P(("ctx", "exp"), None, None),
        P(("ctx", "exp"), None, None),
        P(("ctx", "exp"), None, None),
    )
    out_specs = (
        P("exp", "ctx", None),
        P("exp", "ctx", None),
        P("exp", "ctx", None),
        P("exp", "ctx", None),
        P("exp", "ctx", None),
        P(("ctx", "exp"), None, None),
        P(("ctx", "exp"), None, None),
    )
    return jax.shard_map(local, mesh=mesh, in_specs=in_specs, out_specs=out_specs, check_vma=False)
```

profile of v0, /device:TPU:1, one launch (start us, length us, event | category | flops | bytes accessed | tf_op | source)
XLA Modules:
  0.0 649.7 jit_solution(14651115743365016117)
XLA Ops:
  12.7 1.5 copy.226
  16.1 3.2 exponential_multiply_fusion
  19.3 1.8 copy.229
  24.9 3.3 convolution_convert_fusion.1
  28.2 7.5 %convolution_convert_fusion = bf16[1536,2304]{1,0:T(8,128)(2,1)} fusion(bf16[1,512,2304]{2,1,0:T(8,128)(2,1)} %param.28, bf16[1,1536,512]{2,1,0:T(8,128)(2,1)S(1)} %copy-done), kind=kOutput, calls=%fused_computation.8 | convolution fusion | flops 3627417600 | bytes 11010048 | tf_op jit(solution)/shard_map/dot_general | solution.py:99
  35.7 11.1 %reshape.413 = bf16[128,12,2304]{2,1,0:T(8,128)(2,1)} reshape(bf16[1536,2304]{1,0:T(8,128)(2,1)} %convolution_convert_fusion) | data formatting | bytes 14155776 | tf_op jit(solution)/shard_map/reshape | solution.py:214
  46.8 12.0 %all-to-all-start = ((bf16[128,12,2304]{2,1,0:T(8,128)(2,1)}), bf16[128,12,2304]{2,1,0:T(8,128)(2,1)}, u32[]{:S(2)}, u32[]{:S(2)}) async-start(bf16[128,12,2304]{2,1,0:T(8,128)(2,1)} %reshape.413), calls=%async_computation | async-start | bytes 18874368 | tf_op jit(solution)/shard_map/all_to_all | solution.py:213
  59.1 155.6 %all_gather.18 = bf16[16,18,128]{2,1,0:T(8,128)(2,1)S(1)} all-gather(bf16[1,18,128]{2,1,0:T(8,128)(2,1)S(1)} %copy.234), channel_id=1, replica_groups=mesh['ctx'=16,'exp'=8] {'ctx'}, dimensions={0}, use_global_device_ids=true | all-gather | bytes 78336 | tf_op jit(solution)/shard_map/all_gather | solution.py:22
  215.4 5.3 convolution_select_fusion
  220.8 11.2 %reshape.414 = bf16[1536,2304]{1,0:T(8,128)(2,1)} reshape(bf16[128,12,2304]{2,1,0:T(8,128)(2,1)} %all-to-all-done) | data formatting | bytes 14155776 | tf_op jit(solution)/shard_map/reshape | solution.py:220
  232.0 13.7 %gather_fusion = bf16[1024,2304]{1,0:T(8,128)(2,1)} fusion(bf16[1536,2304]{1,0:T(8,128)(2,1)} %reshape.414, s32[1024]{0:T(1024)S(1)} %broadcast_clamp_fusion), kind=kCustom, calls=%fused_computation | custom fusion | bytes 9441280 | tf_op jit(solution)/shard_map/gather | solution.py:220
  245.7 3.3 fusion
  250.0 3.5 convolution_bitcast_fusion.2
  256.0 2.7 copy.240
  258.7 1.8 multiply_reduce_fusion.2
  260.7 1.4 fusion.30
  263.1 2.2 multiply_reduce_fusion.1
  265.4 1.8 convert_multiply_fusion.3
  267.2 2.1 copy.254
  269.3 3.4 fusion.25
  273.0 7.7 %scatter_custom_fusion = bf16[1536]{0:T(1024)(128)(2,1)S(1)} fusion(s32[1024]{0:T(1024)} %bitcast.194, bf16[1024]{0:T(1024)(128)(2,1)S(1)} %reshape.445, bf16[]{:T(256)} %constant.108.clone.1), kind=kCustom, calls=%fused_computation.100 | custom fusion | bytes 3584 | tf_op jit(solution)/shard_map/scatter | solution.py:190
  281.4 36.1 %all-to-all-start.1 = ((bf16[128,1,12]{2,1,0:T(2,128)(2,1)}), bf16[128,1,12]{2,1,0:T(2,128)(2,1)S(1)}, u32[]{:S(2)}, u32[]{:S(2)}) async-start(bf16[128,1,12]{2,1,0:T(2,128)(2,1)} %all_to_all.16), calls=%async_computation.1 | async-start | bytes 131072 | tf_op jit(solution)/shard_map/all_to_all | solution.py:200
  317.5 11.6 %scatter_custom_fusion.1 = bf16[1536,2304]{1,0:T(8,128)(2,1)} fusion(s32[1024]{0:T(1024)} %bitcast.195, bf16[]{:T(256)} %constant.108.clone.1, bf16[128,2304]{1,0:T(8,128)(2,1)} %bitcast.174), kind=kCustom, calls=%fused_computation.24 | custom fusion | bytes 7668224 | tf_op jit(solution)/shard_map/scatter | solution.py:185
  329.1 11.1 %reshape.419 = bf16[128,12,2304]{2,1,0:T(8,128)(2,1)} reshape(bf16[1536,2304]{1,0:T(8,128)(2,1)} %scatter_custom_fusion.1) | data formatting | bytes 14155776 | tf_op jit(solution)/shard_map/reshape | solution.py:194
  340.2 10.5 %all-to-all-start.2 = ((bf16[128,12,2304]{2,1,0:T(8,128)(2,1)}), bf16[128,12,2304]{2,1,0:T(8,128)(2,1)}, u32[]{:S(2)}, u32[]{:S(2)}) async-start(bf16[128,12,2304]{2,1,0:T(8,128)(2,1)} %reshape.419), calls=%async_computation.2 | async-start | bytes 18874368 | tf_op jit(solution)/shard_map/all_to_all | solution.py:193
  350.7 4.3 copy.242
  355.0 4.3 copy.272
  359.3 2.7 copy.247
  362.0 2.5 convolution_select_fusion.1
  364.5 3.2 convolution_bitcast_fusion.1
  367.7 2.2 convolution_multiply_fusion.2
  369.9 2.5 fusion.20
  372.5 116.0 %all-to-all-done.2 = bf16[128,12,2304]{2,1,0:T(8,128)(2,1)} async-done(((bf16[128,12,2304]{2,1,0:T(8,128)(2,1)}), bf16[128,12,2304]{2,1,0:T(8,128)(2,1)}, u32[]{:S(2)}, u32[]{:S(2)}) %all-to-all-start.2) | async-done | bytes 7077920 | tf_op jit(solution)/shard_map/all_to_all | solution.py:193
  488.4 9.0 %multiply_convert_fusion = bf16[128,12,2304]{2,1,0:T(8,128)(2,1)} fusion(bf16[128,12,2304]{2,1,0:T(8,128)(2,1)} %all-to-all-done.2, f32[128,12]{1,0:T(8,128)S(1)} %bitcast.187), kind=kLoop, calls=%fused_computation.7 | loop fusion | flops 10616832 | bytes 14161920 | tf_op jit(solution)/shard_map/convert_element_type | solution.py:100
  497.4 11.2 %convert_element_type.271 = bf16[1536,2304]{1,0:T(8,128)(2,1)} reshape(bf16[128,12,2304]{2,1,0:T(8,128)(2,1)} %multiply_convert_fusion) | data formatting | bytes 14155776 | tf_op jit(solution)/shard_map/convert_element_type | solution.py:100
  508.6 11.7 %fusion.13 = (bf16[1,512,2304]{1,2,0:T(8,128)(2,1)}, bf16[1,512,2304]{1,2,0:T(8,128)(2,1)}) fusion(bf16[1,512,2304]{1,2,0:T(8,128)(2,1)} %copy.272, bf16[1,512,2304]{1,2,0:T(8,128)(2,1)} %copy.242, bf16[1536,2304]{1,0:T(8,128)(2,1)} %convert_element_type.271, bf16[1,1536,512]{2,1,0:T(8,128)(2,1)S(1)} %copy-done), kind=kOutput, calls=%fused_computation.27 | convolution fusion | flops 3641573376 | bytes 18087936 | tf_op jit(solution)/shard_map/dot_general | solution.py:103
  520.3 4.3 copy.278
  524.6 4.3 copy.279
  529.0 35.5 %while.27 = (s32[]{:T(128)}, f32[18,128,128]{2,1,0:T(8,128)S(1)}, s32[]{:T(128)}, bf16[16,18,128]{2,1,0:T(8,128)(2,1)}, bf16[16,18,128,128]{3,2,1,0:T(8,128)(2,1...) while((s32[]{:T(128)}, f32[18,128,128]{2,1,0:T(8,128)S(1)}, s32[]{:T(128)}, ...), condition=%wide.region_12.13_spmd, body=%wide.region_11.12_spmd.sunk | while | flops 887046 | bytes 2972315 | solution.py:61
  529.7 1.6 convert_add_fusion.7
  532.0 1.6 convert_add_fusion.7
  534.4 1.6 convert_add_fusion.7
  536.7 1.6 convert_add_fusion.7
  539.0 1.6 convert_add_fusion.7
  541.4 1.6 convert_add_fusion.7
  543.7 1.6 convert_add_fusion.7
  546.1 1.6 convert_add_fusion.7
  548.4 1.6 convert_add_fusion.7
  550.7 1.6 convert_add_fusion.7
  553.1 1.6 convert_add_fusion.7
  555.4 1.6 convert_add_fusion.7
  557.8 1.6 convert_add_fusion.7
  560.1 1.6 convert_add_fusion.7
  562.4 1.6 convert_add_fusion.7
  564.5 5.0 fusion.39
  571.1 4.0 fusion.45
  578.7 2.1 copy.276
  580.8 2.9 fusion.26
  586.9 2.7 copy.266
  589.5 2.8 copy.267
  593.7 2.8 copy.271
  596.5 21.2 %reduce_window_sum.46 = f32[1,128,2304]{2,1,0:T(8,128)} reduce-window(f32[1,128,2304]{2,1,0:T(8,128)S(1)} %copy-done.23, f32[]{:T(128)} %constant.96.clone.1), window={size=1x128x1 pad=0_0x0_127x0_0}, to_apply=%region_15.16 | reduce-window | flops 37453824 | bytes 2359300 | tf_op jit(solution)/shard_map/transpose(jvp(jit(cumsum)))/reduce_window_sum | solution.py:65
  617.7 22.8 %reduce_window_sum.48 = f32[1,128,2304]{2,1,0:T(8,128)} reduce-window(f32[1,128,2304]{2,1,0:T(8,128)} %copy.271, f32[]{:T(128)} %constant.96.clone.1), window={size=1x128x1 pad=0_0x0_127x0_0}, to_apply=%region_16.17 | reduce-window | flops 37453824 | bytes 2359300 | tf_op jit(solution)/shard_map/transpose(jvp(jit(cumsum)))/reduce_window_sum | solution.py:78
  640.5 2.2 add_convert_fusion
  (140 shorter events, 37.8 us)
Async XLA Ops:
  7.2 21.0 %copy-start = (bf16[1,1536,512]{2,1,0:T(8,128)(2,1)S(1)}, bf16[1,1536,512]{2,1,0:T(8,128)(2,1)}, u32[]{:S(2)}) copy-start(bf16[1,1536,512]{2,1,0:T(8,128)(2,1)} %param.27) | copy-start | bytes 4718596
  7.2 242.0 %all-gather.5.cloned.1.call-start = ((), (), s32[]{:S(2)}) async-start(), calls=%async_computation.3 | async-start | bytes 10027008 | tf_op jit(solution)/shard_map/all_gather | solution.py:22
  10.3 1.4 copy-start.26
  19.3 196.1 %copy-start.3 = (f32[128,18,128]{2,0,1:T(8,128)}, f32[128,18,128]{2,0,1:T(8,128)S(1)}, u32[]{:S(2)}) copy-start(f32[128,18,128]{2,0,1:T(8,128)S(1)} %get-tuple-element.224) | copy-start | bytes 3538948
  46.8 12.0 %copy-start.29 = (s32[1,128,8]{1,2,0:T(8,128)S(1)}, s32[1,128,8]{1,2,0:T(8,128)}, u32[]{:S(2)}) copy-start(s32[1,128,8]{1,2,0:T(8,128)} %param.24) | copy-start | bytes 12292
  46.8 12.1 %copy-start.28 = (s32[1,128,8]{1,2,0:T(8,128)S(1)}, s32[1,128,8]{1,2,0:T(8,128)}, u32[]{:S(2)}) copy-start(s32[1,128,8]{1,2,0:T(8,128)} %param.25) | copy-start | bytes 12292
  46.8 174.0 %all-to-all-start = ((bf16[128,12,2304]{2,1,0:T(8,128)(2,1)}), bf16[128,12,2304]{2,1,0:T(8,128)(2,1)}, u32[]{:S(2)}, u32[]{:S(2)}) async-start(bf16[128,12,2304]{2,1,0:T(8,128)(2,1)} %reshape.413), calls=%async_computation | async-start | bytes 18874368 | tf_op jit(solution)/shard_map/all_to_all | solution.py:213
  58.7 470.1 %all-gather.7.cloned.1.call-start = ((), (), s32[]{:S(2)}) async-start(), calls=%async_computation.4 | async-start | bytes 10027008 | tf_op jit(solution)/shard_map/all_gather | solution.py:44
  215.4 5.3 copy-start.17
  249.3 0.7 copy-start.30
  249.7 3.8 copy-start.27
  249.7 118.0 %copy-start.1 = (f32[18,128,128]{2,1,0:T(8,128)}, f32[18,128,128]{2,1,0:T(8,128)S(1)}, u32[]{:S(2)}) copy-start(f32[18,128,128]{2,1,0:T(8,128)S(1)} %get-tuple-element.135) | copy-start | bytes 3538948
  250.0 3.6 copy-start.14
  258.7 1.8 copy-start.9
  258.7 1.9 copy-start.15
  260.7 1.4 copy-start.31
  263.1 2.2 copy-start.10
  263.1 2.2 copy-start.16
  263.1 2.3 copy-start.18
  263.1 2.3 copy-start.32
  281.4 58.8 %all-to-all-start.1 = ((bf16[128,1,12]{2,1,0:T(2,128)(2,1)}), bf16[128,1,12]{2,1,0:T(2,128)(2,1)S(1)}, u32[]{:S(2)}, u32[]{:S(2)}) async-start(bf16[128,1,12]{2,1,0:T(2,128)(2,1)} %all_to_all.16), calls=%async_computation.1 | async-start | bytes 131072 | tf_op jit(solution)/shard_map/all_to_all | solution.py:200
  340.2 148.2 %all-to-all-start.2 = ((bf16[128,12,2304]{2,1,0:T(8,128)(2,1)}), bf16[128,12,2304]{2,1,0:T(8,128)(2,1)}, u32[]{:S(2)}, u32[]{:S(2)}) async-start(bf16[128,12,2304]{2,1,0:T(8,128)(2,1)} %reshape.419), calls=%async_computation.2 | async-start | bytes 18874368 | tf_op jit(solution)/shard_map/all_to_all | solution.py:193
  362.0 2.5 copy-start.8
  364.5 3.2 copy-start.11
  367.7 2.2 copy-start.4
  367.7 2.2 copy-start.6
  564.5 5.0 copy-start.2
  564.5 5.4 copy-start.13
  564.5 5.4 copy-start.19
  564.5 5.4 copy-start.22
  569.5 1.3 copy-start.5
  569.5 1.6 copy-start.7
  575.1 2.5 copy-start.25
  577.6 3.2 copy-start.12
  583.7 2.0 copy-start.21
  589.5 2.8 copy-start.20
  593.7 2.8 copy-start.23
  617.7 22.8 %copy-start.24 = (f32[1,128,2304]{2,1,0:T(8,128)S(1)}, f32[1,128,2304]{2,1,0:T(8,128)}, u32[]{:S(2)}) copy-start(f32[1,128,2304]{2,1,0:T(8,128)} %reduce_window_sum.46) | copy-start | bytes 3538948
Sparse Core Ops, SparseCore 0:
  28.3 174.8 all-gather.4
  272.9 186.0 all-gather.6
where the time goes:
time: 659 us; the launch traced here: 650 us
  blocking collectives  156 us (24%)
  local copies, waits for them, and re-layouts  133 us (20%)
  waiting for transfers between devices  116 us (18%)
  other arithmetic  108 us (16%)
  matrix products  61.8 us (9%)
  starting transfers between devices  58.6 us (9%)
  between operations  15.4 us (2%)
    all_gather x1, blocking collectives, carried_in(): lax.all_gather(a.astype(kind), axis)  156 us
    all_to_all x1, waiting for transfers between devices, local(): lax.all_to_all(outgoing.reshape(expert_count, slot_count, width), ('ctx',...  116 us
    all_to_all x1, starting transfers between devices, local(): lax.all_to_all(outgoing_weight.reshape(expert_count, slot_count), ('ctx',...  36.1 us
    unnamed x78, local copies, waits for them, and re-layouts  28.8 us
    add x15, other arithmetic, compose(): later_pair[0][..., None] * earlier[1] + later_pair[1]  24.1 us
    another operation x2, other arithmetic, block_forward(): cumul = jnp.cumsum(decay_block, axis=0)  24.1 us
    another operation x1, other arithmetic, summary(): cumul = jnp.cumsum(decay_block, axis=0)  21.2 us
    gather x1, local copies, waits for them, and re-layouts, local(): fetched = returned.reshape(expert_count * slot_count, width)[safe_place]  13.7 us
  transfers between devices with their start and end apart: 5, of which 1 were waited for; matrix products, arithmetic and copies ran while one was open for 22% of the time, Pallas kernels for 0%

commit v1 on v0

v1 whole, which is shorter than its diff:
```python
import jax
import jax.numpy as jnp
from jax import lax
from jax.sharding import PartitionSpec as P

HEADS = 18
HD = 128
TOP = 8
NORM_EPS = 1e-06
LION_RATE = 0.001
BETA_ONE = 0.9
BETA_TWO = 0.99
WEIGHT_DECAY = 0.1
BF = jnp.bfloat16
F32 = jnp.float32


def mm(spec, a, b):
    return jnp.einsum(spec, a.astype(BF), b.astype(BF), preferred_element_type=F32)


def split(x):
    hi = x.astype(BF)
    lo = (x - hi.astype(F32)).astype(BF)
    return hi, lo


def heads(array):
    return array[0].reshape(array.shape[1], HEADS, HD).swapaxes(0, 1)


def unheads(array):
    return array.swapaxes(0, 1).reshape(1, array.shape[1], HEADS * HD)


def to_groups(state, count):
    return state.reshape(HEADS, count, HD // count, HD).swapaxes(0, 1)


def from_groups(parts, count):
    return parts.swapaxes(0, 1).reshape(HEADS, HD, HD)


def exchange(x, axis):
    return lax.all_to_all(x, axis, split_axis=0, concat_axis=0, tiled=True)


def scan_states(blocks, passing, reverse):
    count = blocks.shape[0]
    state = jnp.zeros(blocks.shape[1:], F32)
    out = [None] * count
    order = range(count - 1, -1, -1) if reverse else range(count)
    for j in order:
        out[j] = state.astype(BF)
        state = passing[j][:, None, :] * state + blocks[j].astype(F32)
    return jnp.stack(out)


def local(
    queries, key_vectors, values, log_decay, starts, residual_in, out_grad,
    expert_ids, slot_index, router, hidden_saved, w_down, momentum,
):
    tok = queries.shape[1]
    width = queries.shape[2]
    n_ctx = lax.axis_size("ctx")
    n_dev = lax.axis_size(("ctx", "exp"))
    scaling = HD ** (-0.5)
    n_exp = router.shape[1]
    slots = hidden_saved.shape[1] // n_dev
    ids = expert_ids[0]
    rank = slot_index[0]
    keep = rank < slots
    place = jnp.where(keep, ids * slots + rank, -1)
    rows = jnp.arange(n_exp * slots, dtype=jnp.int32)
    hit = jnp.zeros((n_exp * slots, tok), F32)
    for j in range(TOP):
        hit = hit + (rows[:, None] == place[None, :, j]).astype(F32)
    grad_rows = out_grad[0]
    outgoing = jnp.dot(hit.astype(BF), grad_rows, preferred_element_type=F32).astype(BF)
    incoming = exchange(outgoing.reshape(n_exp, slots, width), ("ctx", "exp"))
    start_row = starts[0]
    segment = jnp.cumsum(start_row, dtype=jnp.int32)
    position = jnp.arange(tok, dtype=jnp.int32)
    lower = position[:, None] >= position[None, :]
    allowed = (segment[:, None] == segment[None, :]) & lower
    carried = (segment == 0).astype(F32)[None, :, None]
    tail = (segment == segment[-1]).astype(F32)[None, :, None]
    q = heads(queries).astype(F32)
    k = heads(key_vectors).astype(F32)
    v = heads(values)
    g = heads(log_decay)
    tri = lower.astype(BF)
    cum = jnp.einsum("ts,hsd->htd", tri, g, preferred_element_type=F32)
    last = cum[:, -1:, :]
    grow = jnp.exp(cum)
    shrink = jnp.exp(-cum)
    end_decay = jnp.exp(last - cum) * tail
    q_dec = (q * grow).astype(BF)
    k_dec = (k * shrink).astype(BF)
    key_end = (k * end_decay).astype(BF)
    q_car = (q_dec * carried).astype(BF)
    fresh = mm("hse,hsd->hed", v, key_end)
    passing = jnp.exp(last[:, 0, :]) * (segment[-1] == 0).astype(F32)
    got = exchange(to_groups(fresh, n_ctx).astype(BF), "ctx")
    passing_all = lax.all_gather(passing.astype(BF), "ctx").astype(F32)
    state = from_groups(exchange(scan_states(got, passing_all, False), "ctx"), n_ctx)
    scores = jnp.where(allowed[None], mm("htd,hsd->hts", q_dec, k_dec), 0.0).astype(BF)
    attended = scaling * (mm("hts,hse->hte", scores, v) + mm("htd,hed->hte", q_car, state))
    attn_round = unheads(attended)[0].astype(BF)
    mixed = residual_in[0].astype(F32) + attn_round.astype(F32)
    inverse = lax.rsqrt(jnp.mean(mixed * mixed, axis=-1, keepdims=True) + NORM_EPS)
    normed = (mixed * inverse).astype(BF)
    logits = jnp.dot(normed, router, preferred_element_type=F32)
    onehot = (ids[:, :, None] == jnp.arange(n_exp, dtype=jnp.int32)).astype(F32)
    chosen = jnp.sum(onehot * logits[:, None, :], axis=-1)
    gate = jax.nn.sigmoid(chosen)
    total = jnp.sum(gate, axis=1, keepdims=True)
    weights = gate / total
    slot_ids = jnp.arange(slots, dtype=jnp.int32)
    slot_hot = (rank[:, :, None] == slot_ids).astype(F32)
    w_hot = slot_hot * weights.astype(BF).astype(F32)[:, :, None]
    w_out = jnp.einsum("tje,tjs->es", onehot, w_hot, precision=lax.Precision.HIGHEST)
    w_in = exchange(w_out.astype(BF), ("ctx", "exp"))
    gathered = incoming.reshape(n_dev * slots, width)
    saved = hidden_saved[0]
    produced = jnp.dot(saved, w_down[0], preferred_element_type=F32).astype(BF)
    slot_score = jnp.sum(gathered.astype(F32) * produced.astype(F32), axis=-1)
    score_back = exchange(slot_score.reshape(n_dev, slots), ("ctx", "exp"))
    scaled = (w_in.reshape(-1, 1).astype(F32) * gathered.astype(F32)).astype(BF)
    gradient = lax.dot_general(saved, scaled, (((0,), (0,)), ((), ())), preferred_element_type=F32)
    wf = w_down[0].astype(F32)
    mf = momentum[0].astype(F32)
    direction = jnp.sign(BETA_ONE * mf + (1.0 - BETA_ONE) * gradient)
    new_weight = (wf - LION_RATE * (direction + WEIGHT_DECAY * wf)).astype(BF)
    new_moment = (BETA_TWO * mf + (1.0 - BETA_TWO) * gradient).astype(BF)
    per_expert = jnp.einsum("tje,es->tjs", onehot, score_back, precision=lax.Precision.HIGHEST)
    prob_grad = jnp.sum(per_expert * slot_hot, axis=-1)
    mix_sum = jnp.sum(weights * prob_grad, axis=1, keepdims=True)
    chosen_grad = (prob_grad - mix_sum) / total * gate * (1.0 - gate)
    logit_grad = jnp.sum(onehot * chosen_grad[:, :, None], axis=1).astype(BF)
    normed_grad = lax.dot_general(logit_grad, router, (((1,), (1,)), ((), ())), preferred_element_type=F32)
    mixed_grad = (
        grad_rows.astype(F32)
        + inverse * normed_grad
        - mixed * inverse * inverse * inverse * jnp.mean(normed_grad * mixed, axis=-1, keepdims=True)
    )
    grad_residual = mixed_grad.astype(BF)
    cot = heads(grad_residual[None])
    adjoint = scaling * mm("hte,htd->hed", cot, q_car)
    got_back = exchange(to_groups(adjoint, n_ctx).astype(BF), "ctx")
    state_grad = from_groups(exchange(scan_states(got_back, passing_all, True), "ctx"), n_ctx)
    d_scores = (scaling * jnp.where(allowed[None], mm("hte,hse->hts", cot, v), 0.0)).astype(BF)
    dq_dec = mm("hts,hsd->htd", d_scores, k_dec) + carried * scaling * mm("hte,hed->htd", cot, state)
    dk_dec = mm("hts,htd->hsd", d_scores, q_dec)
    dk_end = mm("hse,hed->hsd", v, state_grad)
    dv = scaling * mm("hts,hte->hse", scores, cot) + mm("hsd,hed->hse", key_end, state_grad)
    dq = dq_dec * grow
    dk = dk_dec * shrink + dk_end * end_decay
    end_term = dk_end * key_end.astype(F32)
    d_cum = dq_dec * q_dec.astype(F32) - dk_dec * k_dec.astype(F32) - end_term
    d_last = jnp.sum(end_term, axis=1, keepdims=True) + passing[:, None, :] * jnp.sum(
        state.astype(F32) * state_grad.astype(F32), axis=1, keepdims=True
    )
    hi, lo = split(d_cum)
    upper = tri.T
    dg = (
        jnp.einsum("ts,hsd->htd", upper, hi, preferred_element_type=F32)
        + jnp.einsum("ts,hsd->htd", upper, lo, preferred_element_type=F32)
        + d_last
    )
    return (
        unheads(dq).astype(BF),
        unheads(dk).astype(BF),
        unheads(dv).astype(BF),
        unheads(dg).astype(BF),
        grad_residual[None],
        new_weight[None],
        new_moment[None],
    )


def solution(mesh):
    tokens = P("exp", "ctx", None)
    owned = P(("ctx", "exp"), None, None)
    in_specs = (tokens,) * 4 + (P("exp", "ctx"),) + (tokens,) * 4 + (P(),) + (owned,) * 3
    out_specs = (tokens,) * 5 + (owned,) * 2
    return jax.shard_map(local, mesh=mesh, in_specs=in_specs, out_specs=out_specs, check_vma=False)
```

time: 659 us -> 383 us (0.58)
  blocking collectives: 156 us -> 22 us
  other arithmetic: 108 us -> 51 us
  local copies, waits for them, and re-layouts: 133 us -> 89.8 us
  between operations: 15.4 us -> 2.04 us
  matrix products: 61.8 us -> 50.3 us
  waiting for transfers between devices: 116 us -> 107 us
    all_gather x1, blocking collectives: 156 us -> 22 us  [local(): passing_all = lax.all_gather(passing.astype(BF), 'ctx').astype(F32)]
    another operation x3 -> x1, other arithmetic: 45.3 us -> 0.64 us  [scan_states(): return jnp.stack(out)]
    unnamed x0 -> x29, other arithmetic: none -> 26.6 us
    add x15 -> x1, other arithmetic: 24.1 us -> 0.03 us  [local(): jnp.sum(end_term, axis=1, keepdims=True)]
    reshape x4 -> x2, local copies, waits for them, and re-layouts: 34.4 us -> 11.9 us  [the longest x1 11 us: local(): incoming = exchange(outgoing.reshape(n_exp, slots, width), ('ctx', 'exp'))]
    scatter x2 -> x0, local copies, waits for them, and re-layouts: 19.3 us -> none  [the longest x1 11.6 us: local(): outgoing = jnp.zeros((expert_count * slot_count, width), jnp.bfloat16).at...]
    convert_element_type x11 -> x13, local copies, waits for them, and re-layouts: 22.8 us -> 38.6 us  [the longest x1 13 us: local(): slot_score = jnp.sum(gathered.astype(F32) * produced.astype(F32), axis=-1)]
    dot_general x15 -> x18, matrix products: 59.6 us -> 45.4 us  [the longest x12 18.1 us: mm(): jnp.einsum(spec, a.astype(BF), b.astype(BF), preferred_element_type=F32)]
  transfers between devices with their start and end apart: 5 -> 7, of which waited for: 1 -> 2; matrix products, arithmetic and copies ran while one was open for 22% -> 23% of each run, Pallas kernels for 0% -> 0%
where the time goes in v1:
time: 383 us; the launch traced here: 380 us
  waiting for transfers between devices  107 us (28%)
  local copies, waits for them, and re-layouts  89.8 us (23%)
  starting transfers between devices  57.7 us (15%)
  other arithmetic  51 us (13%)
  matrix products  50.3 us (13%)
  blocking collectives  22 us (6%)
    all_to_all x7, waiting for transfers between devices, exchange(): return lax.all_to_all(x, axis, split_axis=0, concat_axis=0, tiled=True)  107 us
    all_to_all x7, starting transfers between devices, exchange(): return lax.all_to_all(x, axis, split_axis=0, concat_axis=0, tiled=True)  57.7 us
    unnamed x110, local copies, waits for them, and re-layouts  29.7 us
    unnamed x29, other arithmetic  26.6 us
    all_gather x1, blocking collectives, local(): passing_all = lax.all_gather(passing.astype(BF), 'ctx').astype(F32)  22 us
    dot_general x12, matrix products, mm(): jnp.einsum(spec, a.astype(BF), b.astype(BF), preferred_element_type=F32)  18.1 us
    convert_element_type x1, local copies, waits for them, and re-layouts, local(): slot_score = jnp.sum(gathered.astype(F32) * produced.astype(F32), axis=-1)  13 us
    dot_general x1, matrix products, local(): lax.dot_general(saved, scaled, (((0,), (0,)), ((), ())), preferred_elemen...  11.7 us
  transfers between devices with their start and end apart: 7, of which 2 were waited for; matrix products, arithmetic and copies ran while one was open for 23% of the time, Pallas kernels for 0%

profile of v1, /device:TPU:1, one launch (start us, length us, event | category | flops | bytes accessed | tf_op | source)
XLA Modules:
  0.0 379.8 jit_solution(1400053550588027335)
XLA Ops:
  2.3 2.5 fusion.42
  4.8 1.6 copy.180
  7.8 1.4 copy.177
  9.2 1.3 copy.178
  10.4 1.4 copy.181
  11.8 1.3 copy.182
  13.1 2.1 copy.183
  15.2 3.1 fusion.35
  19.6 7.6 %all-to-all-start = ((bf16[16,18,8,128]{3,2,1,0:T(8,128)(2,1)}), bf16[16,18,8,128]{3,2,1,0:T(8,128)(2,1)S(1)}, u32[]{:S(2)}, u32[]{:S(2)}) async-start(bf16[16,18,8,128]{3,2,1,0:T(8,128)(2,1)} %bitcast.261), calls=%async_computation | async-start | bytes 1179648 | tf_op jit(solution)/shard_map/all_to_all | solution.py:45
  27.1 22.0 %all-gather = bf16[288,1,128]{2,1,0:T(2,128)(2,1)S(1)} all-gather(bf16[18,1,128]{2,1,0:T(2,128)(2,1)S(1)} %get-tuple-element.68), channel_id=2, replica_groups=mesh['ctx'=16,'exp'=8] {'ctx'}, dimensions={0}, use_global_device_ids=true | all-gather | bytes 78336 | tf_op jit(solution)/shard_map/all_gather | solution.py:105
  59.6 3.8 all-to-all-start.1
  63.4 6.5 %convolution_convert_fusion.1 = bf16[1536,2304]{1,0:T(8,128)(2,1)} fusion(bf16[1,128,2304]{2,1,0:T(8,128)(2,1)} %param.19, s32[128]{0:T(128)S(1)} %get-tuple-element.88, s32[128]{0:T(128)S(1)} %get-tuple-element.89, s32[128]{0:T(128)S(1)} %get-tuple-element.90, s32[128]{0:T(128)S(1)} %get-tuple-element.91, s32[128]{0:T(128)S(1)} %get-tuple-element.92, ...), kind=kOutput, calls=%fused_computation.3 | convolution fusion | flops 914227200 | bytes 7671808 | tf_op jit(solution)/shard_map/dot_general | solution.py:79
  69.8 11.0 %reshape.324 = bf16[128,12,2304]{2,1,0:T(8,128)(2,1)} reshape(bf16[1536,2304]{1,0:T(8,128)(2,1)} %convolution_convert_fusion.1) | data formatting | bytes 14155776 | tf_op jit(solution)/shard_map/reshape | solution.py:80
  80.9 17.2 %all-to-all-start.2 = ((bf16[128,12,2304]{2,1,0:T(8,128)(2,1)}), bf16[128,12,2304]{2,1,0:T(8,128)(2,1)}, u32[]{:S(2)}, u32[]{:S(2)}) async-start(bf16[128,12,2304]{2,1,0:T(8,128)(2,1)} %reshape.324), calls=%async_computation.2 | async-start | bytes 18874368 | tf_op jit(solution)/shard_map/all_to_all | solution.py:45
  98.0 4.3 %copy.191 = bf16[1,512,2304]{1,2,0:T(8,128)(2,1)} copy(bf16[1,512,2304]{2,1,0:T(8,128)(2,1)} %param.24) | data formatting | bytes 4718592 | tf_op args[11]
  102.3 4.3 %copy.218 = bf16[1,512,2304]{1,2,0:T(8,128)(2,1)} copy(bf16[1,512,2304]{2,1,0:T(8,128)(2,1)} %param.25) | data formatting | bytes 4718592 | tf_op args[12]
  108.7 1.6 fusion.21
  110.3 2.7 copy.189
  113.0 1.6 copy.190
  114.6 1.4 multiply_reduce_fusion.3
  117.0 97.7 %all-to-all-done.2 = bf16[128,12,2304]{2,1,0:T(8,128)(2,1)} async-done(((bf16[128,12,2304]{2,1,0:T(8,128)(2,1)}), bf16[128,12,2304]{2,1,0:T(8,128)(2,1)}, u32[]{:S(2)}, u32[]{:S(2)}) %all-to-all-start.2) | async-done | bytes 7077920 | tf_op jit(solution)/shard_map/all_to_all | solution.py:45
  214.7 13.0 %reshape.328 = f32[1536,2304]{1,0:T(8,128)} reshape(bf16[128,12,2304]{2,1,0:T(8,128)(2,1)} %all-to-all-done.2) | data formatting | bytes 21233664 | tf_op jit(solution)/shard_map/convert_element_type | solution.py:127
  227.8 7.9 %multiply_reduce_fusion = f32[1536]{0:T(1024)S(1)} fusion(f32[1536,2304]{1,0:T(8,128)} %reshape.328, bf16[1,512,2304]{2,1,0:T(8,128)(2,1)} %param.24, bf16[1,1536,512]{2,1,0:T(8,128)(2,1)S(1)} %copy-done), kind=kOutput, calls=%fused_computation.1 | convolution fusion | flops 3638032896 | bytes 18094080 | tf_op jit(solution)/shard_map/dot_general | solution.py:126
  236.4 11.0 %all-to-all-start.3 = ((f32[128,1,12]{2,1,0:T(1,128)}), f32[128,1,12]{2,1,0:T(1,128)S(1)}, u32[]{:S(2)}, u32[]{:S(2)}) async-start(f32[128,1,12]{2,1,0:T(1,128)} %bitcast.51), calls=%async_computation.3 | async-start | bytes 131072 | tf_op jit(solution)/shard_map/all_to_all | solution.py:45
  247.4 9.3 %all-to-all-done.3 = f32[128,1,12]{2,1,0:T(1,128)S(1)} async-done(((f32[128,1,12]{2,1,0:T(1,128)}), f32[128,1,12]{2,1,0:T(1,128)S(1)}, u32[]{:S(2)}, u32[]{:S(2)}) %all-to-all-start.3) | async-done | bytes 6176 | tf_op jit(solution)/shard_map/all_to_all | solution.py:45
  257.6 1.7 multiply_reduce_fusion.2
  259.4 1.3 subtract_convert_fusion.1
  260.7 1.4 copy.194
  262.6 1.4 fusion.103
  264.0 1.3 fusion.102
  265.3 2.7 convolution_multiply_fusion
  269.2 4.8 %all-to-all-start.6 = ((bf16[128,1,12]{2,1,0:T(2,128)(2,1)}), bf16[128,1,12]{2,1,0:T(2,128)(2,1)S(1)}, u32[]{:S(2)}, u32[]{:S(2)}) async-start(bf16[128,1,12]{2,1,0:T(2,128)(2,1)} %copy.219), calls=%async_computation.6 | async-start | bytes 131072 | tf_op jit(solution)/shard_map/all_to_all | solution.py:45
  274.0 3.3 fusion.33
  278.7 2.6 copy.212
  281.4 2.1 copy.203
  283.5 2.1 copy.220
  285.6 6.8 %all-to-all-start.4 = ((bf16[16,18,8,128]{3,2,1,0:T(8,128)(2,1)}), bf16[16,18,8,128]{3,2,1,0:T(8,128)(2,1)}, u32[]{:S(2)}, u32[]{:S(2)}) async-start(bf16[16,18,8,128]{3,2,1,0:T(8,128)(2,1)} %bitcast.285), calls=%async_computation.4 | async-start | bytes 1179648 | tf_op jit(solution)/shard_map/all_to_all | solution.py:45
  292.4 9.0 %multiply_convert_fusion = bf16[128,12,2304]{2,1,0:T(8,128)(2,1)} fusion(f32[128,12]{1,0:T(8,128)S(1)} %bitcast.289, bf16[128,12,2304]{2,1,0:T(8,128)(2,1)} %all-to-all-done.2), kind=kLoop, calls=%fused_computation | loop fusion | flops 10616832 | bytes 14161920 | tf_op jit(solution)/shard_map/convert_element_type | solution.py:129
  301.5 11.3 %convert_element_type.890 = bf16[1536,2304]{1,0:T(8,128)(2,1)} reshape(bf16[128,12,2304]{2,1,0:T(8,128)(2,1)} %multiply_convert_fusion) | data formatting | bytes 14155776 | tf_op jit(solution)/shard_map/convert_element_type | solution.py:129
  312.8 1.8 constant_dynamic-update-slice_fusion.31
  314.6 1.4 constant_dynamic-update-slice_fusion.30
  316.6 1.4 constant_dynamic-update-slice_fusion.28
  318.7 1.4 constant_dynamic-update-slice_fusion.26
  320.7 1.4 constant_dynamic-update-slice_fusion.24
  322.7 1.4 constant_dynamic-update-slice_fusion.22
  324.7 1.5 constant_dynamic-update-slice_fusion.20
  326.2 1.4 constant_dynamic-update-slice_fusion.19
  327.7 1.4 constant_dynamic-update-slice_fusion.18
  329.1 1.4 constant_dynamic-update-slice_fusion.17
  331.1 6.6 %all-to-all-start.5 = ((bf16[16,18,8,128]{3,2,1,0:T(8,128)(2,1)}), bf16[16,18,8,128]{3,2,1,0:T(8,128)(2,1)}, u32[]{:S(2)}, u32[]{:S(2)}) async-start(bf16[16,18,8,128]{3,2,1,0:T(8,128)(2,1)} %constant_dynamic-update-slice_fusion.16), calls=%async_computation.5 | async-start | bytes 1179648 | tf_op jit(solution)/shard_map/all_to_all | solution.py:45
  337.7 11.7 %fusion.9 = (bf16[1,512,2304]{1,2,0:T(8,128)(2,1)}, bf16[1,512,2304]{1,2,0:T(8,128)(2,1)}) fusion(bf16[1,512,2304]{1,2,0:T(8,128)(2,1)} %copy.218, bf16[1,512,2304]{1,2,0:T(8,128)(2,1)} %copy.191, bf16[1536,2304]{1,0:T(8,128)(2,1)} %convert_element_type.890, bf16[1,1536,512]{2,1,0:T(8,128)(2,1)S(1)} %copy-done), kind=kOutput, calls=%fused_computation.17 | convolution fusion | flops 3641573376 | bytes 18087936 | tf_op jit(solution)/shard_map/dot_general | solution.py:130
  349.5 4.3 %copy.224 = bf16[1,512,2304]{2,1,0:T(8,128)(2,1)} copy(bf16[1,512,2304]{1,2,0:T(8,128)(2,1)} %get-tuple-element.61) | data formatting | bytes 4718592
  353.7 4.3 %copy.225 = bf16[1,512,2304]{2,1,0:T(8,128)(2,1)} copy(bf16[1,512,2304]{1,2,0:T(8,128)(2,1)} %get-tuple-element.60) | data formatting | bytes 4718592
  358.0 3.6 fusion.32
  361.6 2.7 copy.213
  364.3 2.9 fusion.40
  367.2 1.2 multiply_reduce_fusion.1
  368.5 1.1 subtract_convert_fusion
  370.3 1.4 copy.215
  371.9 1.2 add_convert_fusion
  373.2 2.2 copy.223
  375.4 2.0 fusion.26
  377.7 1.1 copy.222
  378.7 1.1 copy.221
  (162 shorter events, 26.6 us)
Async XLA Ops:
  0.6 227.1 %copy-start = (bf16[1,1536,512]{2,1,0:T(8,128)(2,1)S(1)}, bf16[1,1536,512]{2,1,0:T(8,128)(2,1)}, u32[]{:S(2)}) copy-start(bf16[1,1536,512]{2,1,0:T(8,128)(2,1)} %param.23) | copy-start | bytes 4718596
  6.4 8.8 %copy-start.1 = (f32[128,18,128]{2,0,1:T(8,128)}, f32[128,18,128]{2,0,1:T(8,128)S(1)}, u32[]{:S(2)}) copy-start(f32[128,18,128]{2,0,1:T(8,128)S(1)} %copy.180) | copy-start | bytes 3538948
  7.1 8.1 %copy-start.39 = (f32[18,1,128]{2,0,1:T(8,128)}, f32[18,1,128]{2,0,1:T(8,128)S(1)}, u32[]{:S(2)}) copy-start(f32[18,1,128]{2,0,1:T(8,128)S(1)} %copy.276) | copy-start | bytes 27652
  15.2 3.1 copy-start.7
  18.3 1.3 copy-start.3
  18.6 30.5 %copy-start.41 = (s32[1,128,8]{1,2,0:T(8,128)S(1)}, s32[1,128,8]{1,2,0:T(8,128)}, u32[]{:S(2)}) copy-start(s32[1,128,8]{1,2,0:T(8,128)} %param.20) | copy-start | bytes 12292
  18.6 30.5 %copy-start.42 = (s32[1,128,8]{1,2,0:T(8,128)S(1)}, s32[1,128,8]{1,2,0:T(8,128)}, u32[]{:S(2)}) copy-start(s32[1,128,8]{1,2,0:T(8,128)} %param.21) | copy-start | bytes 12292
  19.6 30.3 %all-to-all-start = ((bf16[16,18,8,128]{3,2,1,0:T(8,128)(2,1)}), bf16[16,18,8,128]{3,2,1,0:T(8,128)(2,1)S(1)}, u32[]{:S(2)}, u32[]{:S(2)}) async-start(bf16[16,18,8,128]{3,2,1,0:T(8,128)(2,1)} %bitcast.261), calls=%async_computation | async-start | bytes 1179648 | tf_op jit(solution)/shard_map/all_to_all | solution.py:45
  49.8 7.2 %copy-start.21 = (f32[18,128]{1,0:T(8,128)}, f32[18,128]{1,0:T(8,128)S(1)}, u32[]{:S(2)}) copy-start(f32[18,128]{1,0:T(8,128)S(1)} %get-tuple-element.81) | copy-start | bytes 27652
  49.8 7.1 %copy-start.23 = (f32[18,128]{1,0:T(8,128)}, f32[18,128]{1,0:T(8,128)S(1)}, u32[]{:S(2)}) copy-start(f32[18,128]{1,0:T(8,128)S(1)} %get-tuple-element.74) | copy-start | bytes 27652
  49.8 7.1 %copy-start.25 = (f32[18,128]{1,0:T(8,128)}, f32[18,128]{1,0:T(8,128)S(1)}, u32[]{:S(2)}) copy-start(f32[18,128]{1,0:T(8,128)S(1)} %get-tuple-element.76) | copy-start | bytes 27652
  49.8 7.1 %copy-start.27 = (f32[18,128]{1,0:T(8,128)}, f32[18,128]{1,0:T(8,128)S(1)}, u32[]{:S(2)}) copy-start(f32[18,128]{1,0:T(8,128)S(1)} %get-tuple-element.78) | copy-start | bytes 27652
  49.8 7.1 %copy-start.29 = (f32[18,128]{1,0:T(8,128)}, f32[18,128]{1,0:T(8,128)S(1)}, u32[]{:S(2)}) copy-start(f32[18,128]{1,0:T(8,128)S(1)} %get-tuple-element.80) | copy-start | bytes 27652
  49.9 7.1 %copy-start.33 = (f32[18,128]{1,0:T(8,128)}, f32[18,128]{1,0:T(8,128)S(1)}, u32[]{:S(2)}) copy-start(f32[18,128]{1,0:T(8,128)S(1)} %get-tuple-element.75) | copy-start | bytes 27652
  49.9 7.1 %copy-start.35 = (f32[18,128]{1,0:T(8,128)}, f32[18,128]{1,0:T(8,128)S(1)}, u32[]{:S(2)}) copy-start(f32[18,128]{1,0:T(8,128)S(1)} %get-tuple-element.77) | copy-start | bytes 27652
  49.9 7.1 %copy-start.37 = (f32[18,128]{1,0:T(8,128)}, f32[18,128]{1,0:T(8,128)S(1)}, u32[]{:S(2)}) copy-start(f32[18,128]{1,0:T(8,128)S(1)} %get-tuple-element.79) | copy-start | bytes 27652
  49.9 7.8 %copy-start.31 = (f32[18,128]{1,0:T(8,128)}, f32[18,128]{1,0:T(8,128)S(1)}, u32[]{:S(2)}) copy-start(f32[18,128]{1,0:T(8,128)S(1)} %get-tuple-element.73) | copy-start | bytes 27652
  59.6 21.3 %all-to-all-start.1 = ((bf16[16,18,8,128]{3,2,1,0:T(8,128)(2,1)}), bf16[16,18,8,128]{3,2,1,0:T(8,128)(2,1)S(1)}, u32[]{:S(2)}, u32[]{:S(2)}) async-start(bf16[16,18,8,128]{3,2,1,0:T(8,128)(2,1)} %constant_dynamic-update-slice_fusion), calls=%async_computation.1 | async-start | bytes 1179648 | tf_op jit(solution)/shard_map/all_to_all | solution.py:45
  80.9 27.9 %copy-start.12 = (bf16[16,18,8,128]{3,2,1,0:T(8,128)(2,1)}, bf16[16,18,8,128]{3,2,1,0:T(8,128)(2,1)S(1)}, u32[]{:S(2)}) copy-start(bf16[16,18,8,128]{3,2,1,0:T(8,128)(2,1)S(1)} %all-to-all-done.1) | copy-start | bytes 1769476
  80.9 133.8 %all-to-all-start.2 = ((bf16[128,12,2304]{2,1,0:T(8,128)(2,1)}), bf16[128,12,2304]{2,1,0:T(8,128)(2,1)}, u32[]{:S(2)}, u32[]{:S(2)}) async-start(bf16[128,12,2304]{2,1,0:T(8,128)(2,1)} %reshape.324), calls=%async_computation.2 | async-start | bytes 18874368 | tf_op jit(solution)/shard_map/all_to_all | solution.py:45
  102.3 5.0 %copy-start.5 = (bf16[18,128,128]{2,1,0:T(8,128)(2,1)S(1)}, bf16[18,128,128]{2,1,0:T(8,128)(2,1)}, u32[]{:S(2)}) copy-start(bf16[18,128,128]{2,1,0:T(8,128)(2,1)} %get-tuple-element.63) | copy-start | bytes 1769476
  106.7 1.2 copy-start.8
  107.9 0.8 copy-start.16
  114.6 1.4 copy-start.10
  114.6 1.4 copy-start.20
  116.1 0.6 copy-start.45
  227.8 28.9 %copy-start.43 = (s32[1,128,8]{1,2,0:T(8,128)S(1)}, s32[1,128,8]{1,2,0:T(8,128)}, u32[]{:S(2)}) copy-start(s32[1,128,8]{1,2,0:T(8,128)} %param.21) | copy-start | bytes 12292
  236.4 20.3 %all-to-all-start.3 = ((f32[128,1,12]{2,1,0:T(1,128)}), f32[128,1,12]{2,1,0:T(1,128)S(1)}, u32[]{:S(2)}, u32[]{:S(2)}) async-start(f32[128,1,12]{2,1,0:T(1,128)} %bitcast.51), calls=%async_computation.3 | async-start | bytes 131072 | tf_op jit(solution)/shard_map/all_to_all | solution.py:45
  257.6 1.8 copy-start.11
  257.6 1.8 copy-start.18
  257.6 1.8 copy-start.46
  260.7 1.4 copy-start.9
  262.2 1.8 copy-start.14
  262.6 1.4 copy-start.6
  264.0 1.3 copy-start.17
  265.3 2.7 copy-start.44
  265.3 8.7 %copy-start.2 = (f32[128,18,128]{2,0,1:T(8,128)S(1)}, f32[128,18,128]{2,0,1:T(8,128)}, u32[]{:S(2)}) copy-start(f32[128,18,128]{2,0,1:T(8,128)} %copy-done.1) | copy-start | bytes 3538948
  265.3 8.7 %copy-start.47 = (f32[128]{0:T(128)S(1)}, f32[128]{0:T(128)}, u32[]{:S(2)}) copy-start(f32[128]{0:T(128)} %compare_select_fusion) | copy-start | bytes 1540
  269.2 16.4 %all-to-all-start.6 = ((bf16[128,1,12]{2,1,0:T(2,128)(2,1)}), bf16[128,1,12]{2,1,0:T(2,128)(2,1)S(1)}, u32[]{:S(2)}, u32[]{:S(2)}) async-start(bf16[128,1,12]{2,1,0:T(2,128)(2,1)} %copy.219), calls=%async_computation.6 | async-start | bytes 131072 | tf_op jit(solution)/shard_map/all_to_all | solution.py:45
  274.0 3.3 copy-start.15
  285.6 27.1 %all-to-all-start.4 = ((bf16[16,18,8,128]{3,2,1,0:T(8,128)(2,1)}), bf16[16,18,8,128]{3,2,1,0:T(8,128)(2,1)}, u32[]{:S(2)}, u32[]{:S(2)}) async-start(bf16[16,18,8,128]{3,2,1,0:T(8,128)(2,1)} %bitcast.285), calls=%async_computation.4 | async-start | bytes 1179648 | tf_op jit(solution)/shard_map/all_to_all | solution.py:45
  301.4 11.3 %copy-start.22 = (f32[18,128]{1,0:T(8,128)S(1)}, f32[18,128]{1,0:T(8,128)}, u32[]{:S(2)}) copy-start(f32[18,128]{1,0:T(8,128)} %copy-done.21) | copy-start | bytes 27652
  301.4 11.3 %copy-start.24 = (f32[18,128]{1,0:T(8,128)S(1)}, f32[18,128]{1,0:T(8,128)}, u32[]{:S(2)}) copy-start(f32[18,128]{1,0:T(8,128)} %copy-done.23) | copy-start | bytes 27652
  301.4 11.3 %copy-start.26 = (f32[18,128]{1,0:T(8,128)S(1)}, f32[18,128]{1,0:T(8,128)}, u32[]{:S(2)}) copy-start(f32[18,128]{1,0:T(8,128)} %copy-done.25) | copy-start | bytes 27652
  301.4 11.4 %copy-start.28 = (f32[18,128]{1,0:T(8,128)S(1)}, f32[18,128]{1,0:T(8,128)}, u32[]{:S(2)}) copy-start(f32[18,128]{1,0:T(8,128)} %copy-done.27) | copy-start | bytes 27652
  301.4 11.4 %copy-start.30 = (f32[18,128]{1,0:T(8,128)S(1)}, f32[18,128]{1,0:T(8,128)}, u32[]{:S(2)}) copy-start(f32[18,128]{1,0:T(8,128)} %copy-done.29) | copy-start | bytes 27652
  301.4 11.4 %copy-start.32 = (f32[18,128]{1,0:T(8,128)S(1)}, f32[18,128]{1,0:T(8,128)}, u32[]{:S(2)}) copy-start(f32[18,128]{1,0:T(8,128)} %copy-done.31) | copy-start | bytes 27652
  301.5 11.4 %copy-start.34 = (f32[18,128]{1,0:T(8,128)S(1)}, f32[18,128]{1,0:T(8,128)}, u32[]{:S(2)}) copy-start(f32[18,128]{1,0:T(8,128)} %copy-done.33) | copy-start | bytes 27652
  301.5 11.4 %copy-start.36 = (f32[18,128]{1,0:T(8,128)S(1)}, f32[18,128]{1,0:T(8,128)}, u32[]{:S(2)}) copy-start(f32[18,128]{1,0:T(8,128)} %copy-done.35) | copy-start | bytes 27652
  301.5 11.4 %copy-start.38 = (f32[18,128]{1,0:T(8,128)S(1)}, f32[18,128]{1,0:T(8,128)}, u32[]{:S(2)}) copy-start(f32[18,128]{1,0:T(8,128)} %copy-done.37) | copy-start | bytes 27652
  331.1 26.9 %all-to-all-start.5 = ((bf16[16,18,8,128]{3,2,1,0:T(8,128)(2,1)}), bf16[16,18,8,128]{3,2,1,0:T(8,128)(2,1)}, u32[]{:S(2)}, u32[]{:S(2)}) async-start(bf16[16,18,8,128]{3,2,1,0:T(8,128)(2,1)} %constant_dynamic-update-slice_fusion.16), calls=%async_computation.5 | async-start | bytes 1179648 | tf_op jit(solution)/shard_map/all_to_all | solution.py:45
  353.7 4.3 %copy-start.40 = (f32[18,1,128]{2,0,1:T(8,128)S(1)}, f32[18,1,128]{2,0,1:T(8,128)}, u32[]{:S(2)}) copy-start(f32[18,1,128]{2,0,1:T(8,128)} %copy-done.39) | copy-start | bytes 27652
  364.3 2.9 copy-start.13
  373.2 2.2 copy-start.4
  377.3 1.4 copy-start.19

commit v2 on v1

v2 whole, which is shorter than its diff:
```python
import functools

import jax
import jax.numpy as jnp
from jax import lax
from jax.experimental import pallas as pl
from jax.experimental.pallas import tpu as pltpu
from jax.sharding import PartitionSpec as P

HEADS = 18
HD = 128
TOP = 8
TOK = 128
WIDTH = HEADS * HD
FF = 512
SLOTS = 12
EXPERTS = 128
CAP = EXPERTS * SLOTS
THIRD = WIDTH // 3
SIDE = 4
CTX = 16
GROUP = HEADS * 8
PACK = GROUP + 32
NORM_EPS = 1e-06
LION_RATE = 0.001
BETA_ONE = 0.9
BETA_TWO = 0.99
WEIGHT_DECAY = 0.1
SCALING = HD ** (-0.5)
BF = jnp.bfloat16
F32 = jnp.float32
I32 = jnp.int32
MESH = pl.DeviceIdType.MESH
STRIDE = (32, 8, 2)
AXES = ((0, 1, 2), (1, 2, 0), (2, 0, 1))


def dot(a, b, dims=((1,), (0,))):
    return lax.dot_general(a, b, (dims, ((), ())), preferred_element_type=F32)


NN = ((1,), (0,))
NT = ((1,), (1,))
TN = ((0,), (0,))


def split(x):
    hi = x.astype(BF)
    return hi, (x - hi.astype(F32)).astype(BF)


def iota(shape, dim):
    return lax.broadcasted_iota(I32, shape, dim)


def lower_ones():
    return (iota((TOK, TOK), 0) >= iota((TOK, TOK), 1)).astype(F32).astype(BF)


def segments(starts_ref):
    begin = jnp.broadcast_to(starts_ref[...].astype(F32), (8, TOK)).astype(BF)
    tri = lower_ones()
    row = dot(begin, tri, NT)[0:1]
    col = dot(tri, begin, NT)[:, 0:1]
    return row, col


def head(h):
    return pl.ds(pl.multiple_of(h * HD, HD), HD)


def floor_div(r, by):
    return jnp.floor((r + 0.5) * (1.0 / by))


def row_parts(rows):
    r = iota((rows, 1), 0).astype(F32)
    b = floor_div(r, 48)
    r = r - 48 * b
    a = floor_div(r, SLOTS)
    return b, a, r - SLOTS * a


def mixer(
    og_h, q_h, k_h, v_h, g_h, res_h, router_h, hid_h, w_h, ids_ref, slot_ref, info_ref, starts_ref,
    gres_o, state_o, sgrad_o, grad_o,
    og, q, k, v, g, res, router, hid, w,
    ph1, inf, tab, s2, r2, arr, hp,
    f32buf, fsend, frecv, ssend, srecv, state, asend, arecv, bsend, brecv,
    prow, allowed, carried, mixed, qcar, cot, small, wsend, wmid, wrecv, csend, cmid, crecv, scol, gbuf, cum_s,
    in_sem, out_sem, s1_s, s1_r, i1_s, i1_r, s2_s, s2_r, s3_s, s3_r, f_s, f_r, b_s, b_r,
    w1_s, w1_r, w2_s, w2_r, c1_s, c1_r, c2_s, c2_r, a_s, a_r, e_s, e_r,
):
    ctx, ex = lax.axis_index("ctx"), lax.axis_index("exp")
    here = (lax.div(ctx, SIDE), lax.rem(ctx, SIDE), lax.div(ex, 2), lax.rem(ex, 2))

    def at(coords):
        return (coords[0] * SIDE + coords[1], coords[2] * 2 + coords[3])

    def moved(axis, by, flip=False):
        c = list(here)
        c[axis] = lax.rem(c[axis] + by, SIDE)
        if flip:
            c[3] = 1 - c[3]
        return tuple(c)

    def remote(src, dst, ss, rs, device):
        return pltpu.make_async_remote_copy(
            src_ref=src, dst_ref=dst, send_sem=ss, recv_sem=rs, device_id=device, device_id_type=MESH
        )

    loads = []
    for n, (a, b) in enumerate(
        ((og_h, og), (k_h, k), (v_h, v), (g_h, g), (q_h, q), (res_h, res), (router_h, router), (hid_h, hid), (w_h, w))
    ):
        loads.append(pltpu.make_async_copy(a, b, in_sem.at[n]))
        loads[-1].start()

    barrier = pltpu.get_barrier_semaphore()

    def tell(device):
        pl.semaphore_signal(barrier, inc=1, device_id=device, device_id_type=MESH)

    def tell_ctx(i, _):
        tell((lax.rem(ctx + i, CTX), ex))
        return 0

    def tell_exp(i, _):
        tell((ctx, lax.rem(ex + i, 8)))
        return 0

    lax.fori_loop(1, CTX, tell_ctx, 0)
    lax.fori_loop(1, 8, tell_exp, 0)
    for axis in (0, 1):
        for by in (1, 2, 3):
            tell(at(moved(axis, by, True)))
    pl.semaphore_wait(barrier, CTX - 1 + 7 + 6)

    loads[0].wait()
    sends = []
    locals_ = []
    for by in (1, 3, 2):
        for i in range(3):
            a0 = here[i]
            cp = remote(
                og.at[:, pl.ds(i * THIRD, THIRD)], ph1.at[i, pl.ds(pl.multiple_of(a0 * TOK, TOK), TOK)],
                s1_s.at[i, by], s1_r.at[i, a0], at(moved(i, by)))
            cp.start()
            sends.append(cp)
            cp = remote(info_ref, inf.at[i, a0], i1_s.at[i, by], i1_r.at[i, a0], at(moved(i, by)))
            cp.start()
            sends.append(cp)
    for i in range(3):
        a0 = here[i]
        cp = pltpu.make_async_copy(
            og.at[:, pl.ds(i * THIRD, THIRD)], ph1.at[i, pl.ds(pl.multiple_of(a0 * TOK, TOK), TOK)], s1_r.at[i, a0])
        cp.start()
        cp = pltpu.make_async_copy(info_ref, inf.at[i, a0], i1_r.at[i, a0])
        cp.start()

    for n in (1, 2, 3):
        loads[n].wait()
    seg_row, seg_col = segments(starts_ref)
    last_seg = seg_row[:, TOK - 1:TOK]
    tri = lower_ones()
    allowed[...] = jnp.where(
        (seg_row == seg_col) & (iota((TOK, TOK), 0) >= iota((TOK, TOK), 1)), 1.0, 0.0)
    carried[...] = jnp.broadcast_to(jnp.where(seg_col == 0.0, 1.0, 0.0), (TOK, TOK))
    tail = jnp.broadcast_to(jnp.where(seg_col == last_seg, 1.0, 0.0), (TOK, TOK))
    unbroken = jnp.where(last_seg == 0.0, 1.0, 0.0)
    prow[...] = jnp.zeros_like(prow)

    def own_state(h, _):
        cum = dot(tri, g[:, head(h)])
        cum_s[:, head(h)] = cum
        last = cum[TOK - 1:TOK]
        key_end = (k[:, head(h)].astype(F32) * jnp.exp(last - cum) * tail).astype(BF)
        fresh = dot(v[:, head(h)], key_end, TN)
        f32buf[:, pl.ds(pl.multiple_of(h * 8, 8), 8), :] = fresh.reshape(CTX, 8, HD)
        prow[pl.ds(h, 1), :] = jnp.exp(last) * unbroken
        return 0

    lax.fori_loop(0, HEADS, own_state, 0)
    passing = prow[...].astype(BF)

    def pack(j, _):
        fsend[j, 0:GROUP, :] = f32buf[j].astype(BF)
        fsend[j, GROUP:PACK, :] = passing
        return 0

    lax.fori_loop(0, CTX, pack, 0)

    def ctx_exchange(src, dst, ss, rs):
        def one(i, _):
            t = lax.rem(ctx + i, CTX)
            remote(src.at[t], dst.at[ctx], ss.at[i], rs.at[ctx], (t, ex)).start()
            return 0

        lax.fori_loop(1, CTX, one, 0)
        pltpu.make_async_copy(src.at[ctx], dst.at[ctx], rs.at[ctx]).start()

    def ctx_arrive(src, dst, ss, rs):
        def one(i, _):
            pltpu.make_async_copy(src.at[0], dst.at[i], rs.at[i]).wait()
            return 0

        lax.fori_loop(0, CTX, one, 0)

    def ctx_sent(src, dst, ss, rs):
        def one(i, _):
            pltpu.make_async_copy(src.at[0], dst.at[0], ss.at[i]).wait()
            return 0

        lax.fori_loop(1, CTX, one, 0)

    ctx_exchange(fsend, frecv, f_s, f_r)

    pat_a = floor_div(iota((48, 4 * TOK), 0).astype(F32), SLOTS)
    pat_s = iota((48, 4 * TOK), 0).astype(F32) - SLOTS * pat_a
    pattern = jnp.where(pat_a == floor_div(iota((48, 4 * TOK), 1).astype(F32), TOK), pat_s, -5.0)
    for i, (A, B, C) in enumerate(AXES):
        a0, b0, c0 = here[A], here[B], here[C]
        r = iota((32, TOK), 0).astype(F32)
        bb = floor_div(r, 8)
        cc = floor_div(r - 8 * bb, 2)
        e = bb * STRIDE[B] + cc * STRIDE[C] + (r - 8 * bb - 2 * cc) + (a0 * STRIDE[A]).astype(F32)
        for a in range(SIDE):
            pltpu.make_async_copy(info_ref, inf.at[i, a], i1_r.at[i, a]).wait()
            found = jnp.full((32, TOK), -1.0, F32)
            for j in range(TOP):
                found = jnp.where(inf[i, a, j:j + 1, :] == e, inf[i, a, TOP + j:TOP + j + 1, :], found)
            tab[:, a * TOK:(a + 1) * TOK] = found
            pltpu.make_async_copy(
                og.at[:, pl.ds(0, THIRD)], ph1.at[i, pl.ds(a * TOK, TOK)], s1_r.at[i, a]).wait()

        def select(n, _, i=i, B=B, b0=b0):
            b = lax.rem(b0 + n, SIDE)
            blocks = []
            for m in range(8):
                line = tab[pl.ds(b * 8 + m, 1), :]
                blocks.append(jnp.where(line == pattern, 1.0, 0.0).astype(BF))
            hit = jnp.concatenate(blocks, axis=0)
            s2[i, b] = dot(hit, ph1[i]).astype(BF).reshape(8, 48, THIRD)

            c = list(here)
            c[B] = b
            remote(s2.at[i, b], r2.at[i, b0], s2_s.at[i, n], s2_r.at[i, b0], at(c)).start()
            return 0

        lax.fori_loop(1, SIDE, select, 0)
        blocks = []
        for m in range(8):
            line = tab[pl.ds(b0 * 8 + m, 1), :]
            blocks.append(jnp.where(line == pattern, 1.0, 0.0).astype(BF))
        r2[i, b0] = dot(jnp.concatenate(blocks, axis=0), ph1[i]).astype(BF).reshape(8, 48, THIRD)

    ctx_arrive(fsend, frecv, f_s, f_r)

    def factor(j):
        p = frecv[j, GROUP:PACK, :].astype(F32)
        return jnp.concatenate([jnp.broadcast_to(p[h:h + 1], (8, HD)) for h in range(HEADS)], axis=0)

    def forward(j, acc):
        ssend[j] = acc.astype(BF)
        return factor(j) * acc + frecv[j, 0:GROUP, :].astype(F32)

    lax.fori_loop(0, CTX, forward, jnp.zeros((GROUP, HD), F32))
    ctx_exchange(ssend, srecv, b_s, b_r)

    loads[7].wait()
    pb, pa, ps = row_parts(192)
    for i, (A, B, C) in enumerate(AXES):
        base = (pa * STRIDE[A] + pb * STRIDE[B]) * SLOTS + ps

        def permute(n, _, i=i, C=C, base=base):
            core, c = lax.div(n, SIDE), lax.rem(n, SIDE)
            where = base.astype(I32) + (c * STRIDE[C] + core) * SLOTS
            pick = jnp.where(iota((192, CAP), 1) == where, 1.0, 0.0).astype(BF)
            hp[i, pl.ds(pl.multiple_of(n * 192, 192), 192)] = dot(pick, hid[...]).astype(BF)
            return 0

        lax.fori_loop(0, 8, permute, 0)

    for n in (4, 5, 6):
        loads[n].wait()
    ctx_arrive(ssend, srecv, b_s, b_r)

    def widen(j, _):
        f32buf[j] = srecv[j].astype(F32)
        return 0

    lax.fori_loop(0, CTX, widen, 0)

    def attend(h, _):
        cum = cum_s[:, head(h)]
        q_dec = q[:, head(h)].astype(F32) * jnp.exp(cum)
        k_dec = (k[:, head(h)].astype(F32) * jnp.exp(-cum)).astype(BF)
        scores = (dot(q_dec.astype(BF), k_dec, NT) * allowed[...]).astype(BF)
        q_c = (q_dec * carried[...]).astype(BF)
        qcar[:, head(h)] = q_c
        st = f32buf[:, pl.ds(pl.multiple_of(h * 8, 8), 8), :].reshape(HD, HD).astype(BF)
        state[h] = st
        out = SCALING * (dot(scores, v[:, head(h)]) + dot(q_c, st, NT))
        mixed[:, head(h)] = res[:, head(h)].astype(F32) + out.astype(BF).astype(F32)
        return 0

    lax.fori_loop(0, HEADS, attend, 0)
    state_out = pltpu.make_async_copy(state, state_o, out_sem.at[0])
    state_out.start()

    def square(h, acc):
        m = mixed[:, head(h)]
        return acc + m * m

    sq = lax.fori_loop(0, HEADS, square, jnp.zeros((TOK, HD), F32))
    inverse = lax.rsqrt(jnp.sum(sq, axis=1, keepdims=True) * (1.0 / WIDTH) + NORM_EPS)

    def project(h, acc):
        normed = (mixed[:, head(h)] * inverse).astype(BF)
        return acc + dot(normed, router[head(h), :])

    logits = lax.fori_loop(0, HEADS, project, jnp.zeros((TOK, EXPERTS), F32))
    lanes = iota((TOK, EXPERTS), 1)
    rank = jnp.full((TOK, EXPERTS), -1.0, F32)
    chosen = jnp.zeros((TOK, EXPERTS), F32)
    for j in range(TOP):
        eq = ids_ref[:, j:j + 1] == lanes
        chosen = jnp.where(eq, 1.0, chosen)
        rank = jnp.where(eq, slot_ref[:, j:j + 1].astype(F32), rank)
    gate = chosen * jax.nn.sigmoid(logits)
    total = jnp.sum(gate, axis=1, keepdims=True)
    weights = gate / total
    w_round = weights.astype(BF).astype(F32)
    rows_ = []
    for s in range(SLOTS):
        rows_.append(jnp.sum(jnp.where(rank == float(s), w_round, 0.0), axis=0, keepdims=True))
    w_t = jnp.concatenate(rows_ + [jnp.zeros((4, EXPERTS), F32)], axis=0).astype(BF)
    turn_r, turn_l = iota((EXPERTS, EXPERTS), 0).astype(F32), iota((EXPERTS, EXPERTS), 1).astype(F32)
    turn_e = floor_div(turn_r, CTX)
    turn = jnp.where((turn_r - CTX * turn_e) * 8 + turn_e == turn_l, 1.0, 0.0).astype(BF)
    w_rows = dot(turn, w_t, NT)
    small[...] = jnp.zeros_like(small)
    small[:, 0:16] = w_rows
    wsend[...] = small[...].reshape(8, CTX, EXPERTS)

    def exp_out(src, dst, ss, rs):
        def one(i, _):
            t = lax.rem(ex + i, 8)
            remote(src.at[t], dst.at[:, ex], ss.at[i], rs.at[ex], (ctx, t)).start()
            return 0

        lax.fori_loop(1, 8, one, 0)
        pltpu.make_async_copy(src.at[ex], dst.at[:, ex], rs.at[ex]).start()

    def exp_in(src, dst, ss, rs):
        def one(i, _):
            pltpu.make_async_copy(src.at[0], dst.at[:, i], rs.at[i]).wait()
            return 0

        lax.fori_loop(0, 8, one, 0)

    def exp_sent(src, dst, ss, rs):
        def one(i, _):
            pltpu.make_async_copy(src.at[0], dst.at[:, 0], ss.at[i]).wait()
            return 0

        lax.fori_loop(1, 8, one, 0)

    exp_out(wsend, wmid, w1_s, w1_r)

    for i, (A, B, C) in enumerate(AXES):
        b0, c0 = here[B], here[C]
        slot0 = here[3] * SIDE + c0

        def come(n, _, i=i, b0=b0):
            b = lax.rem(b0 + n, SIDE)
            pltpu.make_async_copy(s2.at[i, 0], r2.at[i, b], s2_r.at[i, b]).wait()
            return 0

        lax.fori_loop(1, SIDE, come, 0)
        for by in (1, 3, 2, 0):
            for flip in (0, 1):
                c = list(here)
                c[C] = lax.rem(c0 + by, SIDE)
                if flip:
                    c[3] = 1 - c[3]
                line = c[C] * 2 + c[3]
                if by == 0 and flip == 0:
                    pltpu.make_async_copy(r2.at[i, :, line], arr.at[i, slot0], s3_r.at[i, slot0]).start()
                else:
                    cp = remote(
                        r2.at[i, :, line], arr.at[i, slot0], s3_s.at[i, by * 2 + flip], s3_r.at[i, slot0], at(c))
                    cp.start()
                    sends.append(cp)

    exp_in(wsend, wmid, w1_s, w1_r)
    ctx_exchange(wmid, wrecv, w2_s, w2_r)

    loads[8].wait()
    small[...] = jnp.zeros_like(small)

    for n in range(8):
        for i, (A, B, C) in enumerate(AXES):
            c0 = here[C]
            step = n // 2
            core = here[3] if n % 2 == 0 else 1 - here[3]
            c = lax.rem(c0 + (0, 1, 3, 2)[step], SIDE)
            piece = core * SIDE + c
            pltpu.make_async_copy(r2.at[i, :, 0], arr.at[i, piece], s3_r.at[i, piece]).wait()
            act = hp[i, pl.ds(pl.multiple_of(piece * 192, 192), 192)]
            part = dot(act, w[:, i * THIRD:(i + 1) * THIRD]).astype(BF).astype(F32)
            part = part * arr[i, piece].reshape(192, THIRD).astype(F32)
            score = jnp.sum(part, axis=1, keepdims=True)
            at_slot = jnp.where(iota((192, EXPERTS), 1) == ps.astype(I32), score, 0.0)
            coord = [None, None, None]
            coord[A], coord[B], coord[C] = pa, pb, c.astype(F32)
            to = (coord[2] * 2 + core.astype(F32)) * CTX + coord[0] * SIDE + coord[1]
            spread = jnp.where(iota((192, EXPERTS), 1) == to.astype(I32), 1.0, 0.0).astype(BF)
            hi, lo = split(at_slot)
            small[...] += dot(spread, hi, TN) + dot(spread, lo, TN)
    csend[...] = small[...].reshape(8, CTX, EXPERTS)
    exp_out(csend, cmid, c1_s, c1_r)
    exp_in(csend, cmid, c1_s, c1_r)
    ctx_exchange(cmid, crecv, c2_s, c2_r)
    ctx_arrive(cmid, crecv, c2_s, c2_r)

    back = jnp.transpose(crecv[...].reshape(EXPERTS, EXPERTS))
    prob = jnp.zeros((TOK, EXPERTS), F32)
    for s in range(SLOTS):
        prob = jnp.where(rank == float(s), back[s:s + 1], prob)
    mix = jnp.sum(weights * prob, axis=1, keepdims=True)
    logit_grad = (chosen * ((prob - mix) / total * gate * (1.0 - gate))).astype(BF)

    def product(h, acc):
        return acc + dot(logit_grad, router[head(h), :], NT) * mixed[:, head(h)]

    mean = jnp.sum(lax.fori_loop(0, HEADS, product, jnp.zeros((TOK, HD), F32)), axis=1, keepdims=True) * (1.0 / WIDTH)
    pull = inverse * inverse * inverse * mean

    def residual(h, _):
        grad = (
            og[:, head(h)].astype(F32)
            + inverse * dot(logit_grad, router[head(h), :], NT)
            - mixed[:, head(h)] * pull
        ).astype(BF)
        cot[:, head(h)] = grad
        adj = SCALING * dot(grad, qcar[:, head(h)], TN)
        f32buf[:, pl.ds(pl.multiple_of(h * 8, 8), 8), :] = adj.reshape(CTX, 8, HD)
        return 0

    lax.fori_loop(0, HEADS, residual, 0)

    def pack_back(j, _):
        asend[j] = f32buf[j].astype(BF)
        return 0

    lax.fori_loop(0, CTX, pack_back, 0)
    ctx_exchange(asend, arecv, a_s, a_r)
    gres_out = pltpu.make_async_copy(cot, gres_o, out_sem.at[1])
    gres_out.start()

    ctx_arrive(wmid, wrecv, w2_s, w2_r)
    w_in = wrecv[...].reshape(EXPERTS, EXPERTS).astype(BF)

    def expert_grad(i):
        A, B, C = AXES[i]

        def column(n, _):
            core, c = lax.div(n, SIDE), lax.rem(n, SIDE)
            src = pa * STRIDE[A] + pb * STRIDE[B]
            src = src.astype(I32) + c * STRIDE[C] + core
            pick = jnp.where(iota((192, EXPERTS), 1) == src, 1.0, 0.0).astype(BF)
            mine = dot(pick, w_in)
            col = jnp.sum(jnp.where(iota((192, EXPERTS), 1) == ps.astype(I32), mine, 0.0), axis=1, keepdims=True)
            scaled = (arr[i, n].reshape(192, THIRD).astype(F32) * col).astype(BF)
            part = dot(hp[i, pl.ds(pl.multiple_of(n * 192, 192), 192)], scaled, TN)

            @pl.when(n == 0)
            def _():
                gbuf[i] = part

            @pl.when(n > 0)
            def _():
                gbuf[i] += part

            return 0

        lax.fori_loop(0, 8, column, 0)
        cp = pltpu.make_async_copy(gbuf.at[i], grad_o.at[:, pl.ds(i * THIRD, THIRD)], out_sem.at[3 + i])
        cp.start()
        return cp

    grads = [expert_grad(0)]
    ctx_arrive(asend, arecv, a_s, a_r)

    def backward(n, acc):
        j = CTX - 1 - n
        bsend[j] = acc.astype(BF)
        return factor(j) * acc + arecv[j].astype(F32)

    lax.fori_loop(0, CTX, backward, jnp.zeros((GROUP, HD), F32))
    ctx_exchange(bsend, brecv, e_s, e_r)
    grads.append(expert_grad(1))
    grads.append(expert_grad(2))
    ctx_arrive(bsend, brecv, e_s, e_r)

    def widen_back(j, _):
        f32buf[j] = brecv[j].astype(F32)
        return 0

    lax.fori_loop(0, CTX, widen_back, 0)
    state_out.wait()

    def gather(h, _):
        state[h] = f32buf[:, pl.ds(pl.multiple_of(h * 8, 8), 8), :].reshape(HD, HD).astype(BF)
        return 0

    lax.fori_loop(0, HEADS, gather, 0)
    sgrad_out = pltpu.make_async_copy(state, sgrad_o, out_sem.at[2])
    sgrad_out.start()

    for cp in sends:
        cp.wait_send()
    for i in range(3):
        for n in (1, 2, 3):
            pltpu.make_async_copy(s2.at[i, 0], r2.at[i, 0], s2_s.at[i, n]).wait()
    ctx_sent(fsend, frecv, f_s, f_r)
    ctx_sent(ssend, srecv, b_s, b_r)
    ctx_sent(asend, arecv, a_s, a_r)
    ctx_sent(bsend, brecv, e_s, e_r)
    exp_sent(wsend, wmid, w1_s, w1_r)
    exp_sent(csend, cmid, c1_s, c1_r)
    ctx_sent(wmid, wrecv, w2_s, w2_r)
    ctx_sent(cmid, crecv, c2_s, c2_r)
    gres_out.wait()
    sgrad_out.wait()
    for cp in grads:
        cp.wait()


def finish(
    q_ref, k_ref, v_ref, g_ref, cot_ref, state_ref, sgrad_ref, starts_ref, w_ref, m_ref, grad_ref,
    dq_o, dk_o, dv_o, dg_o, gres_o, nw_o, nm_o,
):
    seg_row, seg_col = segments(starts_ref)
    last_seg = seg_row[:, TOK - 1:TOK]
    lower = iota((TOK, TOK), 0) >= iota((TOK, TOK), 1)
    tri = lower.astype(F32).astype(BF)
    allowed = jnp.where((seg_row == seg_col) & lower, 1.0, 0.0)
    carried = jnp.where(seg_col == 0.0, 1.0, 0.0)
    tail = jnp.where(seg_col == last_seg, 1.0, 0.0)
    unbroken = jnp.where(last_seg == 0.0, 1.0, 0.0)
    for n in range(state_ref.shape[0]):
        cols = slice(n * HD, (n + 1) * HD)
        v, cot = v_ref[:, cols], cot_ref[:, cols]
        st, sg = state_ref[n], sgrad_ref[n]
        cum = dot(tri, g_ref[:, cols])
        last = cum[TOK - 1:TOK]
        grow, shrink, to_end = jnp.exp(cum), jnp.exp(-cum), jnp.exp(last - cum) * tail
        k = k_ref[:, cols].astype(F32)
        q_dec = (q_ref[:, cols].astype(F32) * grow).astype(BF)
        k_dec = (k * shrink).astype(BF)
        key_end = (k * to_end).astype(BF)
        scores = (SCALING * allowed * dot(q_dec, k_dec, NT)).astype(BF)
        d_scores = (SCALING * allowed * dot(cot, v, NT)).astype(BF)
        dq_dec = dot(d_scores, k_dec) + (SCALING * carried) * dot(cot, st)
        dk_dec = dot(d_scores, q_dec, TN)
        dk_end = dot(v, sg)
        dv_o[:, cols] = (dot(scores, cot, TN) + dot(key_end, sg, NT)).astype(BF)
        dq_o[:, cols] = (dq_dec * grow).astype(BF)
        dk_o[:, cols] = (dk_dec * shrink + dk_end * to_end).astype(BF)
        end_term = dk_end * key_end.astype(F32)
        d_cum = dq_dec * q_dec.astype(F32) - dk_dec * k_dec.astype(F32) - end_term
        d_last = jnp.sum(end_term, axis=0, keepdims=True) + unbroken * jnp.exp(last) * jnp.sum(
            st.astype(F32) * sg.astype(F32), axis=0, keepdims=True)
        hi, lo = split(d_cum)
        dg_o[:, cols] = (dot(tri, hi, TN) + dot(tri, lo, TN) + d_last).astype(BF)
        gres_o[:, cols] = cot
    wf, mf, grad = w_ref[...].astype(F32), m_ref[...].astype(F32), grad_ref[...]
    turn = BETA_ONE * mf + (1.0 - BETA_ONE) * grad
    direction = jnp.where(turn > 0.0, 1.0, jnp.where(turn < 0.0, -1.0, 0.0))
    nw_o[...] = (wf - LION_RATE * (direction + WEIGHT_DECAY * wf)).astype(BF)
    nm_o[...] = (BETA_TWO * mf + (1.0 - BETA_TWO) * grad).astype(BF)


def local(
    queries, key_vectors, values, log_decay, starts, residual_in, out_grad,
    expert_ids, slot_index, router, hidden_saved, w_down, momentum,
):
    any_, vm = pl.BlockSpec(memory_space=pl.ANY), pl.BlockSpec(memory_space=pltpu.VMEM)
    dma = pltpu.SemaphoreType.DMA
    V = pltpu.VMEM
    info = jnp.concatenate([expert_ids[0].T, slot_index[0].T], axis=0).astype(F32)
    scratch = [
        *[V((TOK, WIDTH), BF)] * 6, V((WIDTH, EXPERTS), BF), V((CAP, FF), BF), V((FF, WIDTH), BF),
        V((3, SIDE * TOK, THIRD), BF), V((3, SIDE, 16, TOK), F32), V((32, SIDE * TOK), F32),
        V((3, SIDE, 8, 48, THIRD), BF), V((3, SIDE, 8, 48, THIRD), BF), V((3, 8, SIDE, 48, THIRD), BF),
        V((3, CAP, FF), BF),
        V((CTX, GROUP, HD), F32), V((CTX, PACK, HD), BF), V((CTX, PACK, HD), BF),
        V((CTX, GROUP, HD), BF), V((CTX, GROUP, HD), BF), V((HEADS, HD, HD), BF),
        *[V((CTX, GROUP, HD), BF)] * 4,
        V((32, HD), F32), V((TOK, TOK), F32), V((TOK, TOK), F32), V((TOK, WIDTH), F32),
        V((TOK, WIDTH), BF), V((TOK, WIDTH), BF), V((EXPERTS, EXPERTS), F32),
        V((8, CTX, EXPERTS), F32), V((CTX, 8, EXPERTS), F32), V((CTX, 8, EXPERTS), F32),
        V((8, CTX, EXPERTS), F32), V((CTX, 8, EXPERTS), F32), V((CTX, 8, EXPERTS), F32),
        V((8, 128), F32), V((3, FF, THIRD), F32), V((TOK, WIDTH), F32),
        dma((9,)), dma((6,)),
        dma((3, 4)), dma((3, 4)), dma((3, 4)), dma((3, 4)), dma((3, 4)), dma((3, 4)), dma((3, 8)), dma((3, 8)),
        dma((CTX,)), dma((CTX,)), dma((CTX,)), dma((CTX,)),
        dma((8,)), dma((8,)), dma((CTX,)), dma((CTX,)), dma((8,)), dma((8,)), dma((CTX,)), dma((CTX,)),
        dma((CTX,)), dma((CTX,)), dma((CTX,)), dma((CTX,)),
    ]
    gres, state, sgrad, grad = pl.pallas_call(
        mixer,
        name="dispatch_and_scan",
        out_shape=(
            jax.ShapeDtypeStruct((TOK, WIDTH), BF),
            jax.ShapeDtypeStruct((HEADS, HD, HD), BF),
            jax.ShapeDtypeStruct((HEADS, HD, HD), BF),
            jax.ShapeDtypeStruct((FF, WIDTH), F32),
        ),
        in_specs=[any_] * 9 + [vm] * 4,
        out_specs=(any_,) * 4,
        scratch_shapes=scratch,
        compiler_params=pltpu.CompilerParams(
            collective_id=0, has_side_effects=True, vmem_limit_bytes=62 * 2**20),
    )(
        out_grad[0], queries[0], key_vectors[0], values[0], log_decay[0], residual_in[0], router,
        hidden_saved[0], w_down[0], expert_ids[0], slot_index[0], info, starts,
    )
    per = 2
    tok = pl.BlockSpec((TOK, per * HD), lambda i: (0, i))
    st = pl.BlockSpec((per, HD, HD), lambda i: (i, 0, 0))
    ex = pl.BlockSpec((FF, per * HD), lambda i: (0, i))
    outs = pl.pallas_call(
        finish,
        name="backward_and_step",
        grid=(HEADS // per,),
        out_shape=(jax.ShapeDtypeStruct((TOK, WIDTH), BF),) * 5 + (jax.ShapeDtypeStruct((FF, WIDTH), BF),) * 2,
        in_specs=[tok] * 5 + [st] * 2 + [pl.BlockSpec((1, TOK), lambda i: (0, 0))] + [ex] * 3,
        out_specs=(tok,) * 5 + (ex,) * 2,
        compiler_params=pltpu.CompilerParams(vmem_limit_bytes=40 * 2**20),
    )(
        queries[0], key_vectors[0], values[0], log_decay[0], gres, state, sgrad, starts,
        w_down[0], momentum[0], grad,
    )
    return tuple(x[None] for x in outs)


def solution(mesh):
    tokens = P("exp", "ctx", None)
    owned = P(("ctx", "exp"), None, None)
    in_specs = (tokens,) * 4 + (P("exp", "ctx"),) + (tokens,) * 4 + (P(),) + (owned,) * 3
    out_specs = (tokens,) * 5 + (owned,) * 2
    return jax.shard_map(local, mesh=mesh, in_specs=in_specs, out_specs=out_specs, check_vma=False)
```

time: 383 us -> 177 us (0.46)
  Pallas kernels: 0 us -> 162 us
  waiting for transfers between devices: 107 us -> 0 us
  local copies, waits for them, and re-layouts: 89.8 us -> 12.8 us
  starting transfers between devices: 57.7 us -> 0 us
  matrix products: 50.3 us -> 0 us
  other arithmetic: 51 us -> 1.31 us
  blocking collectives: 22 us -> 0 us
    pallas_call x0 -> x2, Pallas kernels: none -> 162 us  [the longest x1 146 us: local(): pl.pallas_call(mixer, name='dispatch_and_scan', out_shape=(jax.ShapeDtype...]
    all_to_all x7 -> x0, waiting for transfers between devices: 107 us -> none  [exchange(): return lax.all_to_all(x, axis, split_axis=0, concat_axis=0, tiled=True)]
    all_to_all x7 -> x0, starting transfers between devices: 57.7 us -> none  [exchange(): return lax.all_to_all(x, axis, split_axis=0, concat_axis=0, tiled=True)]
    dot_general x19 -> x0, matrix products: 47.2 us -> none  [the longest x12 18.1 us: mm(): jnp.einsum(spec, a.astype(BF), b.astype(BF), preferred_element_type=F32)]
    convert_element_type x13 -> x0, local copies, waits for them, and re-layouts: 38.6 us -> none  [the longest x1 13 us: local(): slot_score = jnp.sum(gathered.astype(F32) * produced.astype(F32), axis=-1)]
    unnamed x29 -> x0, other arithmetic: 26.6 us -> none
    all_gather x1 -> x0, blocking collectives: 22 us -> none  [local(): passing_all = lax.all_gather(passing.astype(BF), 'ctx').astype(F32)]
    unnamed x110 -> x22, local copies, waits for them, and re-layouts: 29.7 us -> 9.93 us
  transfers between devices with their start and end apart: 7 -> 0, of which waited for: 2 -> 0; matrix products, arithmetic and copies ran while one was open for 23% -> 0% of each run, Pallas kernels for 0% -> 0%
where the time goes in v2:
time: 177 us; the launch traced here: 176 us
  Pallas kernels  162 us (92%)
  local copies, waits for them, and re-layouts  12.8 us (7%)
    pallas_call x1, Pallas kernels, local(): pl.pallas_call(mixer, name='dispatch_and_scan', out_shape=(jax.ShapeDtype...  146 us
    pallas_call x1, Pallas kernels, local(): pl.pallas_call(finish, name='backward_and_step', grid=(HEADS // per,), ou...  15.3 us
    unnamed x22, local copies, waits for them, and re-layouts  9.93 us

profile of v2, /device:TPU:1, one launch (start us, length us, event | category | flops | bytes accessed | tf_op | source)
XLA Modules:
  0.0 176.3 jit_solution(10018388520289622823)
XLA Ops:
  0.6 1.3 add_convert_fusion.info_ref
  1.9 1.4 copy.21.slot_ref
  3.4 1.4 copy.20.ids_ref
  4.8 0.0 copy-start.3
  4.8 0.0 copy-start.4
  4.8 0.0 copy-start.5
  4.8 0.0 copy-start.10
  4.8 146.2 %dispatch_and_scan.1 = (bf16[128,2304]{1,0:T(8,128)(2,1)}, bf16[18,128,128]{2,1,0:T(8,128)(2,1)}, bf16[18,128,128]{2,1,0:T(8,128)(2,1)}, f32[512,2304]{1,0:T(8,128)}) custom-call(bf16[128,2304]{1,0:T(8,128)(2,1)} %bitcast.34, bf16[128,2304]{1,0:T(8,128)(2,1)} %bitcast.25, bf16[128,2304]{1,0:T(8,128)(2,1)} %bitcast.27, bf16[128,2304]{1,0:T(8,128)(2,1)} %bitcast.29, ...), custom_call_target="tpu_custom_call" | custom-call | tf_op jit(solution)/shard_map/dispatch_and_scan/pallas_call | solution.py:613
  151.0 0.0 copy-done.3
  151.0 0.0 copy-done.4
  151.0 0.0 copy-done.5
  151.0 0.0 copy-done.10
  151.1 0.0 copy-start
  151.1 1.7 copy-done
  152.7 0.0 copy-start.1
  152.7 2.3 %copy-done.1 = f32[512,2304]{1,0:T(8,128)S(1)} copy-done((f32[512,2304]{1,0:T(8,128)S(1)}, f32[512,2304]{1,0:T(8,128)}, u32[]{:S(2)}) %copy-start.1) | copy-done | bytes 4718616
  155.1 0.0 copy-start.2
  155.1 1.7 copy-done.2
  156.7 0.0 copy-start.6
  156.7 1.1 copy-done.6
  157.8 0.0 copy-start.7
  157.8 1.1 copy-done.7
  158.9 0.0 copy-start.8
  158.9 1.1 copy-done.8
  159.9 0.0 copy-start.9
  159.9 1.1 copy-done.9
  161.0 15.3 %backward_and_step.1 = (bf16[128,2304]{1,0:T(8,128)(2,1)}, bf16[128,2304]{1,0:T(8,128)(2,1)}, bf16[128,2304]{1,0:T(8,128)(2,1)}, bf16[128,2304]{1,0:T(8,128)(2,1...) custom-call(bf16[128,2304]{1,0:T(8,128)(2,1)S(1)} %bitcast.26, ...), custom_call_target="tpu_custom_call" | custom-call | tf_op jit(solution)/shard_map/backward_and_step/pallas_call | solution.py:635
Async XLA Ops:
  4.8 146.2 %copy-start.3 = (bf16[1,128,2304]{2,1,0:T(8,128)(2,1)S(1)}, bf16[1,128,2304]{2,1,0:T(8,128)(2,1)}, u32[]{:S(2)}) copy-start(bf16[1,128,2304]{2,1,0:T(8,128)(2,1)} %param.13) | copy-start | bytes 1769476
  4.8 146.3 %copy-start.4 = (bf16[1,128,2304]{2,1,0:T(8,128)(2,1)S(1)}, bf16[1,128,2304]{2,1,0:T(8,128)(2,1)}, u32[]{:S(2)}) copy-start(bf16[1,128,2304]{2,1,0:T(8,128)(2,1)} %param.14) | copy-start | bytes 1769476
  4.8 146.3 %copy-start.5 = (bf16[1,128,2304]{2,1,0:T(8,128)(2,1)S(1)}, bf16[1,128,2304]{2,1,0:T(8,128)(2,1)}, u32[]{:S(2)}) copy-start(bf16[1,128,2304]{2,1,0:T(8,128)(2,1)} %param.15) | copy-start | bytes 1769476
  4.8 146.3 %copy-start.10 = (s32[1,128]{1,0:T(1,128)S(1)}, s32[1,128]{1,0:T(1,128)}, u32[]{:S(2)}) copy-start(s32[1,128]{1,0:T(1,128)} %starts_ref.3) | copy-start | bytes 1540
  151.1 1.7 copy-start
  152.7 2.3 %copy-start.1 = (f32[512,2304]{1,0:T(8,128)S(1)}, f32[512,2304]{1,0:T(8,128)}, u32[]{:S(2)}) copy-start(f32[512,2304]{1,0:T(8,128)} %get-tuple-element.21.grad_ref) | copy-start | bytes 14155780
  155.1 1.7 copy-start.2
  156.7 1.1 copy-start.6
  157.8 1.1 copy-start.7
  158.9 1.1 copy-start.8
  159.9 1.1 copy-start.9

commit v3 on v2

v3 whole, which is shorter than its diff:
```python
import functools

import jax
import jax.numpy as jnp
from jax import lax
from jax.experimental import pallas as pl
from jax.experimental.pallas import tpu as pltpu
from jax.sharding import PartitionSpec as P

HEADS = 18
HD = 128
TOP = 8
TOK = 128
WIDTH = HEADS * HD
FF = 512
SLOTS = 12
EXPERTS = 128
CAP = EXPERTS * SLOTS
THIRD = WIDTH // 3
SIDE = 4
CTX = 16
GROUP = HEADS * 8
PACK = GROUP + 32
NORM_EPS = 1e-06
LION_RATE = 0.001
BETA_ONE = 0.9
BETA_TWO = 0.99
WEIGHT_DECAY = 0.1
SCALING = HD ** (-0.5)
BF = jnp.bfloat16
F32 = jnp.float32
I32 = jnp.int32
UNROLL = 3
PER = 3
MESH = pl.DeviceIdType.MESH
STRIDE = (32, 8, 2)
AXES = ((0, 1, 2), (1, 2, 0), (2, 0, 1))


def dot(a, b, dims=((1,), (0,))):
    return lax.dot_general(a, b, (dims, ((), ())), preferred_element_type=F32)


NN = ((1,), (0,))
NT = ((1,), (1,))
TN = ((0,), (0,))


def split(x):
    hi = x.astype(BF)
    return hi, (x - hi.astype(F32)).astype(BF)


def iota(shape, dim):
    return lax.broadcasted_iota(I32, shape, dim)


def lower_ones():
    return (iota((TOK, TOK), 0) >= iota((TOK, TOK), 1)).astype(F32).astype(BF)


def segments(starts_ref):
    begin = jnp.broadcast_to(starts_ref[...].astype(F32), (8, TOK)).astype(BF)
    tri = lower_ones()
    row = dot(begin, tri, NT)[0:1]
    col = dot(tri, begin, NT)[:, 0:1]
    return row, col


def head(h):
    return pl.ds(pl.multiple_of(h * HD, HD), HD)


def floor_div(r, by):
    return jnp.floor((r + 0.5) * (1.0 / by))


def digits(r, sizes):
    out = []
    for size in reversed(sizes):
        rest = floor_div(r, size)
        out.append(r - size * rest)
        r = rest
    return [r] + out[::-1]


def mixer(
    og_h, q_h, k_h, v_h, g_h, res_h, router_h, hid_h, w_h, ids_ref, slot_ref, starts_ref,
    gres_o, state_o, sgrad_o, grad_o,
    og, q, k, v, g, res, router, hid, w,
    ph1, info, inf, tab, s2, r2, arr, hp,
    f32buf, fsend, frecv, ssend, srecv, state, asend, arecv, bsend, brecv,
    prow, allowed, carried, mixed, qcar, cot, small, wsend, wmid, wrecv, csend, cmid, crecv, gbuf, cum_s,
    in_sem, out_sem, s1_s, s1_r, i1_s, i1_r, s2_s, s2_r, s3_s, s3_r, f_s, f_r, b_s, b_r,
    w1_s, w1_r, w2_s, w2_r, c1_s, c1_r, c2_s, c2_r, a_s, a_r, e_s, e_r,
):
    ctx, ex = lax.axis_index("ctx"), lax.axis_index("exp")
    here = (lax.div(ctx, SIDE), lax.rem(ctx, SIDE), lax.div(ex, 2), lax.rem(ex, 2))

    def at(coords):
        return (coords[0] * SIDE + coords[1], coords[2] * 2 + coords[3])

    def moved(axis, by, flip=False):
        c = list(here)
        c[axis] = lax.rem(c[axis] + by, SIDE)
        if flip:
            c[3] = 1 - c[3]
        return tuple(c)

    def remote(src, dst, ss, rs, device):
        return pltpu.make_async_remote_copy(
            src_ref=src, dst_ref=dst, send_sem=ss, recv_sem=rs, device_id=device, device_id_type=MESH
        )

    loads = []
    for n, (a, b) in enumerate(
        ((og_h, og), (k_h, k), (v_h, v), (g_h, g), (q_h, q), (res_h, res), (router_h, router), (hid_h, hid), (w_h, w))
    ):
        loads.append(pltpu.make_async_copy(a, b, in_sem.at[n]))
        loads[-1].start()

    info[0:TOP] = ids_ref[...].astype(F32)
    info[TOP:2 * TOP] = slot_ref[...].astype(F32)

    barrier = pltpu.get_barrier_semaphore()

    def tell(device):
        pl.semaphore_signal(barrier, inc=1, device_id=device, device_id_type=MESH)

    def tell_ctx(i, _):
        tell((lax.rem(ctx + i, CTX), ex))
        return 0

    def tell_exp(i, _):
        tell((ctx, lax.rem(ex + i, 8)))
        return 0

    lax.fori_loop(1, CTX, tell_ctx, 0)
    lax.fori_loop(1, 8, tell_exp, 0)
    for axis in (0, 1):
        for by in (1, 2, 3):
            tell(at(moved(axis, by, True)))
    pl.semaphore_wait(barrier, CTX - 1 + 7 + 6)

    loads[0].wait()
    sends = []

    def send(src, dst, ss, rs, device):
        cp = remote(src, dst, ss, rs, device)
        cp.start()
        sends.append(cp)

    def rows_of(n, size):
        return pl.ds(pl.multiple_of(n * size, size), size)

    for by in (1, 3, 2):
        for i in range(3):
            send(info, inf.at[i, here[i]], i1_s.at[i, by], i1_r.at[i, here[i]], at(moved(i, by)))
    for by in (1, 3, 2):
        for i in range(3):
            send(og.at[:, pl.ds(i * THIRD, THIRD)], ph1.at[i, rows_of(here[i], TOK)],
                 s1_s.at[i, by], s1_r.at[i, here[i]], at(moved(i, by)))
    for i in range(3):
        pltpu.make_async_copy(
            og.at[:, pl.ds(i * THIRD, THIRD)], ph1.at[i, rows_of(here[i], TOK)], s1_r.at[i, here[i]]).start()
        pltpu.make_async_copy(info, inf.at[i, here[i]], i1_r.at[i, here[i]]).start()

    for n in (1, 2, 3):
        loads[n].wait()
    seg_row, seg_col = segments(starts_ref)
    last_seg = seg_row[:, TOK - 1:TOK]
    tri = lower_ones()
    allowed[...] = jnp.where(
        (seg_row == seg_col) & (iota((TOK, TOK), 0) >= iota((TOK, TOK), 1)), 1.0, 0.0)
    carried[...] = jnp.broadcast_to(jnp.where(seg_col == 0.0, 1.0, 0.0), (TOK, TOK))
    tail = jnp.broadcast_to(jnp.where(seg_col == last_seg, 1.0, 0.0), (TOK, TOK))
    unbroken = jnp.where(last_seg == 0.0, 1.0, 0.0)
    prow[...] = jnp.zeros_like(prow)

    def own_state(h, _):
        cum = dot(tri, g[:, head(h)])
        cum_s[:, head(h)] = cum
        last = cum[TOK - 1:TOK]
        key_end = (k[:, head(h)].astype(F32) * jnp.exp(last - cum) * tail).astype(BF)
        fresh = dot(v[:, head(h)], key_end, TN)
        f32buf[:, rows_of(h, 8), :] = fresh.reshape(CTX, 8, HD)
        prow[pl.ds(h, 1), :] = jnp.exp(last) * unbroken
        return 0

    lax.fori_loop(0, HEADS, own_state, 0, unroll=UNROLL)
    passing = prow[...].astype(BF)

    def pack(j, _):
        fsend[j, 0:GROUP, :] = f32buf[j].astype(BF)
        fsend[j, GROUP:PACK, :] = passing
        return 0

    lax.fori_loop(0, CTX, pack, 0, unroll=4)

    def ctx_exchange(src, dst, ss, rs):
        def one(i, _):
            t = lax.rem(ctx + i, CTX)
            remote(src.at[t], dst.at[ctx], ss.at[i], rs.at[ctx], (t, ex)).start()
            return 0

        lax.fori_loop(1, CTX, one, 0)
        pltpu.make_async_copy(src.at[ctx], dst.at[ctx], rs.at[ctx]).start()

    def ctx_arrive(src, dst, ss, rs):
        def one(i, _):
            pltpu.make_async_copy(src.at[0], dst.at[i], rs.at[i]).wait()
            return 0

        lax.fori_loop(0, CTX, one, 0)

    def ctx_sent(src, dst, ss, rs):
        def one(i, _):
            pltpu.make_async_copy(src.at[0], dst.at[0], ss.at[i]).wait()
            return 0

        lax.fori_loop(1, CTX, one, 0)

    ctx_exchange(fsend, frecv, f_s, f_r)

    pat_a, pat_s = digits(iota((48, SIDE * TOK), 0).astype(F32), (SLOTS,))
    pattern = jnp.where(pat_a == floor_div(iota((48, SIDE * TOK), 1).astype(F32), TOK), pat_s, -5.0)
    bb, cc, kk = digits(iota((32, TOK), 0).astype(F32), (SIDE, 2))
    for i, (A, B, C) in enumerate(AXES):
        e = bb * STRIDE[B] + cc * STRIDE[C] + kk + (here[A] * STRIDE[A]).astype(F32)
        for a in range(SIDE):
            pltpu.make_async_copy(info, inf.at[i, a], i1_r.at[i, a]).wait()
            found = jnp.full((32, TOK), -1.0, F32)
            for j in range(TOP):
                found = jnp.where(inf[i, a, j:j + 1, :] == e, inf[i, a, TOP + j:TOP + j + 1, :], found)
            tab[i, :, a * TOK:(a + 1) * TOK] = found

    def select(i, b):
        blocks = []
        for m in range(8):
            line = tab[i, pl.ds(b * 8 + m, 1), :]
            blocks.append(jnp.where(line == pattern, 1.0, 0.0).astype(BF))
        return dot(jnp.concatenate(blocks, axis=0), ph1[i]).astype(BF)

    for by in (1, 3, 2):
        for i, (A, B, C) in enumerate(AXES):
            if by == 1:
                for a in range(SIDE):
                    pltpu.make_async_copy(
                        og.at[:, pl.ds(0, THIRD)], ph1.at[i, pl.ds(a * TOK, TOK)], s1_r.at[i, a]).wait()
            b = lax.rem(here[B] + by, SIDE)
            s2[i, rows_of(b, 384)] = select(i, b)
            remote(s2.at[i, rows_of(b, 384)], r2.at[i, rows_of(here[B], 384)],
                   s2_s.at[i, by], s2_r.at[i, here[B]], at(moved(B, by))).start()
    for i, (A, B, C) in enumerate(AXES):
        r2[i, rows_of(here[B], 384)] = select(i, here[B])

    def onward(b_by):
        for i, (A, B, C) in enumerate(AXES):
            b = lax.rem(here[B] + b_by, SIDE)
            if b_by:
                pltpu.make_async_copy(
                    s2.at[i, pl.ds(0, 384)], r2.at[i, rows_of(b, 384)], s2_r.at[i, b]).wait()
        for by in (1, 3, 2, 0):
            for flip in (0, 1):
                for i, (A, B, C) in enumerate(AXES):
                    b = lax.rem(here[B] + b_by, SIDE)
                    slot = here[3] * SIDE + here[C]
                    to = moved(C, by, bool(flip))
                    src = r2.at[i, rows_of(b * 8 + to[C] * 2 + to[3], 48)]
                    dst = arr.at[i, rows_of(slot * SIDE + b, 48)]
                    if by == 0 and flip == 0:
                        pltpu.make_async_copy(src, dst, s3_r.at[i, slot]).start()
                    else:
                        send(src, dst, s3_s.at[i, by * 2 + flip, b_by], s3_r.at[i, slot], at(to))

    onward(0)

    ctx_arrive(fsend, frecv, f_s, f_r)

    def factor(j):
        p = frecv[j, GROUP:PACK, :].astype(F32)
        return jnp.concatenate([jnp.broadcast_to(p[h:h + 1], (8, HD)) for h in range(HEADS)], axis=0)

    def forward(j, acc):
        ssend[j] = acc.astype(BF)
        return factor(j) * acc + frecv[j, 0:GROUP, :].astype(F32)

    lax.fori_loop(0, CTX, forward, jnp.zeros((GROUP, HD), F32), unroll=2)
    ctx_exchange(ssend, srecv, b_s, b_r)

    loads[7].wait()
    d = iota((384, 1), 0).astype(F32)
    lanes384 = iota((384, 384), 1)

    def pick_from(where):
        return jnp.where(lanes384 == where.astype(I32), 1.0, 0.0).astype(BF)

    core_, z_, x_, s_ = digits(d, (SIDE, SIDE, SLOTS))
    pick = pick_from(x_ * 96 + z_ * 24 + core_ * 12 + s_)
    for y in range(SIDE):
        block = jnp.concatenate([hid[x * 384 + y * 96:x * 384 + y * 96 + 96, :] for x in range(SIDE)], axis=0)
        got = dot(pick, block).astype(BF)
        for n in range(8):
            hp[0, n * 192 + y * 48:n * 192 + y * 48 + 48] = got[n * 48:n * 48 + 48]
    pick = pick_from(x_ * 96 + z_ * 24 + core_ * 12 + s_)
    for x in range(SIDE):
        got = dot(pick, hid[x * 384:x * 384 + 384, :]).astype(BF)
        for core in range(2):
            n = core * SIDE + x
            hp[1, n * 192:n * 192 + 192] = got[core * 192:core * 192 + 192]
    core_, y_, z_, s_ = digits(d, (SIDE, SIDE, SLOTS))
    pick = pick_from(y_ * 96 + z_ * 24 + core_ * 12 + s_)
    for x in range(SIDE):
        got = dot(pick, hid[x * 384:x * 384 + 384, :]).astype(BF)
        for n in range(8):
            hp[2, n * 192 + x * 48:n * 192 + x * 48 + 48] = got[n * 48:n * 48 + 48]

    onward(1)
    onward(3)

    for n in (4, 5, 6):
        loads[n].wait()
    ctx_arrive(ssend, srecv, b_s, b_r)

    def widen(j, _):
        f32buf[j] = srecv[j].astype(F32)
        return 0

    lax.fori_loop(0, CTX, widen, 0, unroll=4)

    def attend(h, _):
        cum = cum_s[:, head(h)]
        q_dec = q[:, head(h)].astype(F32) * jnp.exp(cum)
        k_dec = (k[:, head(h)].astype(F32) * jnp.exp(-cum)).astype(BF)
        scores = (dot(q_dec.astype(BF), k_dec, NT) * allowed[...]).astype(BF)
        q_c = (q_dec * carried[...]).astype(BF)
        qcar[:, head(h)] = q_c
        st = f32buf[:, rows_of(h, 8), :].reshape(HD, HD).astype(BF)
        state[h] = st
        out = SCALING * (dot(scores, v[:, head(h)]) + dot(q_c, st, NT))
        mixed[:, head(h)] = res[:, head(h)].astype(F32) + out.astype(BF).astype(F32)
        return 0

    lax.fori_loop(0, HEADS, attend, 0, unroll=UNROLL)
    state_out = pltpu.make_async_copy(state, state_o, out_sem.at[0])
    state_out.start()

    def third(i):
        return slice(i * THIRD, (i + 1) * THIRD)

    def lane_sum(x):
        acc = x[:, 0:HD]
        for n in range(1, x.shape[1] // HD):
            acc = acc + x[:, n * HD:(n + 1) * HD]
        return jnp.sum(acc, axis=1, keepdims=True)

    sq = sum(lane_sum(mixed[:, third(i)] * mixed[:, third(i)]) for i in range(3))
    inverse = lax.rsqrt(sq * (1.0 / WIDTH) + NORM_EPS)
    logits = sum(dot((mixed[:, third(i)] * inverse).astype(BF), router[third(i), :]) for i in range(3))
    rank_t = jnp.full((EXPERTS, TOK), -1.0, F32)
    for j in range(TOP):
        eq = info[j:j + 1, :] == iota((EXPERTS, TOK), 0).astype(F32)
        rank_t = jnp.where(eq, info[TOP + j:TOP + j + 1, :], rank_t)
    rank = jnp.transpose(rank_t)
    chosen = jnp.where(rank >= 0.0, 1.0, 0.0)
    gate = chosen * jax.nn.sigmoid(logits)
    total = jnp.sum(gate, axis=1, keepdims=True)
    weights = gate / total
    w_round = weights.astype(BF).astype(F32)
    rows_ = []
    for s in range(SLOTS):
        rows_.append(jnp.sum(jnp.where(rank == float(s), w_round, 0.0), axis=0, keepdims=True))
    w_t = jnp.concatenate(rows_ + [jnp.zeros((4, EXPERTS), F32)], axis=0).astype(BF)
    turn_e, turn_c = digits(iota((EXPERTS, EXPERTS), 0).astype(F32), (CTX,))
    turn = jnp.where(turn_c * 8 + turn_e == iota((EXPERTS, EXPERTS), 1).astype(F32), 1.0, 0.0).astype(BF)
    small[...] = jnp.zeros_like(small)
    small[:, 0:16] = dot(turn, w_t, NT)
    wsend[...] = small[...].reshape(8, CTX, EXPERTS)

    def exp_out(src, dst, ss, rs):
        def one(i, _):
            t = lax.rem(ex + i, 8)
            remote(src.at[t], dst.at[:, ex], ss.at[i], rs.at[ex], (ctx, t)).start()
            return 0

        lax.fori_loop(1, 8, one, 0)
        pltpu.make_async_copy(src.at[ex], dst.at[:, ex], rs.at[ex]).start()

    def exp_in(src, dst, ss, rs):
        def one(i, _):
            pltpu.make_async_copy(src.at[0], dst.at[:, i], rs.at[i]).wait()
            return 0

        lax.fori_loop(0, 8, one, 0)

    def exp_sent(src, dst, ss, rs):
        def one(i, _):
            pltpu.make_async_copy(src.at[0], dst.at[:, 0], ss.at[i]).wait()
            return 0

        lax.fori_loop(1, 8, one, 0)

    exp_out(wsend, wmid, w1_s, w1_r)
    onward(2)

    for i in range(3):
        for by in (1, 2, 3):
            pltpu.make_async_copy(s2.at[i, pl.ds(0, 384)], r2.at[i, pl.ds(0, 384)], s2_s.at[i, by]).wait()
    loads[8].wait()
    for i in range(3):
        def produce(n, _, i=i):
            s2[i, rows_of(n, 384)] = dot(hp[i, rows_of(n, 384)], w[:, third(i)]).astype(BF)
            return 0

        lax.fori_loop(0, SIDE, produce, 0)
    exp_in(wsend, wmid, w1_s, w1_r)
    ctx_exchange(wmid, wrecv, w2_s, w2_r)

    pb, pa, ps = digits(iota((192, 1), 0).astype(F32), (SIDE, SLOTS))
    lanes192 = iota((192, EXPERTS), 1)
    own_slot = lanes192 == ps.astype(I32)
    small[...] = jnp.zeros_like(small)
    for n in range(8):
        for i, (A, B, C) in enumerate(AXES):
            core = here[3] if n % 2 == 0 else 1 - here[3]
            c = lax.rem(here[C] + (0, 1, 3, 2)[n // 2], SIDE)
            piece = core * SIDE + c
            rows = rows_of(piece, 192)
            pltpu.make_async_copy(s2.at[i, pl.ds(0, 192)], arr.at[i, rows], s3_r.at[i, piece]).wait()
            score = lane_sum(s2[i, rows].astype(F32) * arr[i, rows].astype(F32))
            at_slot = jnp.where(own_slot, score, 0.0)
            coord = [None, None, None]
            coord[A], coord[B], coord[C] = pa, pb, c.astype(F32)
            to = (coord[2] * 2 + core.astype(F32)) * CTX + coord[0] * SIDE + coord[1]
            spread = jnp.where(lanes192 == to.astype(I32), 1.0, 0.0).astype(BF)
            hi, lo = split(at_slot)
            small[...] += dot(spread, hi, TN) + dot(spread, lo, TN)
    csend[...] = small[...].reshape(8, CTX, EXPERTS)
    exp_out(csend, cmid, c1_s, c1_r)

    ctx_arrive(wmid, wrecv, w2_s, w2_r)
    w_in = wrecv[...].reshape(EXPERTS, EXPERTS).astype(BF)

    def expert_grad(i):
        A, B, C = AXES[i]

        def part(n):
            rows = 2 * 192
            d2, b2, a2, s2_ = digits(iota((rows, 1), 0).astype(F32), (SIDE, SIDE, SLOTS))
            core = lax.div(n, 2)
            c2 = (lax.rem(n, 2) * 2).astype(F32) + d2
            src = a2 * STRIDE[A] + b2 * STRIDE[B] + c2 * STRIDE[C] + core.astype(F32)
            lanes_ = iota((rows, EXPERTS), 1)
            pick = jnp.where(lanes_ == src.astype(I32), 1.0, 0.0).astype(BF)
            col = jnp.sum(jnp.where(lanes_ == s2_.astype(I32), dot(pick, w_in), 0.0), axis=1, keepdims=True)
            scaled = (arr[i, rows_of(n, 384)].astype(F32) * col).astype(BF)
            return dot(hp[i, rows_of(n, 384)], scaled, TN)

        gbuf[i] = part(jnp.int32(0))

        def more(n, _):
            gbuf[i] += part(n)
            return 0

        lax.fori_loop(1, SIDE, more, 0)
        cp = pltpu.make_async_copy(gbuf.at[i], grad_o.at[:, pl.ds(i * THIRD, THIRD)], out_sem.at[3 + i])
        cp.start()
        return cp

    exp_in(csend, cmid, c1_s, c1_r)
    ctx_exchange(cmid, crecv, c2_s, c2_r)
    grads = [expert_grad(0)]
    ctx_arrive(cmid, crecv, c2_s, c2_r)

    back = jnp.transpose(crecv[...].reshape(EXPERTS, EXPERTS))
    prob = jnp.zeros((TOK, EXPERTS), F32)
    for s in range(SLOTS):
        prob = jnp.where(rank == float(s), back[s:s + 1], prob)
    mix = jnp.sum(weights * prob, axis=1, keepdims=True)
    logit_grad = (chosen * ((prob - mix) / total * gate * (1.0 - gate))).astype(BF)
    mean = 0.0
    for i in range(3):
        ng = dot(logit_grad, router[third(i), :], NT)
        cum_s[:, third(i)] = ng
        mean = mean + lane_sum(ng * mixed[:, third(i)])
    pull = inverse * inverse * inverse * (mean * (1.0 / WIDTH))

    def residual(h, _):
        grad = (
            og[:, head(h)].astype(F32) + inverse * cum_s[:, head(h)] - mixed[:, head(h)] * pull
        ).astype(BF)
        cot[:, head(h)] = grad
        adj = SCALING * dot(grad, qcar[:, head(h)], TN)
        f32buf[:, rows_of(h, 8), :] = adj.reshape(CTX, 8, HD)
        return 0

    lax.fori_loop(0, HEADS, residual, 0, unroll=UNROLL)

    def pack_back(j, _):
        asend[j] = f32buf[j].astype(BF)
        return 0

    lax.fori_loop(0, CTX, pack_back, 0, unroll=4)
    ctx_exchange(asend, arecv, a_s, a_r)
    gres_out = pltpu.make_async_copy(cot, gres_o, out_sem.at[1])
    gres_out.start()
    grads.append(expert_grad(1))
    ctx_arrive(asend, arecv, a_s, a_r)

    def backward(n, acc):
        j = CTX - 1 - n
        bsend[j] = acc.astype(BF)
        return factor(j) * acc + arecv[j].astype(F32)

    lax.fori_loop(0, CTX, backward, jnp.zeros((GROUP, HD), F32), unroll=2)
    ctx_exchange(bsend, brecv, e_s, e_r)
    grads.append(expert_grad(2))
    ctx_arrive(bsend, brecv, e_s, e_r)

    def widen_back(j, _):
        f32buf[j] = brecv[j].astype(F32)
        return 0

    lax.fori_loop(0, CTX, widen_back, 0, unroll=4)
    state_out.wait()

    def gather(h, _):
        state[h] = f32buf[:, rows_of(h, 8), :].reshape(HD, HD).astype(BF)
        return 0

    lax.fori_loop(0, HEADS, gather, 0, unroll=UNROLL)
    sgrad_out = pltpu.make_async_copy(state, sgrad_o, out_sem.at[2])
    sgrad_out.start()

    for cp in sends:
        cp.wait_send()
    ctx_sent(fsend, frecv, f_s, f_r)
    ctx_sent(ssend, srecv, b_s, b_r)
    ctx_sent(asend, arecv, a_s, a_r)
    ctx_sent(bsend, brecv, e_s, e_r)
    exp_sent(wsend, wmid, w1_s, w1_r)
    exp_sent(csend, cmid, c1_s, c1_r)
    ctx_sent(wmid, wrecv, w2_s, w2_r)
    ctx_sent(cmid, crecv, c2_s, c2_r)
    gres_out.wait()
    sgrad_out.wait()
    for cp in grads:
        cp.wait()


def finish(
    q_ref, k_ref, v_ref, g_ref, cot_ref, state_ref, sgrad_ref, starts_ref, w_ref, m_ref, grad_ref,
    dq_o, dk_o, dv_o, dg_o, gres_o, nw_o, nm_o,
):
    seg_row, seg_col = segments(starts_ref)
    last_seg = seg_row[:, TOK - 1:TOK]
    lower = iota((TOK, TOK), 0) >= iota((TOK, TOK), 1)
    tri = lower.astype(F32).astype(BF)
    allowed = jnp.where((seg_row == seg_col) & lower, 1.0, 0.0)
    carried = jnp.where(seg_col == 0.0, 1.0, 0.0)
    tail = jnp.where(seg_col == last_seg, 1.0, 0.0)
    unbroken = jnp.where(last_seg == 0.0, 1.0, 0.0)
    for n in range(state_ref.shape[0]):
        cols = slice(n * HD, (n + 1) * HD)
        v, cot = v_ref[:, cols], cot_ref[:, cols]
        st, sg = state_ref[n], sgrad_ref[n]
        cum = dot(tri, g_ref[:, cols])
        last = cum[TOK - 1:TOK]
        grow, shrink, to_end = jnp.exp(cum), jnp.exp(-cum), jnp.exp(last - cum) * tail
        k = k_ref[:, cols].astype(F32)
        q_dec = (q_ref[:, cols].astype(F32) * grow).astype(BF)
        k_dec = (k * shrink).astype(BF)
        key_end = (k * to_end).astype(BF)
        scores = (SCALING * allowed * dot(q_dec, k_dec, NT)).astype(BF)
        d_scores = (SCALING * allowed * dot(cot, v, NT)).astype(BF)
        dq_dec = dot(d_scores, k_dec) + (SCALING * carried) * dot(cot, st)
        dk_dec = dot(d_scores, q_dec, TN)
        dk_end = dot(v, sg)
        dv_o[:, cols] = (dot(scores, cot, TN) + dot(key_end, sg, NT)).astype(BF)
        dq_o[:, cols] = (dq_dec * grow).astype(BF)
        dk_o[:, cols] = (dk_dec * shrink + dk_end * to_end).astype(BF)
        end_term = dk_end * key_end.astype(F32)
        d_cum = dq_dec * q_dec.astype(F32) - dk_dec * k_dec.astype(F32) - end_term
        d_last = jnp.sum(end_term, axis=0, keepdims=True) + unbroken * jnp.exp(last) * jnp.sum(
            st.astype(F32) * sg.astype(F32), axis=0, keepdims=True)
        hi, lo = split(d_cum)
        dg_o[:, cols] = (dot(tri, hi, TN) + dot(tri, lo, TN) + d_last).astype(BF)
        gres_o[:, cols] = cot
    wf, mf, grad = w_ref[...].astype(F32), m_ref[...].astype(F32), grad_ref[...]
    turn = BETA_ONE * mf + (1.0 - BETA_ONE) * grad
    direction = jnp.where(turn > 0.0, 1.0, jnp.where(turn < 0.0, -1.0, 0.0))
    nw_o[...] = (wf - LION_RATE * (direction + WEIGHT_DECAY * wf)).astype(BF)
    nm_o[...] = (BETA_TWO * mf + (1.0 - BETA_TWO) * grad).astype(BF)


def local(
    queries, key_vectors, values, log_decay, starts, residual_in, out_grad,
    expert_ids, slot_index, router, hidden_saved, w_down, momentum,
):
    any_, vm = pl.BlockSpec(memory_space=pl.ANY), pl.BlockSpec(memory_space=pltpu.VMEM)
    dma = pltpu.SemaphoreType.DMA
    V = pltpu.VMEM
    scratch = [
        *[V((TOK, WIDTH), BF)] * 6, V((WIDTH, EXPERTS), BF), V((CAP, FF), BF), V((FF, WIDTH), BF),
        V((3, SIDE * TOK, THIRD), BF), V((16, TOK), F32), V((3, SIDE, 16, TOK), F32), V((3, 32, SIDE * TOK), F32),
        *[V((3, CAP, THIRD), BF)] * 3,
        V((3, CAP, FF), BF),
        V((CTX, GROUP, HD), F32), V((CTX, PACK, HD), BF), V((CTX, PACK, HD), BF),
        V((CTX, GROUP, HD), BF), V((CTX, GROUP, HD), BF), V((HEADS, HD, HD), BF),
        *[V((CTX, GROUP, HD), BF)] * 4,
        V((32, HD), F32), V((TOK, TOK), F32), V((TOK, TOK), F32), V((TOK, WIDTH), F32),
        V((TOK, WIDTH), BF), V((TOK, WIDTH), BF), V((EXPERTS, EXPERTS), F32),
        V((8, CTX, EXPERTS), F32), V((CTX, 8, EXPERTS), F32), V((CTX, 8, EXPERTS), F32),
        V((8, CTX, EXPERTS), F32), V((CTX, 8, EXPERTS), F32), V((CTX, 8, EXPERTS), F32),
        V((3, FF, THIRD), F32), V((TOK, WIDTH), F32),
        dma((9,)), dma((6,)),
        dma((3, 4)), dma((3, 4)), dma((3, 4)), dma((3, 4)), dma((3, 4)), dma((3, 4)), dma((3, 8, 4)), dma((3, 8)),
        dma((CTX,)), dma((CTX,)), dma((CTX,)), dma((CTX,)),
        dma((8,)), dma((8,)), dma((CTX,)), dma((CTX,)), dma((8,)), dma((8,)), dma((CTX,)), dma((CTX,)),
        dma((CTX,)), dma((CTX,)), dma((CTX,)), dma((CTX,)),
    ]
    gres, state, sgrad, grad = pl.pallas_call(
        mixer,
        name="dispatch_and_scan",
        out_shape=(
            jax.ShapeDtypeStruct((TOK, WIDTH), BF),
            jax.ShapeDtypeStruct((HEADS, HD, HD), BF),
            jax.ShapeDtypeStruct((HEADS, HD, HD), BF),
            jax.ShapeDtypeStruct((FF, WIDTH), F32),
        ),
        in_specs=[any_] * 9 + [vm] * 3,
        out_specs=(any_,) * 4,
        scratch_shapes=scratch,
        compiler_params=pltpu.CompilerParams(
            collective_id=0, has_side_effects=True, vmem_limit_bytes=62 * 2**20),
    )(
        out_grad[0], queries[0], key_vectors[0], values[0], log_decay[0], residual_in[0], router,
        hidden_saved[0], w_down[0], expert_ids[0].T, slot_index[0].T, starts,
    )
    per = PER
    tok = pl.BlockSpec((TOK, per * HD), lambda i: (0, i))
    st = pl.BlockSpec((per, HD, HD), lambda i: (i, 0, 0))
    ex = pl.BlockSpec((FF, per * HD), lambda i: (0, i))
    outs = pl.pallas_call(
        finish,
        name="backward_and_step",
        grid=(HEADS // per,),
        out_shape=(jax.ShapeDtypeStruct((TOK, WIDTH), BF),) * 5 + (jax.ShapeDtypeStruct((FF, WIDTH), BF),) * 2,
        in_specs=[tok] * 5 + [st] * 2 + [pl.BlockSpec((1, TOK), lambda i: (0, 0))] + [ex] * 3,
        out_specs=(tok,) * 5 + (ex,) * 2,
        compiler_params=pltpu.CompilerParams(vmem_limit_bytes=62 * 2**20),
    )(
        queries[0], key_vectors[0], values[0], log_decay[0], gres, state, sgrad, starts,
        w_down[0], momentum[0], grad,
    )
    return tuple(x[None] for x in outs)


def solution(mesh):
    tokens = P("exp", "ctx", None)
    owned = P(("ctx", "exp"), None, None)
    in_specs = (tokens,) * 4 + (P("exp", "ctx"),) + (tokens,) * 4 + (P(),) + (owned,) * 3
    out_specs = (tokens,) * 5 + (owned,) * 2
    return jax.shard_map(local, mesh=mesh, in_specs=in_specs, out_specs=out_specs, check_vma=False)
```

time: 177 us -> 140 us (0.79)
  Pallas kernels: 162 us -> 137 us
  local copies, waits for them, and re-layouts: 12.8 us -> 0 us
    pallas_call x1, Pallas kernels: 146 us -> 121 us  [local(): pl.pallas_call(mixer, name='dispatch_and_scan', out_shape=(jax.ShapeDtype...]
    unnamed x22 -> x0, local copies, waits for them, and re-layouts: 9.93 us -> none
    squeeze x2 -> x0, local copies, waits for them, and re-layouts: 2.83 us -> none  [the longest x1 1.41 us: local(): slot_index[0]]
where the time goes in v3:
time: 140 us; the launch traced here: 138 us
  Pallas kernels  137 us (98%)
    pallas_call x1, Pallas kernels, local(): pl.pallas_call(mixer, name='dispatch_and_scan', out_shape=(jax.ShapeDtype...  121 us
    pallas_call x1, Pallas kernels, local(): pl.pallas_call(finish, name='backward_and_step', grid=(HEADS // per,), ou...  16.1 us

profile of v3, /device:TPU:1, one launch (start us, length us, event | category | flops | bytes accessed | tf_op | source)
XLA Modules:
  0.0 137.9 jit_solution(8828032898193817505)
XLA Ops:
  0.6 121.0 %dispatch_and_scan.1 = (bf16[128,2304]{1,0:T(8,128)(2,1)}, bf16[18,128,128]{2,1,0:T(8,128)(2,1)}, bf16[18,128,128]{2,1,0:T(8,128)(2,1)}, f32[512,2304]{1,0:T(8,128)}) custom-call(bf16[128,2304]{1,0:T(8,128)(2,1)} %bitcast.34, bf16[128,2304]{1,0:T(8,128)(2,1)} %bitcast.25, bf16[128,2304]{1,0:T(8,128)(2,1)} %bitcast.27, bf16[128,2304]{1,0:T(8,128)(2,1)} %bitcast.29, ...), custom_call_target="tpu_custom_call" | custom-call | tf_op jit(solution)/shard_map/dispatch_and_scan/pallas_call | solution.py:622
  121.7 16.1 %backward_and_step.1 = (bf16[128,2304]{1,0:T(8,128)(2,1)}, bf16[128,2304]{1,0:T(8,128)(2,1)}, bf16[128,2304]{1,0:T(8,128)(2,1)}, bf16[128,2304]{1,0:T(8,128)(2,1...) custom-call(bf16[128,2304]{1,0:T(8,128)(2,1)} %bitcast.26, ...), custom_call_target="tpu_custom_call" | custom-call | tf_op jit(solution)/shard_map/backward_and_step/pallas_call | solution.py:644

commit v4 on v3

--- a/solution.py
+++ b/solution.py
@@ -32,6 +32,7 @@
 I32 = jnp.int32
 UNROLL = 3
 PER = 3
+LION_STEPS = 4
 MESH = pl.DeviceIdType.MESH
 STRIDE = (32, 8, 2)
 AXES = ((0, 1, 2), (1, 2, 0), (2, 0, 1))
@@ -85,9 +86,9 @@
 
 
 def mixer(
-    og_h, q_h, k_h, v_h, g_h, res_h, router_h, hid_h, w_h, ids_ref, slot_ref, starts_ref,
+    og_h, q_h, k_h, v_h, g_h, res_h, router_h, hid_h, w_h, ids_h, slot_h, starts_h,
     gres_o, state_o, sgrad_o, grad_o,
-    og, q, k, v, g, res, router, hid, w,
+    ids_ref, slot_ref, starts_ref, og, q, k, v, g, res, router, hid, w,
     ph1, info, inf, tab, s2, r2, arr, hp,
     f32buf, fsend, frecv, ssend, srecv, state, asend, arecv, bsend, brecv,
     prow, allowed, carried, mixed, qcar, cot, small, wsend, wmid, wrecv, csend, cmid, crecv, gbuf, cum_s,
@@ -112,16 +113,6 @@
             src_ref=src, dst_ref=dst, send_sem=ss, recv_sem=rs, device_id=device, device_id_type=MESH
         )
 
-    loads = []
-    for n, (a, b) in enumerate(
-        ((og_h, og), (k_h, k), (v_h, v), (g_h, g), (q_h, q), (res_h, res), (router_h, router), (hid_h, hid), (w_h, w))
-    ):
-        loads.append(pltpu.make_async_copy(a, b, in_sem.at[n]))
-        loads[-1].start()
-
-    info[0:TOP] = ids_ref[...].astype(F32)
-    info[TOP:2 * TOP] = slot_ref[...].astype(F32)
-
     barrier = pltpu.get_barrier_semaphore()
 
     def tell(device):
@@ -140,6 +131,19 @@
     for axis in (0, 1):
         for by in (1, 2, 3):
             tell(at(moved(axis, by, True)))
+    loads = []
+    for n, (a, b) in enumerate(
+        ((ids_h, ids_ref), (slot_h, slot_ref), (starts_h, starts_ref), (og_h, og), (k_h, k), (v_h, v), (g_h, g), (q_h, q), (res_h, res), (router_h, router), (hid_h, hid), (w_h, w))
+    ):
+        loads.append(pltpu.make_async_copy(a, b, in_sem.at[n]))
+        loads[-1].start()
+
+    small_loads, loads = loads[:3], loads[3:]
+    for cp in small_loads:
+        cp.wait()
+    info[0:TOP] = ids_ref[...].astype(F32)
+    info[TOP:2 * TOP] = slot_ref[...].astype(F32)
+
     pl.semaphore_wait(barrier, CTX - 1 + 7 + 6)
 
     loads[0].wait()
@@ -199,7 +203,8 @@
 
     def ctx_exchange(src, dst, ss, rs):
         def one(i, _):
-            t = lax.rem(ctx + i, CTX)
+            i7 = lax.rem(i * 7, CTX)
+            t = lax.rem(here[0] + lax.div(i7, SIDE), SIDE) * SIDE + lax.rem(here[1] + lax.rem(i7, SIDE), SIDE)
             remote(src.at[t], dst.at[ctx], ss.at[i], rs.at[ctx], (t, ex)).start()
             return 0
 
@@ -267,11 +272,11 @@
                     slot = here[3] * SIDE + here[C]
                     to = moved(C, by, bool(flip))
                     src = r2.at[i, rows_of(b * 8 + to[C] * 2 + to[3], 48)]
-                    dst = arr.at[i, rows_of(slot * SIDE + b, 48)]
+                    dst = arr.at[i, rows_of(b * 8 + slot, 48)]
                     if by == 0 and flip == 0:
-                        pltpu.make_async_copy(src, dst, s3_r.at[i, slot]).start()
+                        pltpu.make_async_copy(src, dst, s3_r.at[i, b]).start()
                     else:
-                        send(src, dst, s3_s.at[i, by * 2 + flip, b_by], s3_r.at[i, slot], at(to))
+                        send(src, dst, s3_s.at[i, by * 2 + flip, b_by], s3_r.at[i, b], at(to))
 
     onward(0)
 
@@ -299,21 +304,18 @@
     pick = pick_from(x_ * 96 + z_ * 24 + core_ * 12 + s_)
     for y in range(SIDE):
         block = jnp.concatenate([hid[x * 384 + y * 96:x * 384 + y * 96 + 96, :] for x in range(SIDE)], axis=0)
-        got = dot(pick, block).astype(BF)
-        for n in range(8):
-            hp[0, n * 192 + y * 48:n * 192 + y * 48 + 48] = got[n * 48:n * 48 + 48]
-    pick = pick_from(x_ * 96 + z_ * 24 + core_ * 12 + s_)
-    for x in range(SIDE):
-        got = dot(pick, hid[x * 384:x * 384 + 384, :]).astype(BF)
-        for core in range(2):
-            n = core * SIDE + x
-            hp[1, n * 192:n * 192 + 192] = got[core * 192:core * 192 + 192]
-    core_, y_, z_, s_ = digits(d, (SIDE, SIDE, SLOTS))
+        hp[0, y * 384:y * 384 + 384] = dot(pick, block).astype(BF)
+    z_, core_, y_, s_ = digits(d, (2, SIDE, SLOTS))
     pick = pick_from(y_ * 96 + z_ * 24 + core_ * 12 + s_)
     for x in range(SIDE):
         got = dot(pick, hid[x * 384:x * 384 + 384, :]).astype(BF)
         for n in range(8):
-            hp[2, n * 192 + x * 48:n * 192 + x * 48 + 48] = got[n * 48:n * 48 + 48]
+            to = n // 2 * 384 + (n % 2 * SIDE + x) * 48
+            hp[1, to:to + 48] = got[n * 48:n * 48 + 48]
+    core_, y_, z_, s_ = digits(d, (SIDE, SIDE, SLOTS))
+    pick = pick_from(y_ * 96 + z_ * 24 + core_ * 12 + s_)
+    for x in range(SIDE):
+        hp[2, x * 384:x * 384 + 384] = dot(pick, hid[x * 384:x * 384 + 384, :]).astype(BF)
 
     onward(1)
     onward(3)
@@ -416,60 +418,58 @@
     exp_in(wsend, wmid, w1_s, w1_r)
     ctx_exchange(wmid, wrecv, w2_s, w2_r)
 
-    pb, pa, ps = digits(iota((192, 1), 0).astype(F32), (SIDE, SLOTS))
-    lanes192 = iota((192, EXPERTS), 1)
-    own_slot = lanes192 == ps.astype(I32)
+    p_core, p_c, p_a, p_s = digits(d, (SIDE, SIDE, SLOTS))
+    lanes_r = iota((384, EXPERTS), 1)
+    own_slot = lanes_r == p_s.astype(I32)
     small[...] = jnp.zeros_like(small)
-    for n in range(8):
+
+    def score_group(b_by):
         for i, (A, B, C) in enumerate(AXES):
-            core = here[3] if n % 2 == 0 else 1 - here[3]
-            c = lax.rem(here[C] + (0, 1, 3, 2)[n // 2], SIDE)
-            piece = core * SIDE + c
-            rows = rows_of(piece, 192)
-            pltpu.make_async_copy(s2.at[i, pl.ds(0, 192)], arr.at[i, rows], s3_r.at[i, piece]).wait()
+            b = lax.rem(here[B] + b_by, SIDE)
+            rows = rows_of(b, 384)
+            pltpu.make_async_copy(s2.at[i, pl.ds(0, 384)], arr.at[i, rows], s3_r.at[i, b]).wait()
             score = lane_sum(s2[i, rows].astype(F32) * arr[i, rows].astype(F32))
             at_slot = jnp.where(own_slot, score, 0.0)
             coord = [None, None, None]
-            coord[A], coord[B], coord[C] = pa, pb, c.astype(F32)
-            to = (coord[2] * 2 + core.astype(F32)) * CTX + coord[0] * SIDE + coord[1]
-            spread = jnp.where(lanes192 == to.astype(I32), 1.0, 0.0).astype(BF)
+            coord[A], coord[B], coord[C] = p_a, b.astype(F32), p_c
+            to = (coord[2] * 2 + p_core) * CTX + coord[0] * SIDE + coord[1]
+            spread = jnp.where(lanes_r == to.astype(I32), 1.0, 0.0).astype(BF)
             hi, lo = split(at_slot)
             small[...] += dot(spread, hi, TN) + dot(spread, lo, TN)
+
+    def grad_group(i, b_by):
+        A, B, C = AXES[i]
+        b = lax.rem(here[B] + b_by, SIDE)
+        src = p_a * STRIDE[A] + b.astype(F32) * STRIDE[B] + p_c * STRIDE[C] + p_core
+        pick = jnp.where(lanes_r == src.astype(I32), 1.0, 0.0).astype(BF)
+        w_in = wrecv[...].reshape(EXPERTS, EXPERTS).astype(BF)
+        col = jnp.sum(jnp.where(own_slot, dot(pick, w_in), 0.0), axis=1, keepdims=True)
+        scaled = (arr[i, rows_of(b, 384)].astype(F32) * col).astype(BF)
+        part = dot(hp[i, rows_of(b, 384)], scaled, TN)
+        if b_by == 0:
+            gbuf[i] = part
+        else:
+            gbuf[i] += part
+
+    grads = []
+
+    def last_grad(i):
+        for by in range(SIDE):
+            grad_group(i, by)
+        cp = pltpu.make_async_copy(gbuf.at[i], grad_o.at[:, pl.ds(i * THIRD, THIRD)], out_sem.at[3 + i])
+        cp.start()
+        grads.append(cp)
+
+    score_group(0)
+    score_group(1)
+    score_group(3)
+    score_group(2)
     csend[...] = small[...].reshape(8, CTX, EXPERTS)
     exp_out(csend, cmid, c1_s, c1_r)
-
-    ctx_arrive(wmid, wrecv, w2_s, w2_r)
-    w_in = wrecv[...].reshape(EXPERTS, EXPERTS).astype(BF)
-
-    def expert_grad(i):
-        A, B, C = AXES[i]
-
-        def part(n):
-            rows = 2 * 192
-            d2, b2, a2, s2_ = digits(iota((rows, 1), 0).astype(F32), (SIDE, SIDE, SLOTS))
-            core = lax.div(n, 2)
-            c2 = (lax.rem(n, 2) * 2).astype(F32) + d2
-            src = a2 * STRIDE[A] + b2 * STRIDE[B] + c2 * STRIDE[C] + core.astype(F32)
-            lanes_ = iota((rows, EXPERTS), 1)
-            pick = jnp.where(lanes_ == src.astype(I32), 1.0, 0.0).astype(BF)
-            col = jnp.sum(jnp.where(lanes_ == s2_.astype(I32), dot(pick, w_in), 0.0), axis=1, keepdims=True)
-            scaled = (arr[i, rows_of(n, 384)].astype(F32) * col).astype(BF)
-            return dot(hp[i, rows_of(n, 384)], scaled, TN)
-
-        gbuf[i] = part(jnp.int32(0))
-
-        def more(n, _):
-            gbuf[i] += part(n)
-            return 0
-
-        lax.fori_loop(1, SIDE, more, 0)
-        cp = pltpu.make_async_copy(gbuf.at[i], grad_o.at[:, pl.ds(i * THIRD, THIRD)], out_sem.at[3 + i])
-        cp.start()
-        return cp
-
     exp_in(csend, cmid, c1_s, c1_r)
     ctx_exchange(cmid, crecv, c2_s, c2_r)
-    grads = [expert_grad(0)]
+    ctx_arrive(wmid, wrecv, w2_s, w2_r)
+    last_grad(0)
     ctx_arrive(cmid, crecv, c2_s, c2_r)
 
     back = jnp.transpose(crecv[...].reshape(EXPERTS, EXPERTS))
@@ -504,7 +504,7 @@
     ctx_exchange(asend, arecv, a_s, a_r)
     gres_out = pltpu.make_async_copy(cot, gres_o, out_sem.at[1])
     gres_out.start()
-    grads.append(expert_grad(1))
+    last_grad(1)
     ctx_arrive(asend, arecv, a_s, a_r)
 
     def backward(n, acc):
@@ -514,7 +514,7 @@
 
     lax.fori_loop(0, CTX, backward, jnp.zeros((GROUP, HD), F32), unroll=2)
     ctx_exchange(bsend, brecv, e_s, e_r)
-    grads.append(expert_grad(2))
+    last_grad(2)
     ctx_arrive(bsend, brecv, e_s, e_r)
 
     def widen_back(j, _):
@@ -549,48 +549,120 @@
 
 
 def finish(
-    q_ref, k_ref, v_ref, g_ref, cot_ref, state_ref, sgrad_ref, starts_ref, w_ref, m_ref, grad_ref,
-    dq_o, dk_o, dv_o, dg_o, gres_o, nw_o, nm_o,
+    q_h, k_h, v_h, g_h, cot_h, state_h, sgrad_h, starts_ref, w_h, m_h, grad_h,
+    dq_h, dk_h, dv_h, dg_h, gres_h, nw_h, nm_h,
+    q, k, v, g, cot, state, sgrad, w, m, grad, dq, dk, dv, dg, in_sem, out_sem, l_sem, s_sem,
 ):
+    wide, tall = PER * HD, FF // LION_STEPS
+    head_steps = HEADS // PER
+
+    def cols(n):
+        return pl.ds(n * wide, wide)
+
+    def rows(n):
+        return pl.ds(n * tall, tall)
+
+    def loads(n):
+        out = [
+            pltpu.make_async_copy(a.at[:, cols(n)], b.at[:, cols(n)], in_sem.at[n, j])
+            for j, (a, b) in enumerate(((g_h, g), (k_h, k), (q_h, q), (v_h, v), (cot_h, cot)))
+        ]
+        for j, (a, b) in enumerate(((state_h, state), (sgrad_h, sgrad))):
+            out.append(pltpu.make_async_copy(a.at[pl.ds(n * PER, PER)], b.at[pl.ds(n * PER, PER)], in_sem.at[n, 5 + j]))
+        return out
+
+    def lion_loads(n):
+        return [
+            pltpu.make_async_copy(a.at[rows(n)], b.at[rows(n)], l_sem.at[n, j])
+            for j, (a, b) in enumerate(((w_h, w), (m_h, m), (grad_h, grad)))
+        ]
+
+    stores = []
+
+    def store(a, b, sem):
+        cp = pltpu.make_async_copy(a, b, sem)
+        cp.start()
+        stores.append(cp)
+
+    order = []
+    for n in range(max(head_steps, LION_STEPS)):
+        if n < head_steps:
+            order.append(("heads", n, loads(n)))
+        if n < LION_STEPS:
+            order.append(("lion", n, lion_loads(n)))
+    for _, _, copies in order:
+        for cp in copies:
+            cp.start()
+
     seg_row, seg_col = segments(starts_ref)
     last_seg = seg_row[:, TOK - 1:TOK]
     lower = iota((TOK, TOK), 0) >= iota((TOK, TOK), 1)
-    tri = lower.astype(F32).astype(BF)
-    allowed = jnp.where((seg_row == seg_col) & lower, 1.0, 0.0)
-    carried = jnp.where(seg_col == 0.0, 1.0, 0.0)
+    upper = iota((TOK, TOK), 0) <= iota((TOK, TOK), 1)
+    tri, tri_up = lower.astype(F32).astype(BF), upper.astype(F32).astype(BF)
+    same = seg_row == seg_col
+    below = jnp.where(same & lower, SCALING, 0.0)
+    above = jnp.where(same & upper, SCALING, 0.0)
+    carried = jnp.where(seg_col == 0.0, SCALING, 0.0)
     tail = jnp.where(seg_col == last_seg, 1.0, 0.0)
     unbroken = jnp.where(last_seg == 0.0, 1.0, 0.0)
-    for n in range(state_ref.shape[0]):
-        cols = slice(n * HD, (n + 1) * HD)
-        v, cot = v_ref[:, cols], cot_ref[:, cols]
-        st, sg = state_ref[n], sgrad_ref[n]
-        cum = dot(tri, g_ref[:, cols])
+
+    def heads_step(n):
+        at_ = slice(n * wide, (n + 1) * wide)
+        store(cot.at[:, cols(n)], gres_h.at[:, cols(n)], out_sem.at[n, 4])
+        cum = dot(tri, g[:, at_])
         last = cum[TOK - 1:TOK]
         grow, shrink, to_end = jnp.exp(cum), jnp.exp(-cum), jnp.exp(last - cum) * tail
-        k = k_ref[:, cols].astype(F32)
-        q_dec = (q_ref[:, cols].astype(F32) * grow).astype(BF)
-        k_dec = (k * shrink).astype(BF)
-        key_end = (k * to_end).astype(BF)
-        scores = (SCALING * allowed * dot(q_dec, k_dec, NT)).astype(BF)
-        d_scores = (SCALING * allowed * dot(cot, v, NT)).astype(BF)
-        dq_dec = dot(d_scores, k_dec) + (SCALING * carried) * dot(cot, st)
-        dk_dec = dot(d_scores, q_dec, TN)
-        dk_end = dot(v, sg)
-        dv_o[:, cols] = (dot(scores, cot, TN) + dot(key_end, sg, NT)).astype(BF)
-        dq_o[:, cols] = (dq_dec * grow).astype(BF)
-        dk_o[:, cols] = (dk_dec * shrink + dk_end * to_end).astype(BF)
-        end_term = dk_end * key_end.astype(F32)
-        d_cum = dq_dec * q_dec.astype(F32) - dk_dec * k_dec.astype(F32) - end_term
-        d_last = jnp.sum(end_term, axis=0, keepdims=True) + unbroken * jnp.exp(last) * jnp.sum(
-            st.astype(F32) * sg.astype(F32), axis=0, keepdims=True)
-        hi, lo = split(d_cum)
-        dg_o[:, cols] = (dot(tri, hi, TN) + dot(tri, lo, TN) + d_last).astype(BF)
-        gres_o[:, cols] = cot
-    wf, mf, grad = w_ref[...].astype(F32), m_ref[...].astype(F32), grad_ref[...]
-    turn = BETA_ONE * mf + (1.0 - BETA_ONE) * grad
-    direction = jnp.where(turn > 0.0, 1.0, jnp.where(turn < 0.0, -1.0, 0.0))
-    nw_o[...] = (wf - LION_RATE * (direction + WEIGHT_DECAY * wf)).astype(BF)
-    nm_o[...] = (BETA_TWO * mf + (1.0 - BETA_TWO) * grad).astype(BF)
+        kf = k[:, at_].astype(F32)
+        q_dec = (q[:, at_].astype(F32) * grow).astype(BF)
+        k_dec = (kf * shrink).astype(BF)
+        key_end = (kf * to_end).astype(BF)
+        d_cums, d_lasts = [], []
+        R = range(PER)
+        part = [slice(j * HD, (j + 1) * HD) for j in R]
+        full = [slice(n * wide + j * HD, n * wide + (j + 1) * HD) for j in R]
+        vs, cs = [v[:, c] for c in full], [cot[:, c] for c in full]
+        scores_t = [(above * dot(k_dec[:, c], q_dec[:, c], NT)).astype(BF) for c in part]
+        d_scores = [(below * dot(cs[j], vs[j], NT)).astype(BF) for j in R]
+        d_scores_t = [(above * dot(vs[j], cs[j], NT)).astype(BF) for j in R]
+        dq_dec = [dot(d_scores[j], k_dec[:, part[j]]) + carried * dot(cs[j], state[n * PER + j]) for j in R]
+        dk_dec = [dot(d_scores_t[j], q_dec[:, part[j]]) for j in R]
+        dk_end = [dot(vs[j], sgrad[n * PER + j]) for j in R]
+        for j in R:
+            c, f, st, sg = part[j], full[j], state[n * PER + j], sgrad[n * PER + j]
+            dv[:, f] = (dot(scores_t[j], cs[j]) + dot(key_end[:, c], sg, NT)).astype(BF)
+            dq[:, f] = (dq_dec[j] * grow[:, c]).astype(BF)
+            dk[:, f] = (dk_dec[j] * shrink[:, c] + dk_end[j] * to_end[:, c]).astype(BF)
+            end_term = dk_end[j] * key_end[:, c].astype(F32)
+            d_cums.append(dq_dec[j] * q_dec[:, c].astype(F32) - dk_dec[j] * k_dec[:, c].astype(F32) - end_term)
+            d_lasts.append(
+                jnp.sum(end_term, axis=0, keepdims=True)
+                + unbroken * jnp.exp(last[:, c]) * jnp.sum(st.astype(F32) * sg.astype(F32), axis=0, keepdims=True))
+        hi, lo = split(jnp.concatenate(d_cums, axis=1))
+        dg[:, at_] = (dot(tri_up, hi) + dot(tri_up, lo) + jnp.concatenate(d_lasts, axis=1)).astype(BF)
+        for j, (a, b) in enumerate(((dq, dq_h), (dk, dk_h), (dv, dv_h), (dg, dg_h))):
+            store(a.at[:, cols(n)], b.at[:, cols(n)], out_sem.at[n, j])
+
+    def lion_step(n):
+        r = slice(n * tall, (n + 1) * tall)
+        for third in range(3):
+            c = slice(third * THIRD, (third + 1) * THIRD)
+            wf, mf, gf = w[r, c].astype(F32), m[r, c].astype(F32), grad[r, c]
+            turn = BETA_ONE * mf + (1.0 - BETA_ONE) * gf
+            move = jnp.where(turn > 0.0, -LION_RATE, jnp.where(turn < 0.0, LION_RATE, 0.0))
+            w[r, c] = (wf * (1.0 - LION_RATE * WEIGHT_DECAY) + move).astype(BF)
+            m[r, c] = (BETA_TWO * mf + (1.0 - BETA_TWO) * gf).astype(BF)
+        store(w.at[rows(n)], nw_h.at[rows(n)], s_sem.at[n, 0])
+        store(m.at[rows(n)], nm_h.at[rows(n)], s_sem.at[n, 1])
+
+    for kind, n, copies in order:
+        for cp in copies:
+            cp.wait()
+        if kind == "heads":
+            heads_step(n)
+        else:
+            lion_step(n)
+    for cp in stores:
+        cp.wait()
 
 
 def local(
@@ -601,6 +673,7 @@
     dma = pltpu.SemaphoreType.DMA
     V = pltpu.VMEM
     scratch = [
+        V((TOP, TOK), I32), V((TOP, TOK), I32), V((1, TOK), I32),
         *[V((TOK, WIDTH), BF)] * 6, V((WIDTH, EXPERTS), BF), V((CAP, FF), BF), V((FF, WIDTH), BF),
         V((3, SIDE * TOK, THIRD), BF), V((16, TOK), F32), V((3, SIDE, 16, TOK), F32), V((3, 32, SIDE * TOK), F32),
         *[V((3, CAP, THIRD), BF)] * 3,
@@ -613,8 +686,8 @@
         V((8, CTX, EXPERTS), F32), V((CTX, 8, EXPERTS), F32), V((CTX, 8, EXPERTS), F32),
         V((8, CTX, EXPERTS), F32), V((CTX, 8, EXPERTS), F32), V((CTX, 8, EXPERTS), F32),
         V((3, FF, THIRD), F32), V((TOK, WIDTH), F32),
-        dma((9,)), dma((6,)),
-        dma((3, 4)), dma((3, 4)), dma((3, 4)), dma((3, 4)), dma((3, 4)), dma((3, 4)), dma((3, 8, 4)), dma((3, 8)),
+        dma((12,)), dma((6,)),
+        dma((3, 4)), dma((3, 4)), dma((3, 4)), dma((3, 4)), dma((3, 4)), dma((3, 4)), dma((3, 8, 4)), dma((3, 4)),
         dma((CTX,)), dma((CTX,)), dma((CTX,)), dma((CTX,)),
         dma((8,)), dma((8,)), dma((CTX,)), dma((CTX,)), dma((8,)), dma((8,)), dma((CTX,)), dma((CTX,)),
         dma((CTX,)), dma((CTX,)), dma((CTX,)), dma((CTX,)),
@@ -628,7 +701,7 @@
             jax.ShapeDtypeStruct((HEADS, HD, HD), BF),
             jax.ShapeDtypeStruct((FF, WIDTH), F32),
         ),
-        in_specs=[any_] * 9 + [vm] * 3,
+        in_specs=[any_] * 12,
         out_specs=(any_,) * 4,
         scratch_shapes=scratch,
         compiler_params=pltpu.CompilerParams(
@@ -637,17 +710,17 @@
         out_grad[0], queries[0], key_vectors[0], values[0], log_decay[0], residual_in[0], router,
         hidden_saved[0], w_down[0], expert_ids[0].T, slot_index[0].T, starts,
     )
-    per = PER
-    tok = pl.BlockSpec((TOK, per * HD), lambda i: (0, i))
-    st = pl.BlockSpec((per, HD, HD), lambda i: (i, 0, 0))
-    ex = pl.BlockSpec((FF, per * HD), lambda i: (0, i))
+    tok = V((TOK, WIDTH), BF)
     outs = pl.pallas_call(
         finish,
         name="backward_and_step",
-        grid=(HEADS // per,),
         out_shape=(jax.ShapeDtypeStruct((TOK, WIDTH), BF),) * 5 + (jax.ShapeDtypeStruct((FF, WIDTH), BF),) * 2,
-        in_specs=[tok] * 5 + [st] * 2 + [pl.BlockSpec((1, TOK), lambda i: (0, 0))] + [ex] * 3,
-        out_specs=(tok,) * 5 + (ex,) * 2,
+        in_specs=[any_] * 7 + [vm] + [any_] * 3,
+        out_specs=(any_,) * 7,
+        scratch_shapes=[
+            *[tok] * 5, *[V((HEADS, HD, HD), BF)] * 2, *[V((FF, WIDTH), BF)] * 2, V((FF, WIDTH), F32), *[tok] * 4,
+            dma((HEADS // PER, 7)), dma((HEADS // PER, 5)), dma((LION_STEPS, 3)), dma((LION_STEPS, 2)),
+        ],
         compiler_params=pltpu.CompilerParams(vmem_limit_bytes=62 * 2**20),
     )(
         queries[0], key_vectors[0], values[0], log_decay[0], gres, state, sgrad, starts,

time: 140 us -> 131 us (0.936)
  Pallas kernels: 137 us -> 129 us
    pallas_call x1, Pallas kernels: 16.1 us -> 12 us  [local(): pl.pallas_call(finish, name='backward_and_step', out_shape=(jax.ShapeDtyp...]
    pallas_call x1, Pallas kernels: 121 us -> 117 us  [local(): pl.pallas_call(mixer, name='dispatch_and_scan', out_shape=(jax.ShapeDtype...]
where the time goes in v4:
time: 131 us; the launch traced here: 130 us
  Pallas kernels  129 us (98%)
    pallas_call x1, Pallas kernels, local(): pl.pallas_call(mixer, name='dispatch_and_scan', out_shape=(jax.ShapeDtype...  117 us
    pallas_call x1, Pallas kernels, local(): pl.pallas_call(finish, name='backward_and_step', out_shape=(jax.ShapeDtyp...  12 us

profile of v4, /device:TPU:1, one launch (start us, length us, event | category | flops | bytes accessed | tf_op | source)
XLA Modules:
  0.0 130.2 jit_solution(17439469030097458868)
XLA Ops:
  0.6 117.4 %dispatch_and_scan.1 = (bf16[128,2304]{1,0:T(8,128)(2,1)}, bf16[18,128,128]{2,1,0:T(8,128)(2,1)}, bf16[18,128,128]{2,1,0:T(8,128)(2,1)}, f32[512,2304]{1,0:T(8,128)}) custom-call(bf16[128,2304]{1,0:T(8,128)(2,1)} %bitcast.34, bf16[128,2304]{1,0:T(8,128)(2,1)} %bitcast.25, bf16[128,2304]{1,0:T(8,128)(2,1)} %bitcast.27, bf16[128,2304]{1,0:T(8,128)(2,1)} %bitcast.29, ...), custom_call_target="tpu_custom_call" | custom-call | tf_op jit(solution)/shard_map/dispatch_and_scan/pallas_call | solution.py:695
  118.1 12.0 %backward_and_step.1 = (bf16[128,2304]{1,0:T(8,128)(2,1)}, bf16[128,2304]{1,0:T(8,128)(2,1)}, bf16[128,2304]{1,0:T(8,128)(2,1)}, bf16[128,2304]{1,0:T(8,128)(2,1...) custom-call(bf16[128,2304]{1,0:T(8,128)(2,1)} %bitcast.26, ...), custom_call_target="tpu_custom_call" | custom-call | tf_op jit(solution)/shard_map/backward_and_step/pallas_call | solution.py:714

commit v5 on v4

--- a/solution.py
+++ b/solution.py
@@ -16,7 +16,8 @@
 SLOTS = 12
 EXPERTS = 128
 CAP = EXPERTS * SLOTS
-THIRD = WIDTH // 3
+PARTS = (768, 768, 768)
+STARTS = (0, 768, 1536)
 SIDE = 4
 CTX = 16
 GROUP = HEADS * 8
@@ -31,8 +32,7 @@
 F32 = jnp.float32
 I32 = jnp.int32
 UNROLL = 3
-PER = 3
-LION_STEPS = 4
+PER = 6
 MESH = pl.DeviceIdType.MESH
 STRIDE = (32, 8, 2)
 AXES = ((0, 1, 2), (1, 2, 0), (2, 0, 1))
@@ -50,6 +50,18 @@
 def split(x):
     hi = x.astype(BF)
     return hi, (x - hi.astype(F32)).astype(BF)
+
+
+def part(i):
+    return slice(STARTS[i], STARTS[i] + PARTS[i])
+
+
+def lanes(i):
+    return pl.ds(STARTS[i], PARTS[i])
+
+
+def half_lanes(i, h):
+    return pl.ds(STARTS[i] + h * (PARTS[i] // 2), PARTS[i] // 2)
 
 
 def iota(shape, dim):
@@ -86,9 +98,9 @@
 
 
 def mixer(
-    og_h, q_h, k_h, v_h, g_h, res_h, router_h, hid_h, w_h, ids_h, slot_h, starts_h,
-    gres_o, state_o, sgrad_o, grad_o,
-    ids_ref, slot_ref, starts_ref, og, q, k, v, g, res, router, hid, w,
+    og_h, q_h, k_h, v_h, g_h, res_h, router_h, hid_h, w_h, m_h, ids_h, slot_h, starts_h,
+    gres_o, state_o, sgrad_o, nw_o, nm_o,
+    ids_ref, slot_ref, starts_ref, og, q, k, v, g, res, router, hid, w, m,
     ph1, info, inf, tab, s2, r2, arr, hp,
     f32buf, fsend, frecv, ssend, srecv, state, asend, arecv, bsend, brecv,
     prow, allowed, carried, mixed, qcar, cot, small, wsend, wmid, wrecv, csend, cmid, crecv, gbuf, cum_s,
@@ -133,7 +145,7 @@
             tell(at(moved(axis, by, True)))
     loads = []
     for n, (a, b) in enumerate(
-        ((ids_h, ids_ref), (slot_h, slot_ref), (starts_h, starts_ref), (og_h, og), (k_h, k), (v_h, v), (g_h, g), (q_h, q), (res_h, res), (router_h, router), (hid_h, hid), (w_h, w))
+        ((ids_h, ids_ref), (slot_h, slot_ref), (starts_h, starts_ref), (og_h, og), (k_h, k), (v_h, v), (g_h, g), (q_h, q), (res_h, res), (router_h, router), (hid_h, hid), (w_h, w), (m_h, m))
     ):
         loads.append(pltpu.make_async_copy(a, b, in_sem.at[n]))
         loads[-1].start()
@@ -160,13 +172,16 @@
     for by in (1, 3, 2):
         for i in range(3):
             send(info, inf.at[i, here[i]], i1_s.at[i, by], i1_r.at[i, here[i]], at(moved(i, by)))
-    for by in (1, 3, 2):
-        for i in range(3):
-            send(og.at[:, pl.ds(i * THIRD, THIRD)], ph1.at[i, rows_of(here[i], TOK)],
-                 s1_s.at[i, by], s1_r.at[i, here[i]], at(moved(i, by)))
+    for h in range(2):
+        for by in (1, 3, 2):
+            for i in range(3):
+                send(og.at[:, half_lanes(i, h)], ph1.at[rows_of(here[i], TOK), half_lanes(i, h)],
+                     s1_s.at[i, h, by], s1_r.at[i, h, here[i]], at(moved(i, by)))
     for i in range(3):
-        pltpu.make_async_copy(
-            og.at[:, pl.ds(i * THIRD, THIRD)], ph1.at[i, rows_of(here[i], TOK)], s1_r.at[i, here[i]]).start()
+        for h in range(2):
+            pltpu.make_async_copy(
+                og.at[:, half_lanes(i, h)], ph1.at[rows_of(here[i], TOK), half_lanes(i, h)],
+                s1_r.at[i, h, here[i]]).start()
         pltpu.make_async_copy(info, inf.at[i, here[i]], i1_r.at[i, here[i]]).start()
 
     for n in (1, 2, 3):
@@ -201,26 +216,31 @@
 
     lax.fori_loop(0, CTX, pack, 0, unroll=4)
 
-    def ctx_exchange(src, dst, ss, rs):
+    def ctx_exchange(src, dst, ss, rs, rows=None):
+        def of(ref, n):
+            return ref.at[n] if rows is None else ref.at[n, rows]
+
         def one(i, _):
             i7 = lax.rem(i * 7, CTX)
             t = lax.rem(here[0] + lax.div(i7, SIDE), SIDE) * SIDE + lax.rem(here[1] + lax.rem(i7, SIDE), SIDE)
-            remote(src.at[t], dst.at[ctx], ss.at[i], rs.at[ctx], (t, ex)).start()
+            remote(of(src, t), of(dst, ctx), ss.at[i], rs.at[ctx], (t, ex)).start()
             return 0
 
         lax.fori_loop(1, CTX, one, 0)
-        pltpu.make_async_copy(src.at[ctx], dst.at[ctx], rs.at[ctx]).start()
-
-    def ctx_arrive(src, dst, ss, rs):
+        pltpu.make_async_copy(of(src, ctx), of(dst, ctx), rs.at[ctx]).start()
+
+    def ctx_arrive(src, dst, ss, rs, rows=None):
         def one(i, _):
-            pltpu.make_async_copy(src.at[0], dst.at[i], rs.at[i]).wait()
+            a, b = (src.at[0], dst.at[i]) if rows is None else (src.at[0, rows], dst.at[i, rows])
+            pltpu.make_async_copy(a, b, rs.at[i]).wait()
             return 0
 
         lax.fori_loop(0, CTX, one, 0)
 
-    def ctx_sent(src, dst, ss, rs):
+    def ctx_sent(src, dst, ss, rs, rows=None):
         def one(i, _):
-            pltpu.make_async_copy(src.at[0], dst.at[0], ss.at[i]).wait()
+            a, b = (src.at[0], dst.at[0]) if rows is None else (src.at[0, rows], dst.at[0, rows])
+            pltpu.make_async_copy(a, b, ss.at[i]).wait()
             return 0
 
         lax.fori_loop(1, CTX, one, 0)
@@ -239,40 +259,52 @@
                 found = jnp.where(inf[i, a, j:j + 1, :] == e, inf[i, a, TOP + j:TOP + j + 1, :], found)
             tab[i, :, a * TOK:(a + 1) * TOK] = found
 
-    def select(i, b):
+    def choose(i, b):
         blocks = []
-        for m in range(8):
-            line = tab[i, pl.ds(b * 8 + m, 1), :]
+        for m_ in range(8):
+            line = tab[i, pl.ds(b * 8 + m_, 1), :]
             blocks.append(jnp.where(line == pattern, 1.0, 0.0).astype(BF))
-        return dot(jnp.concatenate(blocks, axis=0), ph1[i]).astype(BF)
-
-    for by in (1, 3, 2):
-        for i, (A, B, C) in enumerate(AXES):
-            if by == 1:
-                for a in range(SIDE):
-                    pltpu.make_async_copy(
-                        og.at[:, pl.ds(0, THIRD)], ph1.at[i, pl.ds(a * TOK, TOK)], s1_r.at[i, a]).wait()
-            b = lax.rem(here[B] + by, SIDE)
-            s2[i, rows_of(b, 384)] = select(i, b)
-            remote(s2.at[i, rows_of(b, 384)], r2.at[i, rows_of(here[B], 384)],
-                   s2_s.at[i, by], s2_r.at[i, here[B]], at(moved(B, by))).start()
+        hp[i, rows_of(b, 384)] = jnp.concatenate(blocks, axis=0)
+
+    def half(i, h):
+        return slice(STARTS[i] + h * (PARTS[i] // 2), STARTS[i] + (h + 1) * (PARTS[i] // 2))
+
+    def select(i, h, b):
+        return dot(hp[i, rows_of(b, 384)], ph1[:, half(i, h)]).astype(BF)
+
+    for h in range(2):
+        for by in (1, 3, 2):
+            for i, (A, B, C) in enumerate(AXES):
+                b = lax.rem(here[B] + by, SIDE)
+                if h == 0:
+                    choose(i, b)
+                if by == 1:
+                    for a in range(SIDE):
+                        pltpu.make_async_copy(
+                            og.at[:, half_lanes(i, h)], ph1.at[pl.ds(a * TOK, TOK), half_lanes(i, h)],
+                            s1_r.at[i, h, a]).wait()
+                s2[rows_of(b, 384), half(i, h)] = select(i, h, b)
+                remote(s2.at[rows_of(b, 384), half_lanes(i, h)], r2.at[rows_of(here[B], 384), half_lanes(i, h)],
+                       s2_s.at[i, h, by], s2_r.at[i, h, here[B]], at(moved(B, by))).start()
     for i, (A, B, C) in enumerate(AXES):
-        r2[i, rows_of(here[B], 384)] = select(i, here[B])
+        choose(i, here[B])
+        for h in range(2):
+            r2[rows_of(here[B], 384), half(i, h)] = select(i, h, here[B])
 
     def onward(b_by):
         for i, (A, B, C) in enumerate(AXES):
             b = lax.rem(here[B] + b_by, SIDE)
             if b_by:
-                pltpu.make_async_copy(
-                    s2.at[i, pl.ds(0, 384)], r2.at[i, rows_of(b, 384)], s2_r.at[i, b]).wait()
-        for by in (1, 3, 2, 0):
-            for flip in (0, 1):
-                for i, (A, B, C) in enumerate(AXES):
-                    b = lax.rem(here[B] + b_by, SIDE)
-                    slot = here[3] * SIDE + here[C]
+                for h in range(2):
+                    pltpu.make_async_copy(
+                        s2.at[pl.ds(0, 384), half_lanes(i, h)], r2.at[rows_of(b, 384), half_lanes(i, h)],
+                        s2_r.at[i, h, b]).wait()
+            slot = here[3] * SIDE + here[C]
+            for by in (2, 1, 3, 0):
+                for flip in (0, 1):
                     to = moved(C, by, bool(flip))
-                    src = r2.at[i, rows_of(b * 8 + to[C] * 2 + to[3], 48)]
-                    dst = arr.at[i, rows_of(b * 8 + slot, 48)]
+                    src = r2.at[rows_of(b * 8 + to[C] * 2 + to[3], 48), lanes(i)]
+                    dst = arr.at[rows_of(b * 8 + slot, 48), lanes(i)]
                     if by == 0 and flip == 0:
                         pltpu.make_async_copy(src, dst, s3_r.at[i, b]).start()
                     else:
@@ -282,9 +314,9 @@
 
     ctx_arrive(fsend, frecv, f_s, f_r)
 
-    def factor(j):
+    def factor(j, first=0, last=HEADS):
         p = frecv[j, GROUP:PACK, :].astype(F32)
-        return jnp.concatenate([jnp.broadcast_to(p[h:h + 1], (8, HD)) for h in range(HEADS)], axis=0)
+        return jnp.concatenate([jnp.broadcast_to(p[h:h + 1], (8, HD)) for h in range(first, last)], axis=0)
 
     def forward(j, acc):
         ssend[j] = acc.astype(BF)
@@ -319,6 +351,7 @@
 
     onward(1)
     onward(3)
+    onward(2)
 
     for n in (4, 5, 6):
         loads[n].wait()
@@ -347,18 +380,15 @@
     state_out = pltpu.make_async_copy(state, state_o, out_sem.at[0])
     state_out.start()
 
-    def third(i):
-        return slice(i * THIRD, (i + 1) * THIRD)
-
     def lane_sum(x):
         acc = x[:, 0:HD]
         for n in range(1, x.shape[1] // HD):
             acc = acc + x[:, n * HD:(n + 1) * HD]
         return jnp.sum(acc, axis=1, keepdims=True)
 
-    sq = sum(lane_sum(mixed[:, third(i)] * mixed[:, third(i)]) for i in range(3))
+    sq = sum(lane_sum(mixed[:, part(i)] * mixed[:, part(i)]) for i in range(3))
     inverse = lax.rsqrt(sq * (1.0 / WIDTH) + NORM_EPS)
-    logits = sum(dot((mixed[:, third(i)] * inverse).astype(BF), router[third(i), :]) for i in range(3))
+    logits = sum(dot((mixed[:, part(i)] * inverse).astype(BF), router[part(i), :]) for i in range(3))
     rank_t = jnp.full((EXPERTS, TOK), -1.0, F32)
     for j in range(TOP):
         eq = info[j:j + 1, :] == iota((EXPERTS, TOK), 0).astype(F32)
@@ -403,15 +433,17 @@
         lax.fori_loop(1, 8, one, 0)
 
     exp_out(wsend, wmid, w1_s, w1_r)
-    onward(2)
 
     for i in range(3):
         for by in (1, 2, 3):
-            pltpu.make_async_copy(s2.at[i, pl.ds(0, 384)], r2.at[i, pl.ds(0, 384)], s2_s.at[i, by]).wait()
+            for h in range(2):
+                pltpu.make_async_copy(
+                    s2.at[pl.ds(0, 384), half_lanes(i, h)], r2.at[pl.ds(0, 384), half_lanes(i, h)],
+                    s2_s.at[i, h, by]).wait()
     loads[8].wait()
     for i in range(3):
         def produce(n, _, i=i):
-            s2[i, rows_of(n, 384)] = dot(hp[i, rows_of(n, 384)], w[:, third(i)]).astype(BF)
+            s2[rows_of(n, 384), part(i)] = dot(hp[i, rows_of(n, 384)], w[:, part(i)]).astype(BF)
             return 0
 
         lax.fori_loop(0, SIDE, produce, 0)
@@ -427,8 +459,8 @@
         for i, (A, B, C) in enumerate(AXES):
             b = lax.rem(here[B] + b_by, SIDE)
             rows = rows_of(b, 384)
-            pltpu.make_async_copy(s2.at[i, pl.ds(0, 384)], arr.at[i, rows], s3_r.at[i, b]).wait()
-            score = lane_sum(s2[i, rows].astype(F32) * arr[i, rows].astype(F32))
+            pltpu.make_async_copy(s2.at[pl.ds(0, 384), lanes(i)], arr.at[rows, lanes(i)], s3_r.at[i, b]).wait()
+            score = lane_sum(s2[rows, part(i)].astype(F32) * arr[rows, part(i)].astype(F32))
             at_slot = jnp.where(own_slot, score, 0.0)
             coord = [None, None, None]
             coord[A], coord[B], coord[C] = p_a, b.astype(F32), p_c
@@ -444,21 +476,33 @@
         pick = jnp.where(lanes_r == src.astype(I32), 1.0, 0.0).astype(BF)
         w_in = wrecv[...].reshape(EXPERTS, EXPERTS).astype(BF)
         col = jnp.sum(jnp.where(own_slot, dot(pick, w_in), 0.0), axis=1, keepdims=True)
-        scaled = (arr[i, rows_of(b, 384)].astype(F32) * col).astype(BF)
-        part = dot(hp[i, rows_of(b, 384)], scaled, TN)
+        scaled = (arr[rows_of(b, 384), part(i)].astype(F32) * col).astype(BF)
+        piece = dot(hp[i, rows_of(b, 384)], scaled, TN)
         if b_by == 0:
-            gbuf[i] = part
+            gbuf[:, 0:PARTS[i]] = piece
         else:
-            gbuf[i] += part
+            gbuf[:, 0:PARTS[i]] += piece
 
     grads = []
 
     def last_grad(i):
         for by in range(SIDE):
             grad_group(i, by)
-        cp = pltpu.make_async_copy(gbuf.at[i], grad_o.at[:, pl.ds(i * THIRD, THIRD)], out_sem.at[3 + i])
-        cp.start()
-        grads.append(cp)
+
+        def step(n, _):
+            r = rows_of(n, 64)
+            wf, mf, gf = w[r, part(i)].astype(F32), m[r, part(i)].astype(F32), gbuf[r, 0:PARTS[i]]
+            turn = BETA_ONE * mf + (1.0 - BETA_ONE) * gf
+            move = jnp.where(turn > 0.0, -LION_RATE, jnp.where(turn < 0.0, LION_RATE, 0.0))
+            w[r, part(i)] = (wf * (1.0 - LION_RATE * WEIGHT_DECAY) + move).astype(BF)
+            m[r, part(i)] = (BETA_TWO * mf + (1.0 - BETA_TWO) * gf).astype(BF)
+            return 0
+
+        lax.fori_loop(0, FF // 64, step, 0)
+        for n, (a, b) in enumerate(((w, nw_o), (m, nm_o))):
+            cp = pltpu.make_async_copy(a.at[:, lanes(i)], b.at[:, lanes(i)], out_sem.at[3 + 2 * i + n])
+            cp.start()
+            grads.append(cp)
 
     score_group(0)
     score_group(1)
@@ -469,7 +513,8 @@
     exp_in(csend, cmid, c1_s, c1_r)
     ctx_exchange(cmid, crecv, c2_s, c2_r)
     ctx_arrive(wmid, wrecv, w2_s, w2_r)
-    last_grad(0)
+    loads[9].wait()
+    last_grad(2)
     ctx_arrive(cmid, crecv, c2_s, c2_r)
 
     back = jnp.transpose(crecv[...].reshape(EXPERTS, EXPERTS))
@@ -480,9 +525,9 @@
     logit_grad = (chosen * ((prob - mix) / total * gate * (1.0 - gate))).astype(BF)
     mean = 0.0
     for i in range(3):
-        ng = dot(logit_grad, router[third(i), :], NT)
-        cum_s[:, third(i)] = ng
-        mean = mean + lane_sum(ng * mixed[:, third(i)])
+        ng = dot(logit_grad, router[part(i), :], NT)
+        cum_s[:, part(i)] = ng
+        mean = mean + lane_sum(ng * mixed[:, part(i)])
     pull = inverse * inverse * inverse * (mean * (1.0 / WIDTH))
 
     def residual(h, _):
@@ -494,28 +539,37 @@
         f32buf[:, rows_of(h, 8), :] = adj.reshape(CTX, 8, HD)
         return 0
 
-    lax.fori_loop(0, HEADS, residual, 0, unroll=UNROLL)
-
-    def pack_back(j, _):
-        asend[j] = f32buf[j].astype(BF)
-        return 0
-
-    lax.fori_loop(0, CTX, pack_back, 0, unroll=4)
-    ctx_exchange(asend, arecv, a_s, a_r)
+    halves = ((0, 10), (10, HEADS))
+
+    def half_rows(n):
+        first, last = halves[n]
+        return pl.ds(first * 8, (last - first) * 8)
+
+    for n, (first, last) in enumerate(halves):
+        lax.fori_loop(first, last, residual, 0, unroll=2)
+
+        def pack_back(j, _, n=n):
+            asend[j, half_rows(n), :] = f32buf[j, half_rows(n), :].astype(BF)
+            return 0
+
+        lax.fori_loop(0, CTX, pack_back, 0, unroll=4)
+        ctx_exchange(asend, arecv, a_s.at[n], a_r.at[n], half_rows(n))
     gres_out = pltpu.make_async_copy(cot, gres_o, out_sem.at[1])
     gres_out.start()
+    last_grad(0)
+    for n, (first, last) in enumerate(halves):
+        ctx_arrive(asend, arecv, a_s.at[n], a_r.at[n], half_rows(n))
+
+        def backward(t, acc, n=n, first=first, last=last):
+            j = CTX - 1 - t
+            bsend[j, half_rows(n), :] = acc.astype(BF)
+            return factor(j, first, last) * acc + arecv[j, half_rows(n), :].astype(F32)
+
+        lax.fori_loop(0, CTX, backward, jnp.zeros(((last - first) * 8, HD), F32), unroll=2)
+        ctx_exchange(bsend, brecv, e_s.at[n], e_r.at[n], half_rows(n))
     last_grad(1)
-    ctx_arrive(asend, arecv, a_s, a_r)
-
-    def backward(n, acc):
-        j = CTX - 1 - n
-        bsend[j] = acc.astype(BF)
-        return factor(j) * acc + arecv[j].astype(F32)
-
-    lax.fori_loop(0, CTX, backward, jnp.zeros((GROUP, HD), F32), unroll=2)
-    ctx_exchange(bsend, brecv, e_s, e_r)
-    last_grad(2)
-    ctx_arrive(bsend, brecv, e_s, e_r)
+    for n in range(2):
+        ctx_arrive(bsend, brecv, e_s.at[n], e_r.at[n], half_rows(n))
 
     def widen_back(j, _):
         f32buf[j] = brecv[j].astype(F32)
@@ -536,8 +590,9 @@
         cp.wait_send()
     ctx_sent(fsend, frecv, f_s, f_r)
     ctx_sent(ssend, srecv, b_s, b_r)
-    ctx_sent(asend, arecv, a_s, a_r)
-    ctx_sent(bsend, brecv, e_s, e_r)
+    for n in range(2):
+        ctx_sent(asend, arecv, a_s.at[n], a_r.at[n], half_rows(n))
+        ctx_sent(bsend, brecv, e_s.at[n], e_r.at[n], half_rows(n))
     exp_sent(wsend, wmid, w1_s, w1_r)
     exp_sent(csend, cmid, c1_s, c1_r)
     ctx_sent(wmid, wrecv, w2_s, w2_r)
@@ -549,18 +604,15 @@
 
 
 def finish(
-    q_h, k_h, v_h, g_h, cot_h, state_h, sgrad_h, starts_ref, w_h, m_h, grad_h,
+    q_h, k_h, v_h, g_h, cot_h, state_h, sgrad_h, starts_ref, stepped_h, moment_h,
     dq_h, dk_h, dv_h, dg_h, gres_h, nw_h, nm_h,
-    q, k, v, g, cot, state, sgrad, w, m, grad, dq, dk, dv, dg, in_sem, out_sem, l_sem, s_sem,
+    q, k, v, g, cot, state, sgrad, stepped, moment, dq, dk, dv, dg, in_sem, out_sem, pass_sem,
 ):
-    wide, tall = PER * HD, FF // LION_STEPS
+    wide = PER * HD
     head_steps = HEADS // PER
 
     def cols(n):
         return pl.ds(n * wide, wide)
-
-    def rows(n):
-        return pl.ds(n * tall, tall)
 
     def loads(n):
         out = [
@@ -571,12 +623,6 @@
             out.append(pltpu.make_async_copy(a.at[pl.ds(n * PER, PER)], b.at[pl.ds(n * PER, PER)], in_sem.at[n, 5 + j]))
         return out
 
-    def lion_loads(n):
-        return [
-            pltpu.make_async_copy(a.at[rows(n)], b.at[rows(n)], l_sem.at[n, j])
-            for j, (a, b) in enumerate(((w_h, w), (m_h, m), (grad_h, grad)))
-        ]
-
     stores = []
 
     def store(a, b, sem):
@@ -584,15 +630,14 @@
         cp.start()
         stores.append(cp)
 
-    order = []
-    for n in range(max(head_steps, LION_STEPS)):
-        if n < head_steps:
-            order.append(("heads", n, loads(n)))
-        if n < LION_STEPS:
-            order.append(("lion", n, lion_loads(n)))
-    for _, _, copies in order:
+    order = [loads(n) for n in range(head_steps)]
+    for copies in order:
         for cp in copies:
             cp.start()
+    through = []
+    for j, (a, b) in enumerate(((stepped_h, stepped), (moment_h, moment))):
+        through.append(pltpu.make_async_copy(a, b, pass_sem.at[j]))
+        through[-1].start()
 
     seg_row, seg_col = segments(starts_ref)
     last_seg = seg_row[:, TOK - 1:TOK]
@@ -642,25 +687,13 @@
         for j, (a, b) in enumerate(((dq, dq_h), (dk, dk_h), (dv, dv_h), (dg, dg_h))):
             store(a.at[:, cols(n)], b.at[:, cols(n)], out_sem.at[n, j])
 
-    def lion_step(n):
-        r = slice(n * tall, (n + 1) * tall)
-        for third in range(3):
-            c = slice(third * THIRD, (third + 1) * THIRD)
-            wf, mf, gf = w[r, c].astype(F32), m[r, c].astype(F32), grad[r, c]
-            turn = BETA_ONE * mf + (1.0 - BETA_ONE) * gf
-            move = jnp.where(turn > 0.0, -LION_RATE, jnp.where(turn < 0.0, LION_RATE, 0.0))
-            w[r, c] = (wf * (1.0 - LION_RATE * WEIGHT_DECAY) + move).astype(BF)
-            m[r, c] = (BETA_TWO * mf + (1.0 - BETA_TWO) * gf).astype(BF)
-        store(w.at[rows(n)], nw_h.at[rows(n)], s_sem.at[n, 0])
-        store(m.at[rows(n)], nm_h.at[rows(n)], s_sem.at[n, 1])
-
-    for kind, n, copies in order:
+    for n, copies in enumerate(order):
         for cp in copies:
             cp.wait()
-        if kind == "heads":
-            heads_step(n)
-        else:
-            lion_step(n)
+        heads_step(n)
+        if n in (1, 2):
+            through[n - 1].wait()
+            store((stepped, moment)[n - 1], (nw_h, nm_h)[n - 1], pass_sem.at[n + 1])
     for cp in stores:
         cp.wait()
 
@@ -674,9 +707,9 @@
     V = pltpu.VMEM
     scratch = [
         V((TOP, TOK), I32), V((TOP, TOK), I32), V((1, TOK), I32),
-        *[V((TOK, WIDTH), BF)] * 6, V((WIDTH, EXPERTS), BF), V((CAP, FF), BF), V((FF, WIDTH), BF),
-        V((3, SIDE * TOK, THIRD), BF), V((16, TOK), F32), V((3, SIDE, 16, TOK), F32), V((3, 32, SIDE * TOK), F32),
-        *[V((3, CAP, THIRD), BF)] * 3,
+        *[V((TOK, WIDTH), BF)] * 6, V((WIDTH, EXPERTS), BF), V((CAP, FF), BF), V((FF, WIDTH), BF), V((FF, WIDTH), BF),
+        V((SIDE * TOK, WIDTH), BF), V((16, TOK), F32), V((3, SIDE, 16, TOK), F32), V((3, 32, SIDE * TOK), F32),
+        *[V((CAP, WIDTH), BF)] * 3,
         V((3, CAP, FF), BF),
         V((CTX, GROUP, HD), F32), V((CTX, PACK, HD), BF), V((CTX, PACK, HD), BF),
         V((CTX, GROUP, HD), BF), V((CTX, GROUP, HD), BF), V((HEADS, HD, HD), BF),
@@ -685,46 +718,47 @@
         V((TOK, WIDTH), BF), V((TOK, WIDTH), BF), V((EXPERTS, EXPERTS), F32),
         V((8, CTX, EXPERTS), F32), V((CTX, 8, EXPERTS), F32), V((CTX, 8, EXPERTS), F32),
         V((8, CTX, EXPERTS), F32), V((CTX, 8, EXPERTS), F32), V((CTX, 8, EXPERTS), F32),
-        V((3, FF, THIRD), F32), V((TOK, WIDTH), F32),
-        dma((12,)), dma((6,)),
-        dma((3, 4)), dma((3, 4)), dma((3, 4)), dma((3, 4)), dma((3, 4)), dma((3, 4)), dma((3, 8, 4)), dma((3, 4)),
+        V((FF, max(PARTS)), F32), V((TOK, WIDTH), F32),
+        dma((13,)), dma((9,)),
+        dma((3, 2, 4)), dma((3, 2, 4)), dma((3, 4)), dma((3, 4)), dma((3, 2, 4)), dma((3, 2, 4)), dma((3, 8, 4)), dma((3, 4)),
         dma((CTX,)), dma((CTX,)), dma((CTX,)), dma((CTX,)),
         dma((8,)), dma((8,)), dma((CTX,)), dma((CTX,)), dma((8,)), dma((8,)), dma((CTX,)), dma((CTX,)),
-        dma((CTX,)), dma((CTX,)), dma((CTX,)), dma((CTX,)),
+        dma((2, CTX)), dma((2, CTX)), dma((2, CTX)), dma((2, CTX)),
     ]
-    gres, state, sgrad, grad = pl.pallas_call(
+    gres, state, sgrad, stepped, moment = pl.pallas_call(
         mixer,
         name="dispatch_and_scan",
         out_shape=(
             jax.ShapeDtypeStruct((TOK, WIDTH), BF),
             jax.ShapeDtypeStruct((HEADS, HD, HD), BF),
             jax.ShapeDtypeStruct((HEADS, HD, HD), BF),
-            jax.ShapeDtypeStruct((FF, WIDTH), F32),
+            jax.ShapeDtypeStruct((FF, WIDTH), BF),
+            jax.ShapeDtypeStruct((FF, WIDTH), BF),
         ),
-        in_specs=[any_] * 12,
-        out_specs=(any_,) * 4,
+        in_specs=[any_] * 13,
+        out_specs=(any_,) * 5,
         scratch_shapes=scratch,
         compiler_params=pltpu.CompilerParams(
             collective_id=0, has_side_effects=True, vmem_limit_bytes=62 * 2**20),
     )(
         out_grad[0], queries[0], key_vectors[0], values[0], log_decay[0], residual_in[0], router,
-        hidden_saved[0], w_down[0], expert_ids[0].T, slot_index[0].T, starts,
+        hidden_saved[0], w_down[0], momentum[0], expert_ids[0].T, slot_index[0].T, starts,
     )
     tok = V((TOK, WIDTH), BF)
     outs = pl.pallas_call(
         finish,
         name="backward_and_step",
         out_shape=(jax.ShapeDtypeStruct((TOK, WIDTH), BF),) * 5 + (jax.ShapeDtypeStruct((FF, WIDTH), BF),) * 2,
-        in_specs=[any_] * 7 + [vm] + [any_] * 3,
+        in_specs=[any_] * 7 + [vm] + [any_] * 2,
         out_specs=(any_,) * 7,
         scratch_shapes=[
-            *[tok] * 5, *[V((HEADS, HD, HD), BF)] * 2, *[V((FF, WIDTH), BF)] * 2, V((FF, WIDTH), F32), *[tok] * 4,
-            dma((HEADS // PER, 7)), dma((HEADS // PER, 5)), dma((LION_STEPS, 3)), dma((LION_STEPS, 2)),
+            *[tok] * 5, *[V((HEADS, HD, HD), BF)] * 2, *[V((FF, WIDTH), BF)] * 2, *[tok] * 4,
+            dma((HEADS // PER, 7)), dma((HEADS // PER, 5)), dma((4,)),
         ],
         compiler_params=pltpu.CompilerParams(vmem_limit_bytes=62 * 2**20),
     )(
         queries[0], key_vectors[0], values[0], log_decay[0], gres, state, sgrad, starts,
-        w_down[0], momentum[0], grad,
+        stepped, moment,
     )
     return tuple(x[None] for x in outs)
 

time: 131 us -> 125 us (0.954)
  Pallas kernels: 129 us -> 123 us
    pallas_call x1, Pallas kernels: 12 us -> 8.12 us  [local(): pl.pallas_call(finish, name='backward_and_step', out_shape=(jax.ShapeDtyp...]
    pallas_call x1, Pallas kernels: 117 us -> 115 us  [local(): pl.pallas_call(mixer, name='dispatch_and_scan', out_shape=(jax.ShapeDtype...]
where the time goes in v5:
time: 125 us; the launch traced here: 124 us
  Pallas kernels  123 us (98%)
    pallas_call x1, Pallas kernels, local(): pl.pallas_call(mixer, name='dispatch_and_scan', out_shape=(jax.ShapeDtype...  115 us
    pallas_call x1, Pallas kernels, local(): pl.pallas_call(finish, name='backward_and_step', out_shape=(jax.ShapeDtyp...  8.12 us

profile of v5, /device:TPU:1, one launch (start us, length us, event | category | flops | bytes accessed | tf_op | source)
XLA Modules:
  0.0 124.2 jit_solution(6754968438647610788)
XLA Ops:
  0.6 115.3 %dispatch_and_scan.1 = (bf16[128,2304]{1,0:T(8,128)(2,1)}, bf16[18,128,128]{2,1,0:T(8,128)(2,1)}, bf16[18,128,128]{2,1,0:T(8,128)(2,1)}, bf16[512,2304]{1,0:T(8,128)(2,1)}, bf16[512,2304]{1,0:T(8,128)(2,1)}) custom-call(bf16[128,2304]{1,0:T(8,128)(2,1)} %bitcast.33, bf16[128,2304]{1,0:T(8,128)(2,1)} %bitcast.22, bf16[128,2304]{1,0:T(8,128)(2,1)} %bitcast.24, ...), custom_call_target="tpu_custom_call" | custom-call | tf_op jit(solution)/shard_map/dispatch_and_scan/pallas_call | solution.py:728
  115.9 8.1 %backward_and_step.1 = (bf16[128,2304]{1,0:T(8,128)(2,1)}, bf16[128,2304]{1,0:T(8,128)(2,1)}, bf16[128,2304]{1,0:T(8,128)(2,1)}, bf16[128,2304]{1,0:T(8,128)(2,1...) custom-call(bf16[128,2304]{1,0:T(8,128)(2,1)} %bitcast.23, ...), custom_call_target="tpu_custom_call" | custom-call | tf_op jit(solution)/shard_map/backward_and_step/pallas_call | solution.py:748

commit v6 on v5

--- a/solution.py
+++ b/solution.py
@@ -31,8 +31,8 @@
 BF = jnp.bfloat16
 F32 = jnp.float32
 I32 = jnp.int32
-UNROLL = 3
-PER = 6
+UNROLL = 6
+PER = 9
 MESH = pl.DeviceIdType.MESH
 STRIDE = (32, 8, 2)
 AXES = ((0, 1, 2), (1, 2, 0), (2, 0, 1))
@@ -546,7 +546,7 @@
         return pl.ds(first * 8, (last - first) * 8)
 
     for n, (first, last) in enumerate(halves):
-        lax.fori_loop(first, last, residual, 0, unroll=2)
+        lax.fori_loop(first, last, residual, 0, unroll=last - first)
 
         def pack_back(j, _, n=n):
             asend[j, half_rows(n), :] = f32buf[j, half_rows(n), :].astype(BF)
@@ -565,7 +565,7 @@
             bsend[j, half_rows(n), :] = acc.astype(BF)
             return factor(j, first, last) * acc + arecv[j, half_rows(n), :].astype(F32)
 
-        lax.fori_loop(0, CTX, backward, jnp.zeros(((last - first) * 8, HD), F32), unroll=2)
+        lax.fori_loop(0, CTX, backward, jnp.zeros(((last - first) * 8, HD), F32), unroll=4)
         ctx_exchange(bsend, brecv, e_s.at[n], e_r.at[n], half_rows(n))
     last_grad(1)
     for n in range(2):
@@ -691,9 +691,8 @@
         for cp in copies:
             cp.wait()
         heads_step(n)
-        if n in (1, 2):
-            through[n - 1].wait()
-            store((stepped, moment)[n - 1], (nw_h, nm_h)[n - 1], pass_sem.at[n + 1])
+        through[n].wait()
+        store((stepped, moment)[n], (nw_h, nm_h)[n], pass_sem.at[n + 2])
     for cp in stores:
         cp.wait()
 

time: 125 us -> 125 us (level)
  no operation moved by 1% of the time
where the time goes in v6:
time: 125 us
  Pallas kernels  124 us (99%)
    pallas_call x1, Pallas kernels, local(): pl.pallas_call(mixer, name='dispatch_and_scan', out_shape=(jax.ShapeDtype...  116 us
    pallas_call x1, Pallas kernels, local(): pl.pallas_call(finish, name='backward_and_step', out_shape=(jax.ShapeDtyp...  7.84 us

profile of v6, /device:TPU:1, one launch (start us, length us, event | category | flops | bytes accessed | tf_op | source)
XLA Modules:
  0.0 124.6 jit_solution(16556120693180861070)
XLA Ops:
  0.6 115.9 %dispatch_and_scan.1 = (bf16[128,2304]{1,0:T(8,128)(2,1)}, bf16[18,128,128]{2,1,0:T(8,128)(2,1)}, bf16[18,128,128]{2,1,0:T(8,128)(2,1)}, bf16[512,2304]{1,0:T(8,128)(2,1)}, bf16[512,2304]{1,0:T(8,128)(2,1)}) custom-call(bf16[128,2304]{1,0:T(8,128)(2,1)} %bitcast.33, bf16[128,2304]{1,0:T(8,128)(2,1)} %bitcast.22, bf16[128,2304]{1,0:T(8,128)(2,1)} %bitcast.24, ...), custom_call_target="tpu_custom_call" | custom-call | tf_op jit(solution)/shard_map/dispatch_and_scan/pallas_call | solution.py:727
  116.6 7.8 %backward_and_step.1 = (bf16[128,2304]{1,0:T(8,128)(2,1)}, bf16[128,2304]{1,0:T(8,128)(2,1)}, bf16[128,2304]{1,0:T(8,128)(2,1)}, bf16[128,2304]{1,0:T(8,128)(2,1...) custom-call(bf16[128,2304]{1,0:T(8,128)(2,1)} %bitcast.23, ...), custom_call_target="tpu_custom_call" | custom-call | tf_op jit(solution)/shard_map/backward_and_step/pallas_call | solution.py:747
